TPU v7x, 128 devices: a whole 4x4x4 slice. The times are simulated.
128 devices in a mesh: lat: 32 (over z, x_lo, y), grp: 4 (over x_hi, core).
Axes of the slice: x: 4 (x_hi: 2, x_lo: 2; x = x_hi * 2 + x_lo), y: 4, z: 4, core: 2. Of those that a mesh axis runs over, the one named last changes fastest.
Arguments:
- tokens: bfloat16 [384, 256, 1024], P('grp', 'lat'), may hold values from -6 to 6
- cotangent: bfloat16 [384, 256, 1024], P('grp', 'lat'), may hold values from -6 to 6
- gain: float32 [384], P('grp'), may hold values from 0.5 to 1.5
- shift: float32 [384], P('grp'), may hold values from -3 to 3
- w_in: float32 [4, 2, 96, 96], P('grp'), may hold values from -0.4375 to 0.4375
- b_in: float32 [4, 2, 96], P('grp'), may hold values from -0.3 to 0.3
- w_out: float32 [4, 2, 96, 96], P('grp'), may hold values from -0.4375 to 0.4375
- b_out: float32 [4, 2, 96], P('grp'), may hold values from -0.12 to 0.12
Outputs:
- mixed: bfloat16 [384, 256, 1024], P('grp', 'lat')
- grad_tokens: bfloat16 [384, 256, 1024], P('grp', 'lat')
- grad_weights: float32 [4, 36864], P('grp', 'lat')
All inputs are finite; a program needn't handle non-finite values.
Results may differ from a plain program's by a relative error of at most 0.012.
Values sent between devices are 32-bit elements; how exact they have to be, the bound alone decides.
No kernel may reach another device: no remote copies, remote signals or barrier semaphores. Data moves between devices by JAX's collectives and lax.ppermute only.
A program may use at most 128 MiB of HBM per device.

v0:
```python
import math

import jax
import jax.numpy as jnp
from jax import lax
from jax.sharding import PartitionSpec as P

highest = lax.Precision.HIGHEST
shrink_level = 0.01
norm_eps = 1e-05


def contract(form, left, right):
    return jnp.einsum(form, left, right, precision=highest)


def angle_table(left_count, right_count, length):
    left_index = jnp.arange(left_count, dtype=jnp.int32)[:, None]
    right_index = jnp.arange(right_count, dtype=jnp.int32)[None, :]
    phase = left_index * right_index % length
    theta = phase.astype(jnp.float32) * (2.0 * math.pi / length)
    return (jnp.cos(theta), jnp.sin(theta))


def lon_forward(field, modes):
    length = field.shape[2]
    cos_tab, sin_tab = angle_table(length, modes, length)
    scale = 1.0 / math.sqrt(length)
    out_real = contract("crn,nm->cmr", field, cos_tab) * scale
    out_imag = contract("crn,nm->cmr", field, sin_tab) * -scale
    return jnp.stack([out_real, out_imag])


def lon_inverse(stack, length, weighted):
    modes = stack.shape[2]
    cos_tab, sin_tab = angle_table(modes, length, length)
    scale = 1.0 / math.sqrt(length)
    real_part = stack[0]
    imag_part = stack[1]
    if weighted:
        mode_weight = jnp.where(jnp.arange(modes) == 0, 1.0, 2.0).astype(jnp.float32)[None, :, None]
        real_part = real_part * mode_weight
        imag_part = imag_part * mode_weight
    out = contract("cmr,mn->crn", real_part, cos_tab) - contract("cmr,mn->crn", imag_part, sin_tab)
    return out * scale


def lat_forward(stack):
    real_part, imag_part = (stack[0], stack[1])
    length = real_part.shape[-1]
    cos_tab, sin_tab = angle_table(length, length, length)
    scale = 1.0 / math.sqrt(length)
    out_real = contract("cql,lk->cqk", real_part, cos_tab) + contract(
        "cql,lk->cqk", imag_part, sin_tab
    )
    out_imag = contract("cql,lk->cqk", imag_part, cos_tab) - contract(
        "cql,lk->cqk", real_part, sin_tab
    )
    return (out_real * scale, out_imag * scale)


def lat_inverse(real_part, imag_part):
    length = real_part.shape[-1]
    cos_tab, sin_tab = angle_table(length, length, length)
    scale = 1.0 / math.sqrt(length)
    out_real = contract("cql,lk->cqk", real_part, cos_tab) - contract(
        "cql,lk->cqk", imag_part, sin_tab
    )
    out_imag = contract("cql,lk->cqk", imag_part, cos_tab) + contract(
        "cql,lk->cqk", real_part, sin_tab
    )
    return jnp.stack([out_real * scale, out_imag * scale])


def complex_mix(left_real, left_imag, weight):
    form = "bihk,bio->bohk"
    w_real = weight[:, 0]
    w_imag = weight[:, 1]
    out_real = contract(form, left_real, w_real) - contract(form, left_imag, w_imag)
    out_imag = contract(form, left_imag, w_real) + contract(form, left_real, w_imag)
    return (out_real, out_imag)


def mix_back(grad_real, grad_imag, weight):
    form = "bohk,bio->bihk"
    w_real = weight[:, 0]
    w_imag = weight[:, 1]
    back_real = contract(form, grad_real, w_real) + contract(form, grad_imag, w_imag)
    back_imag = contract(form, grad_imag, w_real) - contract(form, grad_real, w_imag)
    return (back_real, back_imag)


def weight_grad(left_real, left_imag, grad_real, grad_imag):
    form = "bihk,bohk->bio"
    grad_wreal = contract(form, left_real, grad_real) + contract(form, left_imag, grad_imag)
    grad_wimag = contract(form, left_real, grad_imag) - contract(form, left_imag, grad_real)
    return (grad_wreal, grad_wimag)


def shrink(value):
    return jnp.sign(value) * jnp.maximum(jnp.abs(value) - shrink_level, 0.0)


def per_device(tokens, cotangent, gain, shift, w_in, b_in, w_out, b_out):
    chans, rows, length = tokens.shape
    grp_count = lax.axis_size("grp")
    all_chans = chans * grp_count
    modes = length // 2
    tok_val = tokens.astype(jnp.float32)
    grad_val = cotangent.astype(jnp.float32)
    first_sum, second_sum = lax.psum(
        (jnp.sum(tok_val, axis=0), jnp.sum(tok_val * tok_val, axis=0)), "grp"
    )
    token_mean = first_sum / all_chans
    inv_std = lax.rsqrt(second_sum / all_chans - token_mean * token_mean + norm_eps)
    normed = (tok_val - token_mean) * inv_std
    normal_out = normed * gain[:, None, None] + shift[:, None, None]
    mode_weight = jnp.where(jnp.arange(modes) == 0, 1.0, 2.0).astype(jnp.float32)[
        None, None, :, None
    ]
    spec_field = lon_forward(normal_out, modes)
    spec_grad = lon_forward(grad_val, modes) * mode_weight
    modes_field, modes_grad = (
        lax.all_to_all(spec_field, "lat", split_axis=2, concat_axis=3, tiled=True),
        lax.all_to_all(spec_grad, "lat", split_axis=2, concat_axis=3, tiled=True),
    )
    block_in, bias_in, block_out, bias_out = (w_in, b_in, w_out, b_out)
    block_count = block_in.shape[0]
    block_size = block_in.shape[2]
    quarter = modes_field.shape[2]
    lat_len = modes_field.shape[3]
    spec_real, spec_imag = lat_forward(modes_field)
    grad_real, grad_imag = lat_forward(modes_grad)
    blocked = (block_count, block_size, quarter, lat_len)
    spec_real = spec_real.reshape(blocked)
    spec_imag = spec_imag.reshape(blocked)
    grad_real = grad_real.reshape(blocked)
    grad_imag = grad_imag.reshape(blocked)
    pre_real, pre_imag = complex_mix(spec_real, spec_imag, block_in)
    pre_real = pre_real + bias_in[:, 0, :, None, None]
    pre_imag = pre_imag + bias_in[:, 1, :, None, None]
    act_real = jax.nn.relu(pre_real)
    act_imag = jax.nn.relu(pre_imag)
    post_real, post_imag = complex_mix(act_real, act_imag, block_out)
    post_real = post_real + bias_out[:, 0, :, None, None]
    post_imag = post_imag + bias_out[:, 1, :, None, None]
    shrunk_real = shrink(post_real)
    shrunk_imag = shrink(post_imag)
    d_post_real = jnp.where(jnp.abs(post_real) > shrink_level, grad_real, 0.0)
    d_post_imag = jnp.where(jnp.abs(post_imag) > shrink_level, grad_imag, 0.0)
    g_out_real, g_out_imag = weight_grad(act_real, act_imag, d_post_real, d_post_imag)
    d_act_real, d_act_imag = mix_back(d_post_real, d_post_imag, block_out)
    d_pre_real = jnp.where(pre_real > 0.0, d_act_real, 0.0)
    d_pre_imag = jnp.where(pre_imag > 0.0, d_act_imag, 0.0)
    g_in_real, g_in_imag = weight_grad(spec_real, spec_imag, d_pre_real, d_pre_imag)
    d_spec_real, d_spec_imag = mix_back(d_pre_real, d_pre_imag, block_in)
    flat_shape = (block_count * block_size, quarter, lat_len)
    back_field = lat_inverse(shrunk_real.reshape(flat_shape), shrunk_imag.reshape(flat_shape))
    back_grad = lat_inverse(d_spec_real.reshape(flat_shape), d_spec_imag.reshape(flat_shape))
    grad_stack = jnp.stack([g_in_real, g_in_imag, g_out_real, g_out_imag], axis=1)
    grad_term = grad_stack.reshape(block_count, 4 * block_size * block_size) * (
        1.0 / math.sqrt(lat_len * modes)
    )
    rows_field, rows_grad = (
        lax.all_to_all(back_field, "lat", split_axis=3, concat_axis=2, tiled=True),
        lax.all_to_all(back_grad, "lat", split_axis=3, concat_axis=2, tiled=True),
    )
    grad_weights = lax.psum_scatter(grad_term, "lat", scatter_dimension=1, tiled=True)
    filtered = lon_inverse(rows_field, length, True)
    pulled = lon_inverse(rows_grad, length, False)
    mixed = (filtered + normal_out + tok_val).astype(jnp.bfloat16)
    d_normal = grad_val + pulled
    dnorm = d_normal * gain[:, None, None]
    back_one, back_two = lax.psum((jnp.sum(dnorm, axis=0), jnp.sum(dnorm * normed, axis=0)), "grp")
    grad_tokens = grad_val + inv_std * (
        dnorm - back_one / all_chans - normed * (back_two / all_chans)
    )
    return (mixed, grad_tokens.astype(jnp.bfloat16), grad_weights)


def solution(mesh):
    in_specs = (
        P("grp", "lat", None),
        P("grp", "lat", None),
        P("grp"),
        P("grp"),
        P("grp", None, None, None),
        P("grp", None, None),
        P("grp", None, None, None),
        P("grp", None, None),
    )
    out_specs = (P("grp", "lat", None), P("grp", "lat", None), P("grp", "lat"))
    return jax.shard_map(
        per_device, mesh=mesh, in_specs=in_specs, out_specs=out_specs, check_vma=False
    )
```

profile of v0, /device:TPU:1, one launch (start us, length us, event | category | flops | bytes accessed | tf_op | source)
XLA Modules:
  0.0 742.5 jit_solution(13960759402539351811)
XLA Ops:
  7.2 12.5 %multiply_bitcast_fusion.2 = f32[1,96,512,8]{2,1,3,0:T(8,128)S(1)} fusion(bf16[96,8,1024]{2,1,0:T(8,128)(2,1)} %param.9), kind=kOutput, calls=%fused_computation.96 | convolution fusion | flops 4839571456 | bytes 3145728 | tf_op jit(solution)/shard_map/crn,nm->cmr/dot_general | solution.py:14
  19.7 11.2 %multiply_bitcast_fusion.3 = f32[1,96,512,8]{2,1,3,0:T(8,128)S(1)} fusion(bf16[96,8,1024]{2,1,0:T(8,128)(2,1)S(1)} %copy-done.30), kind=kOutput, calls=%fused_computation.97 | convolution fusion | flops 4839571456 | bytes 3145728 | tf_op jit(solution)/shard_map/crn,nm->cmr/dot_general | solution.py:14
  31.3 3.6 copy.301
  34.8 10.1 %all-to-all-start.2 = ((f32[2,96,512,8]{1,3,0,2:T(8,128)}), f32[2,96,512,8]{1,3,0,2:T(8,128)}, u32[]{:S(2)}, u32[]{:S(2)}) async-start(f32[2,96,512,8]{1,3,0,2:T(8,128)} %copy.301), calls=%async_computation.2 | async-start | bytes 8388608 | tf_op jit(solution)/shard_map/all_to_all | solution.py:125
  46.5 45.6 %all-reduce.7.cloned.1.call-done = (f32[8,1024]{1,0:T(8,128)}, f32[8,1024]{1,0:T(8,128)}) async-done(((f32[8,1024]{1,0:T(8,128)}, f32[8,1024]{1,0:T(8,128)}), (f32[8,1024]{1,0:T(8,128)}, f32[8,1024]{1,0:T(8,128)})) %all-reduce.7.cloned.1.call-update) | async-done | bytes 65552 | tf_op jit(solution)/shard_map/psum | solution.py:111
  93.5 13.9 %multiply_bitcast_fusion.6 = f32[1,96,512,8]{2,1,3,0:T(8,128)S(1)} fusion(f32[96,8,1024]{2,1,0:T(8,128)S(1)} %fusion.6), kind=kOutput, calls=%fused_computation.104 | convolution fusion | flops 4839571456 | bytes 4718592 | tf_op jit(solution)/shard_map/crn,nm->cmr/dot_general | solution.py:14
  107.4 14.1 %multiply_bitcast_fusion.7 = f32[1,96,512,8]{2,1,3,0:T(8,128)S(1)} fusion(f32[96,8,1024]{2,1,0:T(8,128)S(1)} %fusion.6), kind=kOutput, calls=%fused_computation.105 | convolution fusion | flops 4839571456 | bytes 4718592 | tf_op jit(solution)/shard_map/crn,nm->cmr/dot_general | solution.py:14
  125.4 7.4 all-to-all-start
  140.7 3.8 copy.577
  153.7 35.6 %all-to-all-done = f32[2,96,512,8]{1,3,0,2:T(8,128)} async-done(((f32[2,96,512,8]{1,3,0,2:T(8,128)}), f32[2,96,512,8]{1,3,0,2:T(8,128)}, u32[]{:S(2)}, u32[]{:S(2)}) %all-to-all-start) | async-done | bytes 3145760 | tf_op jit(solution)/shard_map/all_to_all | solution.py:124
  247.9 3.6 fusion.104
  251.5 3.6 fusion.106
  259.8 3.6 fusion.112
  263.4 3.6 fusion.114
  275.0 5.4 copy.293
  280.4 9.3 %all-to-all-start.1 = ((f32[2,96,16,256]{1,2,0,3:T(8,128)}), f32[2,96,16,256]{1,2,0,3:T(8,128)}, u32[]{:S(2)}, u32[]{:S(2)}) async-start(f32[2,96,16,256]{1,2,0,3:T(8,128)} %copy.293), calls=%async_computation.1 | async-start | bytes 8388608 | tf_op jit(solution)/shard_map/all_to_all | solution.py:165
  289.7 16.5 %fusion.55 = (f32[96,16,256]{2,1,0:T(8,128)S(1)}, f32[96,16,256]{2,1,0:T(8,128)S(1)}) fusion(f32[16,256,96]{1,2,0:T(8,128)} %fusion.112, f32[16,256,96]{1,2,0:T(8,128)} %fusion.104, f32[96]{0:T(128)S(1)} %get-tuple-element.25, f32[16,256,96]{1,2,0:T(8,128)} %copy-done.20, f32[16,256,96]{1,2,0:T(8,128)} %copy-done.22, f32[16,256,96]{1,2,0:T(8,128)} %fusion.106, ...), kind=kLoop, calls=%fused_computation.76 | loop fusion | flops 3932160 | bytes 15729408 | tf_op jit(solution)/shard_map/jit(_where)/select_n | solution.py:154
  331.2 5.4 copy.333
  336.6 4.9 fusion.145
  344.0 7.9 %all-to-all-start.3 = ((f32[2,96,16,256]{1,2,0,3:T(8,128)}), f32[2,96,16,256]{1,2,0,3:T(8,128)}, u32[]{:S(2)}, u32[]{:S(2)}) async-start(f32[2,96,16,256]{1,2,0,3:T(8,128)} %copy.333), calls=%async_computation.3 | async-start | bytes 8388608 | tf_op jit(solution)/shard_map/all_to_all | solution.py:166
  352.2 5.1 fusion.140
  363.6 3.6 fusion.205
  376.8 20.0 %mul.457 = f32[1,36864]{0,1:T(8,128)} reshape(f32[1,4,96,96]{3,2,1,0:T(8,128)S(1)} %maximum_multiply_fusion.7) | data formatting | bytes 294912 | tf_op jit(solution)/shard_map/mul | solution.py:161
  396.8 206.6 %reduce-scatter.4.cloned.1.call-done = f32[1152,1]{1,0:T(8,128)} async-done(((f32[36864,1]{1,0:T(8,128)}), f32[1152,1]{1,0:T(8,128)}) %reduce-scatter.4.cloned.1.call-update) | async-done | bytes 4624
  605.2 4.6 copy.576
  618.4 15.6 %fusion.24 = f32[96,8,1024]{2,1,0:T(8,128)} fusion(f32[96,512,8]{1,2,0:T(8,128)} %copy.298), kind=kOutput, calls=%fused_computation.42 | convolution fusion | flops 4839178240 | bytes 4718592 | tf_op jit(solution)/shard_map/cmr,mn->crn/dot_general | solution.py:14
  634.0 4.6 copy.575
  642.5 15.9 %fusion.22 = f32[96,8,1024]{2,1,0:T(8,128)} fusion(f32[96,512,8]{1,2,0:T(8,128)} %copy.338), kind=kOutput, calls=%fused_computation.40 | convolution fusion | flops 4839178240 | bytes 4718592 | tf_op jit(solution)/shard_map/cmr,mn->crn/dot_general | solution.py:14
  663.1 17.8 %fusion.421 = (f32[8,1024]{1,0:T(8,128)}, f32[8,1024]{1,0:T(8,128)}, f32[96,8,1024]{2,1,0:T(8,128)}) fusion(f32[8,1024]{1,0:T(8,128)S(1)} %get-tuple-element.20, f32[8,1024]{1,0:T(8,128)S(1)} %get-tuple-element.19, bf16[96,8,1024]{2,1,0:T(8,128)(2,1)S(1)} %copy-done.18, f32[96]{0:T(128)S(1)} %copy-done.35, f32[96,8,1024]{2,1,0:T(8,128)} %fusion.22, ...), kind=kOutput, calls=%fused_computation.374 | convolution fusion | flops 4847812608 | bytes 11141504 | tf_op jit(solution)/shard_map/cmr,mn->crn/dot_general | solution.py:14
  680.9 16.3 %fusion.11 = bf16[96,8,1024]{2,1,0:T(8,128)(2,1)} fusion(bf16[96,8,1024]{2,1,0:T(8,128)(2,1)S(1)} %copy-done.18, f32[96,8,1024]{2,1,0:T(8,128)} %fusion.24, f32[96,512,8]{1,2,0:T(8,128)S(1)} %copy-done.28, f32[96]{0:T(128)S(1)} %copy-done.34, f32[96]{0:T(128)S(1)} %copy-done.35, f32[8,1024]{1,0:T(8,128)S(1)} %get-tuple-element.20, ...), kind=kOutput, calls=%fused_computation.19 | convolution fusion | flops 4847042560 | bytes 7930624 | tf_op jit(solution)/shard_map/cmr,mn->crn/dot_general | solution.py:14
  697.2 32.2 %all-reduce.5.cloned.1.call-done = (f32[8,1024]{1,0:T(8,128)}, f32[8,1024]{1,0:T(8,128)}) async-done(((f32[8,1024]{1,0:T(8,128)}, f32[8,1024]{1,0:T(8,128)}), (f32[8,1024]{1,0:T(8,128)}, f32[8,1024]{1,0:T(8,128)})) %all-reduce.5.cloned.1.call-update) | async-done | bytes 65552 | tf_op jit(solution)/shard_map/psum | solution.py:174
  731.0 4.5 fusion.1
  (155 shorter events, 159.1 us)
Async XLA Ops:
  7.2 12.5 %copy-start.30 = (bf16[96,8,1024]{2,1,0:T(8,128)(2,1)S(1)}, bf16[96,8,1024]{2,1,0:T(8,128)(2,1)}, u32[]{:S(2)}) copy-start(bf16[96,8,1024]{2,1,0:T(8,128)(2,1)} %param.9) | copy-start | bytes 4718596
  34.8 10.6 %copy-start.17 = (bf16[96,8,1024]{2,1,0:T(8,128)(2,1)S(1)}, bf16[96,8,1024]{2,1,0:T(8,128)(2,1)}, u32[]{:S(2)}) copy-start(bf16[96,8,1024]{2,1,0:T(8,128)(2,1)} %param.8) | copy-start | bytes 4718596
  34.8 90.5 %all-to-all-start.2 = ((f32[2,96,512,8]{1,3,0,2:T(8,128)}), f32[2,96,512,8]{1,3,0,2:T(8,128)}, u32[]{:S(2)}, u32[]{:S(2)}) async-start(f32[2,96,512,8]{1,3,0,2:T(8,128)} %copy.301), calls=%async_computation.2 | async-start | bytes 8388608 | tf_op jit(solution)/shard_map/all_to_all | solution.py:125
  44.9 48.0 %copy-start.34 = (f32[96]{0:T(128)S(1)}, f32[96]{0:T(128)}, u32[]{:S(2)}) copy-start(f32[96]{0:T(128)} %param.11) | copy-start | bytes 1156
  44.9 48.0 %copy-start.35 = (f32[96]{0:T(128)S(1)}, f32[96]{0:T(128)}, u32[]{:S(2)}) copy-start(f32[96]{0:T(128)} %param.10) | copy-start | bytes 1156
  44.9 47.2 %all-reduce.7.cloned.1.call-start = ((), (), s32[]{:S(2)}) async-start(), calls=%async_computation.7 | async-start | bytes 131072 | tf_op jit(solution)/shard_map/psum | solution.py:111
  125.4 7.4 copy-start.32
  125.4 7.4 copy-start.33
  125.4 64.0 %all-to-all-start = ((f32[2,96,512,8]{1,3,0,2:T(8,128)}), f32[2,96,512,8]{1,3,0,2:T(8,128)}, u32[]{:S(2)}, u32[]{:S(2)}) async-start(f32[2,96,512,8]{1,3,0,2:T(8,128)} %copy.265), calls=%async_computation | async-start | bytes 8388608 | tf_op jit(solution)/shard_map/all_to_all | solution.py:124
  140.7 5.9 copy-start.13
  146.7 3.6 copy-start.11
  197.2 3.5 copy-start.24
  213.1 17.6 %copy-start.19 = (f32[16,256,96]{1,2,0:T(8,128)}, f32[16,256,96]{1,2,0:T(8,128)S(1)}, u32[]{:S(2)}) copy-start(f32[16,256,96]{1,2,0:T(8,128)S(1)} %fusion.138) | copy-start | bytes 4718596
  215.6 7.6 %copy-start.20 = (f32[16,256,96]{1,2,0:T(8,128)}, f32[16,256,96]{1,2,0:T(8,128)S(1)}, u32[]{:S(2)}) copy-start(f32[16,256,96]{1,2,0:T(8,128)S(1)} %fusion.136) | copy-start | bytes 4718596
  220.8 9.9 %copy-start.21 = (f32[16,256,96]{1,2,0:T(8,128)}, f32[16,256,96]{1,2,0:T(8,128)S(1)}, u32[]{:S(2)}) copy-start(f32[16,256,96]{1,2,0:T(8,128)S(1)} %fusion.132) | copy-start | bytes 4718596
  242.5 2.8 copy-start.14
  247.9 3.6 copy-start.4
  259.8 3.6 copy-start.6
  280.4 63.6 %all-to-all-start.1 = ((f32[2,96,16,256]{1,2,0,3:T(8,128)}), f32[2,96,16,256]{1,2,0,3:T(8,128)}, u32[]{:S(2)}, u32[]{:S(2)}) async-start(f32[2,96,16,256]{1,2,0,3:T(8,128)} %copy.293), calls=%async_computation.1 | async-start | bytes 8388608 | tf_op jit(solution)/shard_map/all_to_all | solution.py:165
  306.2 8.1 %copy-start.9 = (f32[96,16,256]{2,1,0:T(8,128)}, f32[96,16,256]{2,1,0:T(8,128)S(1)}, u32[]{:S(2)}) copy-start(f32[96,16,256]{2,1,0:T(8,128)S(1)} %get-tuple-element.29) | copy-start | bytes 4718596
  306.2 10.6 %copy-start.7 = (f32[96,16,256]{2,1,0:T(8,128)}, f32[96,16,256]{2,1,0:T(8,128)S(1)}, u32[]{:S(2)}) copy-start(f32[96,16,256]{2,1,0:T(8,128)S(1)} %get-tuple-element.28) | copy-start | bytes 4718596
  344.0 290.0 %all-to-all-start.3 = ((f32[2,96,16,256]{1,2,0,3:T(8,128)}), f32[2,96,16,256]{1,2,0,3:T(8,128)}, u32[]{:S(2)}, u32[]{:S(2)}) async-start(f32[2,96,16,256]{1,2,0,3:T(8,128)} %copy.333), calls=%async_computation.3 | async-start | bytes 8388608 | tf_op jit(solution)/shard_map/all_to_all | solution.py:166
  351.9 251.4 %reduce-scatter.4.cloned.1.call-start = ((), (), s32[]{:S(2)}) async-start(), calls=%async_computation.5 | async-start | bytes 19464192
  352.1 5.1 copy-start.10
  360.4 3.2 copy-start.3
  360.4 3.2 copy-start.5
  363.6 3.6 copy-start.1
  367.2 3.2 copy-start.8
  396.8 332.7 %all-reduce.5.cloned.1.call-start = ((), (), s32[]{:S(2)}) async-start(), calls=%async_computation.6 | async-start | bytes 131072 | tf_op jit(solution)/shard_map/psum | solution.py:174
  642.5 15.9 %copy-start.23 = (f32[1,96,32,16,8]{1,4,2,3,0:T(8,128)S(1)}, f32[1,96,32,16,8]{1,4,2,3,0:T(8,128)}, u32[]{:S(2)}) copy-start(f32[1,96,32,16,8]{1,4,2,3,0:T(8,128)} %get-tuple-element.11) | copy-start | bytes 4718596
  660.1 3.1 copy-start.18
  663.1 17.8 %copy-start.28 = (f32[96,512,8]{1,2,0:T(8,128)S(1)}, f32[96,512,8]{1,2,0:T(8,128)}, u32[]{:S(2)}) copy-start(f32[96,512,8]{1,2,0:T(8,128)} %copy.296) | copy-start | bytes 4718596
  (11 other events, 24.5 us)
Sparse Core Ops, SparseCore 0:
  48.9 43.2 all-reduce.6
  396.9 206.4 reduce-scatter.3
  681.1 48.3 all-reduce.4
where the time goes:
time: 752 us; the launch traced here: 743 us
  waiting for transfers between devices  323 us (43%)
  matrix products  239 us (32%)
  local copies, waits for them, and re-layouts  90.2 us (12%)
  other arithmetic  40.2 us (5%)
  starting transfers between devices  35.4 us (5%)
  between operations  15.1 us (2%)
    dot_general x48, matrix products, contract(): return jnp.einsum(form, left, right, precision=highest)  239 us
    unnamed x4, waiting for transfers between devices  207 us
    psum x1, waiting for transfers between devices, per_device(): lax.psum((jnp.sum(tok_val, axis=0), jnp.sum(tok_val * tok_val, axis=0)),...  45.6 us
    all_to_all x1, waiting for transfers between devices, per_device(): lax.all_to_all(spec_field, 'lat', split_axis=2, concat_axis=3, tiled=True)  35.6 us
    psum x1, waiting for transfers between devices, per_device(): lax.psum((jnp.sum(dnorm, axis=0), jnp.sum(dnorm * normed, axis=0)), 'grp')  32.2 us
    mul x1, local copies, waits for them, and re-layouts, per_device(): grad_stack.reshape(block_count, 4 * block_size * block_size)  20 us
    select_n x1, other arithmetic, per_device(): d_pre_imag = jnp.where(pre_imag > 0.0, d_act_imag, 0.0)  16.5 us
  transfers between devices with their start and end apart: 7, of which 5 were waited for; matrix products, arithmetic and copies ran while one was open for 27% of the time, Pallas kernels for 0%

commit v1 on v0

v1 whole, which is shorter than its diff:
```python
import functools
import math

import jax
import jax.numpy as jnp
import ml_dtypes
import numpy as np
from jax import lax
from jax.experimental import pallas as pl
from jax.experimental.pallas import tpu as pltpu
from jax.sharding import PartitionSpec as P

shrink_level = 0.01
norm_eps = 1e-05
f32 = jnp.float32
bf16 = jnp.bfloat16

CH = 96
RW = 8
LON = 1024
HALF = 512
PEERS = 32
LANES = RW * CH
QB = 4
KB = 128
STEPS = 4
TILES = LANES // 128
WIRE_SHAPE = jax.ShapeDtypeStruct((PEERS, TILES, 32, 128), jnp.float32)


def host_split(table):
    high = table.astype(ml_dtypes.bfloat16)
    low = (table - high.astype(np.float64)).astype(ml_dtypes.bfloat16)
    return np.stack([high, low])


def lon_table():
    parts = []
    n = np.arange(HALF)
    for parity in range(2):
        m = 2 * np.arange(256) + parity
        theta = 2.0 * np.pi * ((m[:, None] * n[None, :]) % LON) / LON
        table = np.stack([np.cos(theta), -np.sin(theta)], axis=1).reshape(HALF, HALF)
        parts.append(host_split(table / 32.0))
    return np.stack(parts)


def lat_table():
    parts = []
    row = np.arange(RW)[:, None]
    peer = np.arange(16)[None, :]
    place = (8 * peer + row).reshape(-1)
    for parity in range(2):
        k = 2 * np.arange(KB) + parity
        theta = 2.0 * np.pi * ((k[:, None] * place[None, :]) % 256) / 256
        c, s = np.cos(theta), np.sin(theta)
        table = np.concatenate(
            [np.concatenate([c, s], axis=1), np.concatenate([-s, c], axis=1)], axis=0
        )
        parts.append(host_split(table / 16.0))
    return np.stack(parts)


def split(value):
    high = value.astype(bf16)
    low = (value - high.astype(f32)).astype(bf16)
    return high, low


def dot(left, right, dims=((1,), (0,))):
    return lax.dot_general(left, right, (dims, ((), ())), preferred_element_type=f32)


NT = ((1,), (1,))
TN = ((0,), (0,))


def dot3(left, right, dims=((1,), (0,))):
    return (
        dot(left[0], right[0], dims) + dot(left[0], right[1], dims) + dot(left[1], right[0], dims)
    )


def fill_halves(rows_ref, halves_ref, gain_ref):
    for r in range(RW):
        own = jnp.concatenate(
            [rows_ref[tile, pl.ds(r, CH, stride=RW), :] for tile in range(8)], axis=1
        )
        if gain_ref is not None:
            own = own * gain_ref[...]
        first, second = own[:, :HALF], own[:, HALF:]
        at = pl.ds(r * CH, CH)
        for parity, value in enumerate((first + second, first - second)):
            high, low = split(value)
            halves_ref[parity, 0, at, :] = high
            halves_ref[parity, 1, at, :] = low


def put_tiles(out_ref, value):
    for tile in range(TILES):
        out_ref[:, tile] = value[:, tile * 128 : tile * 128 + 128].reshape(16, 32, 128)


def lon_grad_kernel(x_ref, tab_ref, out_ref, rows_ref, halves_ref):
    parity = pl.program_id(0)

    @pl.when(parity == 0)
    def _():
        for tile in range(8):
            value = x_ref[:, :, tile * 128 : tile * 128 + 128].astype(f32) * 2.0
            rows_ref[tile] = value.reshape(LANES, 128)
        fill_halves(rows_ref, halves_ref, None)

    table = (tab_ref[0, 0], tab_ref[0, 1])
    put_tiles(out_ref, dot3(table, (halves_ref[parity, 0], halves_ref[parity, 1]), NT))

    @pl.when(parity == 0)
    def _():
        out_ref[0, :, 0:2, :] = out_ref[0, :, 0:2, :] * 0.5


def lon_field_kernel(x_ref, stat_ref, gain_ref, shift_ref, tab_ref, out_ref, rows_ref, halves_ref):
    parity = pl.program_id(0)

    @pl.when(parity == 0)
    def _():
        for tile in range(8):
            lanes = slice(tile * 128, tile * 128 + 128)
            value = x_ref[:, :, lanes].astype(f32)
            value = (value - stat_ref[0, :, lanes][None]) * stat_ref[1, :, lanes][None]
            rows_ref[tile] = value.reshape(LANES, 128)
        fill_halves(rows_ref, halves_ref, gain_ref)

    table = (tab_ref[0, 0], tab_ref[0, 1])
    put_tiles(out_ref, dot3(table, (halves_ref[parity, 0], halves_ref[parity, 1]), NT))

    @pl.when(parity == 0)
    def _():
        for tile in range(TILES):
            out_ref[0, tile, 0:1, :] = out_ref[0, tile, 0:1, :] + shift_ref[tile] * 32.0


def lon_forward_call(kernel, name, small_specs):
    return pl.pallas_call(
        kernel,
        name=name,
        grid=(2,),
        in_specs=[pl.BlockSpec((CH, RW, LON), lambda i: (0, 0, 0))]
        + small_specs
        + [pl.BlockSpec((1, 2, HALF, HALF), lambda i: (i, 0, 0, 0))],
        out_specs=pl.BlockSpec((16, TILES, 32, 128), lambda i: (i, 0, 0, 0)),
        out_shape=WIRE_SHAPE,
        scratch_shapes=[
            pltpu.VMEM((8, LANES, 128), f32),
            pltpu.VMEM((2, 2, LANES, HALF), bf16),
        ],
        compiler_params=pltpu.CompilerParams(vmem_limit_bytes=40 * 2**20),
        cost_estimate=pl.CostEstimate(
            flops=6 * LANES * LON * LON, bytes_accessed=7 * 2**20, transcendentals=0
        ),
    )


def unpack_rows(block_ref, halves_ref):
    lane = lax.broadcasted_iota(jnp.int32, (16, 128), 1)
    for q in range(QB):
        for part in range(2):
            own = [
                block_ref[pl.ds(tile * 8 + 2 * q + part, PEERS, stride=TILES * 8), :]
                for tile in range(TILES)
            ]
            first, second = [v[0:16] for v in own], [v[16:32] for v in own]
            sums = [a + b for a, b in zip(first, second)]
            differences = [a - b for a, b in zip(first, second)]
            for parity, value in enumerate((sums, differences)):
                for r in range(RW):
                    tile, skip = divmod(r * CH, 128)
                    piece = value[tile]
                    if skip:
                        piece = pltpu.roll(piece, 128 - skip, 1)
                    if skip + CH > 128:
                        after = pltpu.roll(value[tile + 1], 128 - skip, 1)
                        piece = jnp.where(lane < 128 - skip, piece, after)
                    high, low = split(piece)
                    at = (pl.ds((part * RW + r) * 16, 16), pl.ds(q * 128, 128))
                    halves_ref[(parity, 0) + at] = high
                    halves_ref[(parity, 1) + at] = low


def pack_rows(even, odd, block_ref):
    lane = lax.broadcasted_iota(jnp.int32, (16, 128), 1)
    for q in range(QB):
        for part in range(2):
            e = [even[(part * RW + r) * 16 : (part * RW + r + 1) * 16, q * 128 : q * 128 + 128] for r in range(RW)]
            o = [odd[(part * RW + r) * 16 : (part * RW + r + 1) * 16, q * 128 : q * 128 + 128] for r in range(RW)]
            for side in range(2):
                y = [a + b if side == 0 else a - b for a, b in zip(e, o)]
                for tile in range(TILES):
                    out = None
                    for r in range(RW):
                        low = r * CH - tile * 128
                        if low >= 128 or low + CH <= 0:
                            continue
                        piece = y[r] if low == 0 else pltpu.roll(y[r], low % 128, 1)
                        if out is None:
                            out = piece
                        else:
                            out = jnp.where(lane < low, out, piece)
                    start = (side * 16 * TILES + tile) * 8 + 2 * q + part
                    block_ref[pl.ds(start, 16, stride=TILES * 8), :] = out


def by_frequency(even, odd):
    rows = []
    for q in range(QB):
        for value in (even, odd):
            lanes = slice(q * 128, q * 128 + 128)
            rows.append(jnp.concatenate([value[0:KB, lanes], value[KB : 2 * KB, lanes]], axis=1))
    return jnp.concatenate(rows, axis=0)


def by_part(rows):
    out = []
    for parity in range(2):
        parts = []
        for part in range(2):
            lanes = slice(part * 128, part * 128 + 128)
            parts.append(
                jnp.concatenate(
                    [rows[(2 * q + parity) * KB : (2 * q + parity + 1) * KB, lanes] for q in range(QB)],
                    axis=1,
                )
            )
        out.append(jnp.concatenate(parts, axis=0))
    return out


def lat_forward(block_ref, tab_ref, halves_ref):
    unpack_rows(block_ref, halves_ref)
    out = [
        dot3(
            (tab_ref[parity, 0], tab_ref[parity, 1]),
            (halves_ref[parity, 0], halves_ref[parity, 1]),
        )
        for parity in range(2)
    ]
    return by_frequency(out[0], out[1])


def lat_inverse(rows, tab_ref, block_ref):
    even, odd = by_part(rows)
    pack_rows(dot(tab_ref[0, 0], even, TN), dot(tab_ref[1, 0], odd, TN), block_ref)


def fill_weight(w_ref, out_ref):
    full = jnp.zeros((256, 256), f32)
    out_ref[...] = full
    real, imag = w_ref[0, 0], w_ref[0, 1]
    out_ref[0:CH, 0:CH] = real
    out_ref[0:CH, 128 : 128 + CH] = imag
    out_ref[128 : 128 + CH, 0:CH] = -imag
    out_ref[128 : 128 + CH, 128 : 128 + CH] = real


def fill_bias(b_ref, out_ref):
    out_ref[...] = jnp.zeros((8, 256), f32)
    out_ref[0:1, 0:CH] = b_ref[0, 0:1, :]
    out_ref[0:1, 128 : 128 + CH] = b_ref[0, 1:2, :]


def grad_modes_kernel(block_ref, tab_ref, out_ref, halves_ref):
    out_ref[...] = lat_forward(block_ref.reshape(PEERS * TILES * 8, 128), tab_ref, halves_ref)


def field_modes_kernel(
    block_ref, tab_ref, w_in_ref, b_in_ref, w_out_ref, b_out_ref,
    back_ref, spec_ref, act_ref, mask_ref,
    halves_ref, full_ref, weight_ref, bias_ref,
):
    @pl.when(pl.program_id(0) == 0)
    def _():
        for at, (w_ref, b_ref) in enumerate(((w_in_ref, b_in_ref), (w_out_ref, b_out_ref))):
            fill_weight(w_ref, full_ref)
            weight_ref[at, 0], weight_ref[at, 1] = split(full_ref[...])
            fill_bias(b_ref, bias_ref.at[at])

    spec = split(lat_forward(block_ref.reshape(PEERS * TILES * 8, 128), tab_ref, halves_ref))
    spec_ref[...] = spec[0]
    act = dot3(spec, (weight_ref[0, 0], weight_ref[0, 1])) + bias_ref[0, 0:1, :]
    act = split(jnp.maximum(act, 0.0))
    act_ref[...] = act[0]
    post = dot3(act, (weight_ref[1, 0], weight_ref[1, 1])) + bias_ref[1, 0:1, :]
    mask_ref[...] = jnp.where(jnp.abs(post) > shrink_level, 1.0, 0.0).astype(bf16)
    shrunk = post - jnp.clip(post, -shrink_level, shrink_level)
    lat_inverse(shrunk.astype(bf16), tab_ref, back_ref.reshape(PEERS * TILES * 8, 128))


def pull_modes_kernel(
    grad_ref, spec_ref, act_ref, mask_ref, tab_ref, w_in_ref, w_out_ref,
    back_ref, g_ref,
    full_ref, weight_ref, sum_ref,
):
    step = pl.program_id(0)

    @pl.when(step == 0)
    def _():
        for at, w_ref in enumerate((w_in_ref, w_out_ref)):
            fill_weight(w_ref, full_ref)
            weight_ref[at] = full_ref[...].astype(bf16)
        sum_ref[...] = jnp.zeros_like(sum_ref)

    spec, act = spec_ref[...], act_ref[...]
    d_post = jnp.where(mask_ref[...] > 0.5, grad_ref[...].astype(bf16), jnp.zeros((), bf16))
    sum_ref[1] += dot(act, d_post, TN)
    d_act = dot(d_post, weight_ref[1], NT)
    d_pre = jnp.where(act > 0, d_act.astype(bf16), jnp.zeros((), bf16))
    sum_ref[0] += dot(spec, d_pre, TN)
    d_spec = dot(d_pre, weight_ref[0], NT)
    lat_inverse(d_spec.astype(bf16), tab_ref, back_ref.reshape(PEERS * TILES * 8, 128))

    @pl.when(step == STEPS - 1)
    def _():
        scale = 1.0 / math.sqrt(131072.0)
        for at in range(2):
            total = sum_ref[at]
            rr, ri = total[0:CH, 0:CH], total[0:CH, 128 : 128 + CH]
            ir, ii = total[128 : 128 + CH, 0:CH], total[128 : 128 + CH, 128 : 128 + CH]
            g_ref[2 * at] = (rr + ii) * scale
            g_ref[2 * at + 1] = (ri - ir) * scale


WIRE = pl.BlockSpec((PEERS, TILES, 8, 128), lambda i: (0, 0, i, 0))
LAT_TAB = pl.BlockSpec((2, 2, 256, 256), lambda i: (0, 0, 0, 0))
MODES = pl.BlockSpec((1024, 256), lambda i: (i, 0))
WEIGHT = pl.BlockSpec((1, 2, CH, CH), lambda i: (0, 0, 0, 0))
BIAS = pl.BlockSpec((1, 2, CH), lambda i: (0, 0, 0))


def modes_shape(dtype):
    return jax.ShapeDtypeStruct((4096, 256), dtype)


def grad_modes(block, table):
    return pl.pallas_call(
        grad_modes_kernel,
        name="grad_modes",
        grid=(STEPS,),
        in_specs=[WIRE, LAT_TAB],
        out_specs=MODES,
        out_shape=modes_shape(f32),
        scratch_shapes=[pltpu.VMEM((2, 2, 256, QB * 128), bf16)],
        compiler_params=pltpu.CompilerParams(vmem_limit_bytes=40 * 2**20),
        cost_estimate=pl.CostEstimate(
            flops=6 * 2**31, bytes_accessed=8 * 2**20, transcendentals=0
        ),
    )(block, table)


def field_modes(block, table, w_in, b_in, w_out, b_out):
    return pl.pallas_call(
        field_modes_kernel,
        name="field_modes",
        grid=(STEPS,),
        in_specs=[WIRE, LAT_TAB, WEIGHT, BIAS, WEIGHT, BIAS],
        out_specs=[WIRE, MODES, MODES, MODES],
        out_shape=[WIRE_SHAPE, modes_shape(bf16), modes_shape(bf16), modes_shape(bf16)],
        scratch_shapes=[
            pltpu.VMEM((2, 2, 256, QB * 128), bf16),
            pltpu.VMEM((256, 256), f32),
            pltpu.VMEM((2, 2, 256, 256), bf16),
            pltpu.VMEM((2, 8, 256), f32),
        ],
        compiler_params=pltpu.CompilerParams(vmem_limit_bytes=48 * 2**20),
        cost_estimate=pl.CostEstimate(
            flops=12 * 2**31, bytes_accessed=14 * 2**20, transcendentals=0
        ),
    )(block, table, w_in, b_in, w_out, b_out)


def pull_modes(grad, spec, act, mask, table, w_in, w_out):
    return pl.pallas_call(
        pull_modes_kernel,
        name="pull_modes",
        grid=(STEPS,),
        in_specs=[MODES, MODES, MODES, MODES, LAT_TAB, WEIGHT, WEIGHT],
        out_specs=[WIRE, pl.BlockSpec((4, CH, CH), lambda i: (0, 0, 0))],
        out_shape=[WIRE_SHAPE, jax.ShapeDtypeStruct((4, CH, CH), f32)],
        scratch_shapes=[
            pltpu.VMEM((256, 256), f32),
            pltpu.VMEM((2, 256, 256), bf16),
            pltpu.VMEM((2, 256, 256), f32),
        ],
        compiler_params=pltpu.CompilerParams(vmem_limit_bytes=48 * 2**20),
        cost_estimate=pl.CostEstimate(
            flops=8 * 2**31, bytes_accessed=14 * 2**20, transcendentals=0
        ),
    )(grad, spec, act, mask, table, w_in, w_out)


def lon_inverse(block_ref, tab_ref, rows_ref, weighted):
    sides = []
    for parity in range(2):
        value = jnp.concatenate(
            [
                block_ref[pl.ds(parity * 16, 16), tile].reshape(HALF, 128)
                for tile in range(TILES)
            ],
            axis=1,
        )
        if weighted:
            value = value * 2.0
            if parity == 0:
                row = lax.broadcasted_iota(jnp.int32, (HALF, 1), 0)
                value = value * jnp.where(row == 0, 0.5, 1.0)
        sides.append(dot(value.astype(bf16), tab_ref[parity, 0], TN))
    first, second = sides[0] + sides[1], sides[0] - sides[1]
    for r in range(RW):
        at, rows = pl.ds(r, CH, stride=RW), slice(r * CH, (r + 1) * CH)
        for tile in range(4):
            lanes = slice(tile * 128, tile * 128 + 128)
            rows_ref[tile, at, :] = first[rows, lanes]
            rows_ref[4 + tile, at, :] = second[rows, lanes]


def mixed_kernel(block_ref, tab_ref, tok_ref, stat_ref, gain_ref, shift_ref, out_ref, rows_ref):
    lon_inverse(block_ref, tab_ref, rows_ref, True)
    for tile in range(8):
        lanes = slice(tile * 128, tile * 128 + 128)
        tok = tok_ref[:, :, lanes].astype(f32)
        normed = (tok - stat_ref[0, :, lanes][None]) * stat_ref[1, :, lanes][None]
        normal = normed * gain_ref[...] + shift_ref[...]
        filtered = rows_ref[tile].reshape(CH, RW, 128)
        out_ref[:, :, lanes] = (filtered + normal + tok).astype(bf16)


def pulled_kernel(block_ref, tab_ref, tok_ref, cot_ref, stat_ref, gain_ref, out_ref, sum_ref, rows_ref):
    lon_inverse(block_ref, tab_ref, rows_ref, False)
    for tile in range(8):
        lanes = slice(tile * 128, tile * 128 + 128)
        tok = tok_ref[:, :, lanes].astype(f32)
        normed = (tok - stat_ref[0, :, lanes][None]) * stat_ref[1, :, lanes][None]
        pulled = rows_ref[tile].reshape(CH, RW, 128)
        dnorm = (pulled + cot_ref[:, :, lanes].astype(f32)) * gain_ref[...]
        out_ref[:, :, lanes] = dnorm
        sum_ref[0, :, lanes] = jnp.sum(dnorm, axis=0)
        sum_ref[1, :, lanes] = jnp.sum(dnorm * normed, axis=0)


def whole_call(kernel, name, out_shape):
    return pl.pallas_call(
        kernel,
        name=name,
        out_shape=out_shape,
        scratch_shapes=[pltpu.VMEM((8, LANES, 128), f32)],
        compiler_params=pltpu.CompilerParams(vmem_limit_bytes=48 * 2**20),
        cost_estimate=pl.CostEstimate(
            flops=4 * LANES * LON * LON, bytes_accessed=10 * 2**20, transcendentals=0
        ),
    )


def exchange(value):
    return lax.all_to_all(value, "lat", split_axis=0, concat_axis=0, tiled=True)


def sum_groups(value):
    return jnp.sum(lax.all_gather(value, "grp"), axis=0)


def per_device(tokens, cotangent, gain, shift, w_in, b_in, w_out, b_out):
    all_chans = CH * lax.axis_size("grp")
    lon_tab, lat_tab = jnp.asarray(lon_table()), jnp.asarray(lat_table())
    tok_val = tokens.astype(f32)
    sums = sum_groups(jnp.stack([jnp.sum(tok_val, axis=0), jnp.sum(tok_val * tok_val, axis=0)]))
    token_mean = sums[0] / all_chans
    inv_std = lax.rsqrt(sums[1] / all_chans - token_mean * token_mean + norm_eps)
    stats = jnp.stack([token_mean, inv_std])
    gain_col = gain.reshape(CH, 1)
    gain_cube = jnp.broadcast_to(gain.reshape(CH, 1, 1), (CH, 1, 128))
    shift_cube = jnp.broadcast_to(shift.reshape(CH, 1, 1), (CH, 1, 128))

    spec_grad = lon_forward_call(lon_grad_kernel, "lon_grad", [])(cotangent, lon_tab)
    modes_grad = exchange(spec_grad)
    small = [
        pl.BlockSpec((2, RW, LON), lambda i: (0, 0, 0)),
        pl.BlockSpec((CH, 1), lambda i: (0, 0)),
        pl.BlockSpec((TILES, 1, 128), lambda i: (0, 0, 0)),
    ]
    spec_field = lon_forward_call(lon_field_kernel, "lon_field", small)(
        tokens, stats, gain_col, jnp.tile(shift, RW).reshape(TILES, 1, 128), lon_tab
    )
    modes_field = exchange(spec_field)
    grad_rows = grad_modes(modes_grad, lat_tab)
    back_field, spec, act, mask = field_modes(modes_field, lat_tab, w_in, b_in, w_out, b_out)
    rows_field = exchange(back_field)
    back_grad, grads = pull_modes(grad_rows, spec, act, mask, lat_tab, w_in, w_out)
    rows_grad = exchange(back_grad)
    mixed = whole_call(mixed_kernel, "mixed", jax.ShapeDtypeStruct((CH, RW, LON), bf16))(
        rows_field, lon_tab, tokens, stats, gain_cube, shift_cube
    )
    dnorm, back = whole_call(
        pulled_kernel,
        "pulled",
        [jax.ShapeDtypeStruct((CH, RW, LON), f32), jax.ShapeDtypeStruct((2, RW, LON), f32)],
    )(rows_grad, lon_tab, tokens, cotangent, stats, gain_cube)
    back = sum_groups(back) / all_chans
    normed = (tok_val - token_mean) * inv_std
    grad_tokens = cotangent.astype(f32) + inv_std * (dnorm - back[0] - normed * back[1])
    shares = exchange(grads.reshape(PEERS, 1152))
    grad_weights = jnp.sum(shares, axis=0).reshape(1, 1152)
    return (mixed, grad_tokens.astype(bf16), grad_weights)


def solution(mesh):
    in_specs = (
        P("grp", "lat", None),
        P("grp", "lat", None),
        P("grp"),
        P("grp"),
        P("grp", None, None, None),
        P("grp", None, None),
        P("grp", None, None, None),
        P("grp", None, None),
    )
    out_specs = (P("grp", "lat", None), P("grp", "lat", None), P("grp", "lat"))
    return jax.shard_map(
        per_device, mesh=mesh, in_specs=in_specs, out_specs=out_specs, check_vma=False
    )
```

time: 752 us -> 264 us (0.35)
  waiting for transfers between devices: 323 us -> 34.1 us
  matrix products: 239 us -> 0 us
  blocking collectives: 0 us -> 133 us
  local copies, waits for them, and re-layouts: 90.2 us -> 14.5 us
  Pallas kernels: 0 us -> 47.7 us
  other arithmetic: 40.2 us -> 6.76 us
  between operations: 15.1 us -> 0.87 us
  starting transfers between devices: 35.4 us -> 25.1 us
    dot_general x48 -> x0, matrix products: 239 us -> none  [contract(): return jnp.einsum(form, left, right, precision=highest)]
    unnamed x4 -> x0, waiting for transfers between devices: 207 us -> none
    psum x2 -> x0, waiting for transfers between devices: 77.9 us -> none  [the longest x1 45.6 us: per_device(): lax.psum((jnp.sum(tok_val, axis=0), jnp.sum(tok_val * tok_val, axis=0)),...]
    all_gather x0 -> x2, blocking collectives: none -> 76.2 us  [sum_groups(): return jnp.sum(lax.all_gather(value, 'grp'), axis=0)]
    all_to_all x0 -> x2, blocking collectives: none -> 56.5 us  [exchange(): return lax.all_to_all(value, 'lat', split_axis=0, concat_axis=0, tiled=True)]
    pallas_call x0 -> x7, Pallas kernels: none -> 47.7 us  [the longest x1 13.9 us: field_modes(): pl.pallas_call(field_modes_kernel, name='field_modes', grid=(STEPS,), in_...]
    mul x4 -> x0, local copies, waits for them, and re-layouts: 28.3 us -> none  [the longest x1 20 us: per_device(): grad_stack.reshape(block_count, 4 * block_size * block_size)]
    slice x12 -> x0, local copies, waits for them, and re-layouts: 16.6 us -> none  [the longest x6 11.9 us: lat_forward(): real_part, imag_part = (stack[0], stack[1])]
  transfers between devices with their start and end apart: 7 -> 3, of which waited for: 5 -> 1; matrix products, arithmetic and copies ran while one was open for 27% -> 3% of each run, Pallas kernels for 0% -> 6%
where the time goes in v1:
time: 264 us; the launch traced here: 262 us
  blocking collectives  133 us (50%)
  Pallas kernels  47.7 us (18%)
  waiting for transfers between devices  34.1 us (13%)
  starting transfers between devices  25.1 us (10%)
  local copies, waits for them, and re-layouts  14.5 us (5%)
  other arithmetic  6.76 us (3%)
    all_gather x2, blocking collectives, sum_groups(): return jnp.sum(lax.all_gather(value, 'grp'), axis=0)  76.2 us
    all_to_all x2, blocking collectives, exchange(): return lax.all_to_all(value, 'lat', split_axis=0, concat_axis=0, tiled=True)  56.5 us
    all_to_all x3, waiting for transfers between devices, exchange(): return lax.all_to_all(value, 'lat', split_axis=0, concat_axis=0, tiled=True)  34.1 us
    all_to_all x3, starting transfers between devices, exchange(): return lax.all_to_all(value, 'lat', split_axis=0, concat_axis=0, tiled=True)  25.1 us
    pallas_call x1, Pallas kernels, field_modes(): pl.pallas_call(field_modes_kernel, name='field_modes', grid=(STEPS,), in_...  13.9 us
    unnamed x36, local copies, waits for them, and re-layouts  13.2 us
    pallas_call x1, Pallas kernels, pull_modes(): pl.pallas_call(pull_modes_kernel, name='pull_modes', grid=(STEPS,), in_sp...  7.75 us
    pallas_call x1, Pallas kernels, per_device(): whole_call(pulled_kernel, 'pulled', [jax.ShapeDtypeStruct((CH, RW, LON),...  6.28 us
  transfers between devices with their start and end apart: 3, of which 1 were waited for; matrix products, arithmetic and copies ran while one was open for 3% of the time, Pallas kernels for 6%

profile of v1, /device:TPU:1, one launch (start us, length us, event | category | flops | bytes accessed | tf_op | source)
XLA Modules:
  0.0 261.7 jit_solution(3860268920479447699)
XLA Ops:
  0.6 1.4 copy-done.3
  2.0 1.6 copy-done.9
  3.6 5.0 %lon_grad.1 = f32[32,6,32,128]{3,2,1,0:T(8,128)S(1)} custom-call(bf16[96,8,1024]{2,1,0:T(8,128)(2,1)S(1)} %copy-done.3, bf16[2,2,512,512]{3,2,1,0:T(8,128)(2,1)S(1)} %copy-done.9), custom_call_target="tpu_custom_call" | custom-call | flops 4831838208 | bytes 7340032 | tf_op jit(solution)/shard_map/lon_grad/pallas_call | solution.py:482
  8.6 1.7 copy-done.1
  10.3 10.1 %all-to-all-start.2 = ((f32[32,6,32,128]{3,2,1,0:T(8,128)}), f32[32,6,32,128]{3,2,1,0:T(8,128)}, u32[]{:S(2)}, u32[]{:S(2)}) async-start(f32[32,6,32,128]{3,2,1,0:T(8,128)} %copy-done.1), calls=%async_computation.2 | async-start | bytes 6291456 | tf_op jit(solution)/shard_map/all_to_all | solution.py:463
  20.6 0.4 convert_reduce_fusion
  21.0 41.6 %all-gather = f32[8,8,1024]{2,1,0:T(8,128)S(1)} all-gather(f32[2,8,1024]{2,1,0:T(8,128)S(1)} %pad_maximum_fusion), channel_id=2, replica_groups=mesh['lat'=32,'grp'=4] {'grp'}, dimensions={0}, use_global_device_ids=true | all-gather | bytes 327680 | tf_op jit(solution)/shard_map/all_gather | solution.py:467
  62.6 0.6 fusion.10
  63.2 1.6 copy-done.10
  64.8 4.0 %lon_field.1 = f32[32,6,32,128]{3,2,1,0:T(8,128)S(1)} custom-call(bf16[96,8,1024]{2,1,0:T(8,128)(2,1)S(1)} %copy-done, f32[2,8,1024]{2,1,0:T(8,128)S(1)} %pad_maximum_fusion.1.stat_ref, f32[96,1]{1,0:T(8,128)S(1)} %copy.14.gain_ref, f32[6,1,128]{2,1,0:T(1,128)S(1)} %reshape_tile.3.shift_ref, bf16[2,2,512,512]{3,2,1,0:T(8,128)(2,1)S(1)} %copy-done.10), custom_call_target="tpu_custom_call" | custom-call | flops 4831838208 | bytes 7340032 | tf_op jit(solution)/shard_map/lon_field/pallas_call | solution.py:489
  68.8 1.7 copy-done.2
  70.5 7.9 %all-to-all-start = ((f32[32,6,32,128]{3,2,1,0:T(8,128)}), f32[32,6,32,128]{3,2,1,0:T(8,128)}, u32[]{:S(2)}, u32[]{:S(2)}) async-start(f32[32,6,32,128]{3,2,1,0:T(8,128)} %copy-done.2), calls=%async_computation | async-start | bytes 6291456 | tf_op jit(solution)/shard_map/all_to_all | solution.py:463
  78.5 5.3 %grad_modes.1.grad_ref = f32[4096,256]{1,0:T(8,128)S(1)} custom-call(f32[32,6,32,128]{3,2,1,0:T(8,128)} %all-to-all-done.2.block_ref, bf16[2,2,256,256]{3,2,1,0:T(8,128)(2,1)S(1)} %copy-done.13), custom_call_target="tpu_custom_call" | custom-call | flops 12884901888 | bytes 8388608 | tf_op jit(solution)/shard_map/grad_modes/pallas_call | solution.py:344
  83.8 1.9 copy-done.14
  85.7 34.1 %all-to-all-done.block_ref = f32[32,6,32,128]{3,2,1,0:T(8,128)} async-done(((f32[32,6,32,128]{3,2,1,0:T(8,128)}), f32[32,6,32,128]{3,2,1,0:T(8,128)}, u32[]{:S(2)}, u32[]{:S(2)}) %all-to-all-start) | async-done | bytes 3145760 | tf_op jit(solution)/shard_map/all_to_all | solution.py:463
  119.8 13.9 %field_modes.1 = (f32[32,6,32,128]{3,2,1,0:T(8,128)}, bf16[4096,256]{1,0:T(8,128)(2,1)S(1)}, bf16[4096,256]{1,0:T(8,128)(2,1)S(1)}, bf16[4096,256]{1,0:T(8,128)(2,1)}) custom-call(f32[32,6,32,128]{3,2,1,0:T(8,128)} %all-to-all-done.block_ref, bf16[2,2,256,256]{3,2,1,0:T(8,128)(2,1)S(1)} %copy-done.13, f32[1,2,96,96]{3,2,1,0:T(8,128)S(1)} %copy-done.5, ...), custom_call_target="tpu_custom_call" | custom-call | flops 25769803776 | bytes 14680064 | tf_op jit(solution)/shard_map/field_modes/pallas_call | solution.py:360
  133.7 7.7 %pull_modes.1 = (f32[32,6,32,128]{3,2,1,0:T(8,128)}, f32[4,96,96]{2,1,0:T(8,128)S(1)}) custom-call(f32[4096,256]{1,0:T(8,128)} %copy-done.14, bf16[4096,256]{1,0:T(8,128)(2,1)S(1)} %get-tuple-element.12.spec_ref, bf16[4096,256]{1,0:T(8,128)(2,1)S(1)} %get-tuple-element.13.act_ref, bf16[4096,256]{1,0:T(8,128)(2,1)} %get-tuple-element.14.mask_ref, ...), custom_call_target="tpu_custom_call" | custom-call | flops 17179869184 | bytes 14680064 | tf_op jit(solution)/shard_map/pull_modes/pallas_call | solution.py:381
  141.5 0.2 all_to_all.24
  141.7 14.8 %all_to_all.30 = f32[32,1,1152]{2,1,0:T(1,128)S(1)} all-to-all(f32[32,1,1152]{2,1,0:T(1,128)S(1)} %all_to_all.24), channel_id=1, replica_groups=mesh['lat'=32,'grp'=4] {'lat'}, dimensions={0} | all-to-all | bytes 294912 | tf_op jit(solution)/shard_map/all_to_all | solution.py:463
  156.5 41.8 %all_to_all.31.block_ref = f32[32,6,32,128]{3,2,1,0:T(8,128)} all-to-all(f32[32,6,32,128]{3,2,1,0:T(8,128)} %get-tuple-element.15), channel_id=1, replica_groups=mesh['lat'=32,'grp'=4] {'lat'}, dimensions={0} | all-to-all | bytes 6291456 | tf_op jit(solution)/shard_map/all_to_all | solution.py:463
  198.2 7.2 %all-to-all-start.1 = ((f32[32,6,32,128]{3,2,1,0:T(8,128)}), f32[32,6,32,128]{3,2,1,0:T(8,128)}, u32[]{:S(2)}, u32[]{:S(2)}) async-start(f32[32,6,32,128]{3,2,1,0:T(8,128)} %get-tuple-element.11), calls=%async_computation.1 | async-start | bytes 6291456 | tf_op jit(solution)/shard_map/all_to_all | solution.py:463
  205.5 0.6 reshape.26
  206.1 0.2 broadcast_in_dim.4.gain_ref
  206.3 1.6 copy-done.11
  207.9 6.3 %pulled.1 = (f32[96,8,1024]{2,1,0:T(8,128)}, f32[2,8,1024]{2,1,0:T(8,128)S(1)}) custom-call(f32[32,6,32,128]{3,2,1,0:T(8,128)} %all_to_all.31.block_ref, bf16[2,2,512,512]{3,2,1,0:T(8,128)(2,1)S(1)} %copy-done.11, bf16[96,8,1024]{2,1,0:T(8,128)(2,1)S(1)} %copy-done, bf16[96,8,1024]{2,1,0:T(8,128)(2,1)S(1)} %copy-done.4, ...), custom_call_target="tpu_custom_call" | custom-call | flops 3221225472 | bytes 10485760 | tf_op jit(solution)/shard_map/pulled/pallas_call | solution.py:501
  214.2 34.6 %all-gather.1 = f32[8,8,1024]{2,1,0:T(8,128)S(1)} all-gather(f32[2,8,1024]{2,1,0:T(8,128)S(1)} %get-tuple-element.17), channel_id=3, replica_groups=mesh['lat'=32,'grp'=4] {'grp'}, dimensions={0}, use_global_device_ids=true | all-gather | bytes 327680 | tf_op jit(solution)/shard_map/all_gather | solution.py:467
  248.8 0.6 reduce_sum.48
  249.4 0.8 broadcast_multiply_fusion
  250.3 4.1 %fusion.6 = bf16[96,8,1024]{2,1,0:T(8,128)(2,1)} fusion(bf16[96,8,1024]{2,1,0:T(8,128)(2,1)S(1)} %copy-done, f32[96,8,1024]{2,1,0:T(8,128)} %get-tuple-element.16, bf16[96,8,1024]{2,1,0:T(8,128)(2,1)S(1)} %copy-done.4, f32[8,1024]{1,0:T(8,128)S(1)} %get-tuple-element.22, f32[8,1024]{1,0:T(8,128)} %get-tuple-element.23, f32[8,1024]{1,0:T(8,128)S(1)} %get-tuple-element.21, ...), kind=kLoop, calls=%fused_computation.9 | loop fusion | flops 7864320 | bytes 7995392 | tf_op jit(solution)/shard_map/convert_element_type | solution.py:511
  254.4 0.2 broadcast_in_dim.5.shift_ref
  254.5 1.6 copy-done.12
  256.1 5.6 %mixed.1 = bf16[96,8,1024]{2,1,0:T(8,128)(2,1)} custom-call(f32[32,6,32,128]{3,2,1,0:T(8,128)} %all-to-all-done.1.block_ref, bf16[2,2,512,512]{3,2,1,0:T(8,128)(2,1)S(1)} %copy-done.12, bf16[96,8,1024]{2,1,0:T(8,128)(2,1)S(1)} %copy-done, f32[2,8,1024]{2,1,0:T(8,128)S(1)} %pad_maximum_fusion.1.stat_ref, f32[96,1,128]{2,1,0:T(1,128)S(1)} %broadcast_in_dim.4.gain_ref, ...), custom_call_target="tpu_custom_call" | custom-call | flops 3221225472 | bytes 10485760 | tf_op jit(solution)/shard_map/mixed/pallas_call | solution.py:498
  (38 shorter events, 0.4 us)
Async XLA Ops:
  0.6 1.4 copy-start.3
  2.0 1.6 copy-start.9
  8.6 1.7 copy-start.1
  10.3 10.1 %copy-start.15 = (f32[96]{0:T(128)S(1)}, f32[96]{0:T(128)}, u32[]{:S(2)}) copy-start(f32[96]{0:T(128)} %param.12) | copy-start | bytes 1156
  10.3 10.2 %copy-start.16 = (f32[96]{0:T(128)S(1)}, f32[96]{0:T(128)}, u32[]{:S(2)}) copy-start(f32[96]{0:T(128)} %param.13) | copy-start | bytes 1156
  10.3 10.3 %copy-start = (bf16[96,8,1024]{2,1,0:T(8,128)(2,1)S(1)}, bf16[96,8,1024]{2,1,0:T(8,128)(2,1)}, u32[]{:S(2)}) copy-start(bf16[96,8,1024]{2,1,0:T(8,128)(2,1)} %tok_ref.3) | copy-start | bytes 4718596
  10.3 60.2 %all-to-all-start.2 = ((f32[32,6,32,128]{3,2,1,0:T(8,128)}), f32[32,6,32,128]{3,2,1,0:T(8,128)}, u32[]{:S(2)}, u32[]{:S(2)}) async-start(f32[32,6,32,128]{3,2,1,0:T(8,128)} %copy-done.1), calls=%async_computation.2 | async-start | bytes 6291456 | tf_op jit(solution)/shard_map/all_to_all | solution.py:463
  63.2 1.6 copy-start.10
  68.8 1.7 copy-start.2
  70.5 7.9 %copy-start.13 = (bf16[2,2,256,256]{3,2,1,0:T(8,128)(2,1)S(1)}, bf16[2,2,256,256]{3,2,1,0:T(8,128)(2,1)}, u32[]{:S(2)}) copy-start(bf16[2,2,256,256]{3,2,1,0:T(8,128)(2,1)} %constant.15.clone.tab_ref) | copy-start | bytes 1572868
  70.5 49.3 %all-to-all-start = ((f32[32,6,32,128]{3,2,1,0:T(8,128)}), f32[32,6,32,128]{3,2,1,0:T(8,128)}, u32[]{:S(2)}, u32[]{:S(2)}) async-start(f32[32,6,32,128]{3,2,1,0:T(8,128)} %copy-done.2), calls=%async_computation | async-start | bytes 6291456 | tf_op jit(solution)/shard_map/all_to_all | solution.py:463
  78.4 41.4 %copy-start.5 = (f32[1,2,96,96]{3,2,1,0:T(8,128)S(1)}, f32[1,2,96,96]{3,2,1,0:T(8,128)}, u32[]{:S(2)}) copy-start(f32[1,2,96,96]{3,2,1,0:T(8,128)} %w_in_ref.3) | copy-start | bytes 221188
  78.4 41.4 %copy-start.6 = (f32[1,2,96,96]{3,2,1,0:T(8,128)S(1)}, f32[1,2,96,96]{3,2,1,0:T(8,128)}, u32[]{:S(2)}) copy-start(f32[1,2,96,96]{3,2,1,0:T(8,128)} %w_out_ref.3) | copy-start | bytes 221188
  78.4 41.4 %copy-start.7 = (f32[1,2,96]{2,1,0:T(2,128)S(1)}, f32[1,2,96]{2,1,0:T(2,128)}, u32[]{:S(2)}) copy-start(f32[1,2,96]{2,1,0:T(2,128)} %b_in_ref.1) | copy-start | bytes 2308
  78.5 41.4 %copy-start.8 = (f32[1,2,96]{2,1,0:T(2,128)S(1)}, f32[1,2,96]{2,1,0:T(2,128)}, u32[]{:S(2)}) copy-start(f32[1,2,96]{2,1,0:T(2,128)} %b_out_ref.1) | copy-start | bytes 2308
  83.7 2.0 copy-start.14
  198.2 8.1 %copy-start.4 = (bf16[96,8,1024]{2,1,0:T(8,128)(2,1)S(1)}, bf16[96,8,1024]{2,1,0:T(8,128)(2,1)}, u32[]{:S(2)}) copy-start(bf16[96,8,1024]{2,1,0:T(8,128)(2,1)} %cot_ref.1) | copy-start | bytes 4718596
  198.2 56.1 %all-to-all-start.1 = ((f32[32,6,32,128]{3,2,1,0:T(8,128)}), f32[32,6,32,128]{3,2,1,0:T(8,128)}, u32[]{:S(2)}, u32[]{:S(2)}) async-start(f32[32,6,32,128]{3,2,1,0:T(8,128)} %get-tuple-element.11), calls=%async_computation.1 | async-start | bytes 6291456 | tf_op jit(solution)/shard_map/all_to_all | solution.py:463
  206.3 1.6 copy-start.11
  250.3 4.1 %copy-start.17 = (f32[96]{0:T(128)S(1)}, f32[96]{0:T(128)}, u32[]{:S(2)}) copy-start(f32[96]{0:T(128)} %param.13) | copy-start | bytes 1156
  254.5 1.6 copy-start.12

commit v2 on v1

--- a/solution.py
+++ b/solution.py
@@ -81,13 +81,11 @@
     )
 
 
-def fill_halves(rows_ref, halves_ref, gain_ref):
+def fill_halves(rows_ref, halves_ref):
     for r in range(RW):
         own = jnp.concatenate(
             [rows_ref[tile, pl.ds(r, CH, stride=RW), :] for tile in range(8)], axis=1
         )
-        if gain_ref is not None:
-            own = own * gain_ref[...]
         first, second = own[:, :HALF], own[:, HALF:]
         at = pl.ds(r * CH, CH)
         for parity, value in enumerate((first + second, first - second)):
@@ -96,11 +94,6 @@
             halves_ref[parity, 1, at, :] = low
 
 
-def put_tiles(out_ref, value):
-    for tile in range(TILES):
-        out_ref[:, tile] = value[:, tile * 128 : tile * 128 + 128].reshape(16, 32, 128)
-
-
 def lon_grad_kernel(x_ref, tab_ref, out_ref, rows_ref, halves_ref):
     parity = pl.program_id(0)
 
@@ -109,56 +102,118 @@
         for tile in range(8):
             value = x_ref[:, :, tile * 128 : tile * 128 + 128].astype(f32) * 2.0
             rows_ref[tile] = value.reshape(LANES, 128)
-        fill_halves(rows_ref, halves_ref, None)
+        fill_halves(rows_ref, halves_ref)
 
     table = (tab_ref[0, 0], tab_ref[0, 1])
-    put_tiles(out_ref, dot3(table, (halves_ref[parity, 0], halves_ref[parity, 1]), NT))
+    value = dot3(table, (halves_ref[parity, 0], halves_ref[parity, 1]), NT)
+    for tile in range(TILES):
+        out_ref[:, tile] = value[:, tile * 128 : tile * 128 + 128].reshape(16, 32, 128)
 
     @pl.when(parity == 0)
     def _():
         out_ref[0, :, 0:2, :] = out_ref[0, :, 0:2, :] * 0.5
 
 
-def lon_field_kernel(x_ref, stat_ref, gain_ref, shift_ref, tab_ref, out_ref, rows_ref, halves_ref):
-    parity = pl.program_id(0)
-
-    @pl.when(parity == 0)
-    def _():
-        for tile in range(8):
-            lanes = slice(tile * 128, tile * 128 + 128)
-            value = x_ref[:, :, lanes].astype(f32)
-            value = (value - stat_ref[0, :, lanes][None]) * stat_ref[1, :, lanes][None]
-            rows_ref[tile] = value.reshape(LANES, 128)
-        fill_halves(rows_ref, halves_ref, gain_ref)
-
-    table = (tab_ref[0, 0], tab_ref[0, 1])
-    put_tiles(out_ref, dot3(table, (halves_ref[parity, 0], halves_ref[parity, 1]), NT))
-
-    @pl.when(parity == 0)
-    def _():
+def row_lanes(values):
+    wide = jnp.concatenate([values, jnp.zeros((1, 128 - CH), f32)], axis=1)
+    wide = jnp.broadcast_to(wide, (8, 128))
+    lane = lax.broadcasted_iota(jnp.int32, (8, 128), 1)
+    tiles = []
+    for tile in range(TILES):
+        out = None
+        for r in range(RW):
+            low = r * CH - tile * 128
+            if low >= 128 or low + CH <= 0:
+                continue
+            piece = wide if low == 0 else pltpu.roll(wide, low % 128, 1)
+            out = piece if out is None else jnp.where(lane < low, out, piece)
+        tiles.append(out[0:1])
+    return tiles
+
+
+CHUNKS = 4
+
+
+def lon_field_kernel(
+    x_ref, sums_ref, gain_ref, shift_ref, tab_ref,
+    out_ref, stat_ref,
+    rows_ref, halves_ref, wire_ref, sems,
+):
+    first = sums_ref[0, 0] + sums_ref[1, 0] + sums_ref[2, 0] + sums_ref[3, 0]
+    second = sums_ref[0, 1] + sums_ref[1, 1] + sums_ref[2, 1] + sums_ref[3, 1]
+    count = 4.0 * CH
+    mean = first / count
+    inv_std = lax.rsqrt(second / count - mean * mean + norm_eps)
+    stat_ref[0], stat_ref[1] = mean, inv_std
+    for tile in range(8):
+        lanes = slice(tile * 128, tile * 128 + 128)
+        value = x_ref[:, :, lanes].astype(f32)
+        value = (value - mean[:, lanes][None]) * inv_std[:, lanes][None]
+        rows_ref[tile] = value.reshape(LANES, 128)
+    fill_halves(rows_ref, halves_ref)
+    gain, shift = row_lanes(gain_ref[...]), row_lanes(shift_ref[...])
+    peers = PEERS // CHUNKS
+    copies = []
+    for chunk in range(CHUNKS):
+        parity, place = divmod(chunk, CHUNKS // 2)
+        rows = slice(place * 256, place * 256 + 256)
+        table = (tab_ref[parity, 0, rows], tab_ref[parity, 1, rows])
+        value = dot3(table, (halves_ref[parity, 0], halves_ref[parity, 1]), NT)
+        own = pl.ds(chunk * peers, peers)
         for tile in range(TILES):
-            out_ref[0, tile, 0:1, :] = out_ref[0, tile, 0:1, :] + shift_ref[tile] * 32.0
-
-
-def lon_forward_call(kernel, name, small_specs):
+            piece = value[:, tile * 128 : tile * 128 + 128] * gain[tile]
+            wire_ref[own, tile] = piece.reshape(peers, 32, 128)
+        if chunk == 0:
+            for tile in range(TILES):
+                wire_ref[0, tile, 0:1, :] = wire_ref[0, tile, 0:1, :] + shift[tile] * 32.0
+        copy = pltpu.make_async_copy(wire_ref.at[own], out_ref.at[own], sems.at[chunk])
+        copy.start()
+        copies.append(copy)
+    for copy in copies:
+        copy.wait()
+
+
+def lon_grad(cotangent, table):
     return pl.pallas_call(
-        kernel,
-        name=name,
+        lon_grad_kernel,
+        name="lon_grad",
         grid=(2,),
-        in_specs=[pl.BlockSpec((CH, RW, LON), lambda i: (0, 0, 0))]
-        + small_specs
-        + [pl.BlockSpec((1, 2, HALF, HALF), lambda i: (i, 0, 0, 0))],
+        in_specs=[
+            pl.BlockSpec((CH, RW, LON), lambda i: (0, 0, 0)),
+            pl.BlockSpec((1, 2, HALF, HALF), lambda i: (i, 0, 0, 0)),
+        ],
         out_specs=pl.BlockSpec((16, TILES, 32, 128), lambda i: (i, 0, 0, 0)),
         out_shape=WIRE_SHAPE,
         scratch_shapes=[
             pltpu.VMEM((8, LANES, 128), f32),
             pltpu.VMEM((2, 2, LANES, HALF), bf16),
         ],
-        compiler_params=pltpu.CompilerParams(vmem_limit_bytes=40 * 2**20),
+        compiler_params=pltpu.CompilerParams(vmem_limit_bytes=56 * 2**20),
         cost_estimate=pl.CostEstimate(
             flops=6 * LANES * LON * LON, bytes_accessed=7 * 2**20, transcendentals=0
         ),
-    )
+    )(cotangent, table)
+
+
+def lon_field(tokens, sums, gain, shift, table):
+    vmem = pl.BlockSpec(memory_space=pltpu.VMEM)
+    return pl.pallas_call(
+        lon_field_kernel,
+        name="lon_field",
+        in_specs=[vmem] * 5,
+        out_specs=[pl.BlockSpec(memory_space=pltpu.HBM), vmem],
+        out_shape=[WIRE_SHAPE, jax.ShapeDtypeStruct((2, RW, LON), f32)],
+        scratch_shapes=[
+            pltpu.VMEM((8, LANES, 128), f32),
+            pltpu.VMEM((2, 2, LANES, HALF), bf16),
+            pltpu.VMEM((PEERS, TILES, 32, 128), f32),
+            pltpu.SemaphoreType.DMA((CHUNKS,)),
+        ],
+        compiler_params=pltpu.CompilerParams(vmem_limit_bytes=24 * 2**20),
+        cost_estimate=pl.CostEstimate(
+            flops=6 * LANES * LON * LON, bytes_accessed=7 * 2**20, transcendentals=0
+        ),
+    )(tokens, sums, gain, shift, table)
 
 
 def unpack_rows(block_ref, halves_ref):
@@ -187,7 +242,7 @@
                     halves_ref[(parity, 1) + at] = low
 
 
-def pack_rows(even, odd, block_ref):
+def pack_rows(even, odd, block_ref, peer_rows, tile_rows, first_row):
     lane = lax.broadcasted_iota(jnp.int32, (16, 128), 1)
     for q in range(QB):
         for part in range(2):
@@ -206,8 +261,8 @@
                             out = piece
                         else:
                             out = jnp.where(lane < low, out, piece)
-                    start = (side * 16 * TILES + tile) * 8 + 2 * q + part
-                    block_ref[pl.ds(start, 16, stride=TILES * 8), :] = out
+                    start = side * 16 * peer_rows + tile * tile_rows + 2 * q + part + first_row
+                    block_ref[pl.ds(start, 16, stride=peer_rows), :] = out
 
 
 def by_frequency(even, odd):
@@ -247,9 +302,13 @@
     return by_frequency(out[0], out[1])
 
 
-def lat_inverse(rows, tab_ref, block_ref):
-    even, odd = by_part(rows)
-    pack_rows(dot(tab_ref[0, 0], even, TN), dot(tab_ref[1, 0], odd, TN), block_ref)
+def lat_inverse(rows, tab_ref, block_ref, peer_rows=TILES * 8, tile_rows=8, first_row=0):
+    high, low = by_part(rows[0]), by_part(rows[1])
+    even, odd = [
+        dot3((tab_ref[parity, 0], tab_ref[parity, 1]), (high[parity], low[parity]), TN)
+        for parity in range(2)
+    ]
+    pack_rows(even, odd, block_ref, peer_rows, tile_rows, first_row)
 
 
 def fill_weight(w_ref, out_ref):
@@ -274,7 +333,7 @@
 
 def field_modes_kernel(
     block_ref, tab_ref, w_in_ref, b_in_ref, w_out_ref, b_out_ref,
-    back_ref, spec_ref, act_ref, mask_ref,
+    back_ref, spec_ref, spec_low_ref, act_ref, act_low_ref, mask_ref,
     halves_ref, full_ref, weight_ref, bias_ref,
 ):
     @pl.when(pl.program_id(0) == 0)
@@ -285,19 +344,19 @@
             fill_bias(b_ref, bias_ref.at[at])
 
     spec = split(lat_forward(block_ref.reshape(PEERS * TILES * 8, 128), tab_ref, halves_ref))
-    spec_ref[...] = spec[0]
+    spec_ref[...], spec_low_ref[...] = spec
     act = dot3(spec, (weight_ref[0, 0], weight_ref[0, 1])) + bias_ref[0, 0:1, :]
     act = split(jnp.maximum(act, 0.0))
-    act_ref[...] = act[0]
+    act_ref[...], act_low_ref[...] = act
     post = dot3(act, (weight_ref[1, 0], weight_ref[1, 1])) + bias_ref[1, 0:1, :]
     mask_ref[...] = jnp.where(jnp.abs(post) > shrink_level, 1.0, 0.0).astype(bf16)
     shrunk = post - jnp.clip(post, -shrink_level, shrink_level)
-    lat_inverse(shrunk.astype(bf16), tab_ref, back_ref.reshape(PEERS * TILES * 8, 128))
+    lat_inverse(split(shrunk), tab_ref, back_ref.reshape(PEERS * TILES * 8, 128))
 
 
 def pull_modes_kernel(
-    grad_ref, spec_ref, act_ref, mask_ref, tab_ref, w_in_ref, w_out_ref,
-    back_ref, g_ref,
+    grad_ref, spec_ref, spec_low_ref, act_ref, act_low_ref, mask_ref, tab_ref, w_in_ref, w_out_ref,
+    back_ref,
     full_ref, weight_ref, sum_ref,
 ):
     step = pl.program_id(0)
@@ -306,29 +365,34 @@
     def _():
         for at, w_ref in enumerate((w_in_ref, w_out_ref)):
             fill_weight(w_ref, full_ref)
-            weight_ref[at] = full_ref[...].astype(bf16)
+            weight_ref[at, 0], weight_ref[at, 1] = split(full_ref[...])
         sum_ref[...] = jnp.zeros_like(sum_ref)
-
-    spec, act = spec_ref[...], act_ref[...]
-    d_post = jnp.where(mask_ref[...] > 0.5, grad_ref[...].astype(bf16), jnp.zeros((), bf16))
-    sum_ref[1] += dot(act, d_post, TN)
-    d_act = dot(d_post, weight_ref[1], NT)
-    d_pre = jnp.where(act > 0, d_act.astype(bf16), jnp.zeros((), bf16))
-    sum_ref[0] += dot(spec, d_pre, TN)
-    d_spec = dot(d_pre, weight_ref[0], NT)
-    lat_inverse(d_spec.astype(bf16), tab_ref, back_ref.reshape(PEERS * TILES * 8, 128))
+        back_ref[:, PULL_ROWS - 16 :, :] = jnp.zeros((PEERS, 16, 128), f32)
+
+    spec, act = (spec_ref[...], spec_low_ref[...]), (act_ref[...], act_low_ref[...])
+    d_post = split(jnp.where(mask_ref[...].astype(f32) > 0.5, grad_ref[...], 0.0))
+    sum_ref[1] += dot3(act, d_post, TN)
+    d_act = dot3(d_post, (weight_ref[1, 0], weight_ref[1, 1]), NT)
+    d_pre = split(jnp.where(act[0].astype(f32) > 0.0, d_act, 0.0))
+    sum_ref[0] += dot3(spec, d_pre, TN)
+    d_spec = dot3(d_pre, (weight_ref[0, 0], weight_ref[0, 1]), NT)
+    flat_ref = back_ref.reshape(PEERS * PULL_ROWS, 128)
+    lat_inverse(split(d_spec), tab_ref, flat_ref, PULL_ROWS, 32, step * 8)
 
     @pl.when(step == STEPS - 1)
     def _():
         scale = 1.0 / math.sqrt(131072.0)
         for at in range(2):
-            total = sum_ref[at]
+            total = sum_ref[at] * scale
             rr, ri = total[0:CH, 0:CH], total[0:CH, 128 : 128 + CH]
             ir, ii = total[128 : 128 + CH, 0:CH], total[128 : 128 + CH, 128 : 128 + CH]
-            g_ref[2 * at] = (rr + ii) * scale
-            g_ref[2 * at + 1] = (ri - ir) * scale
-
-
+            for part, value in enumerate((rr + ii, ri - ir)):
+                for k in range(8):
+                    peer = (2 * at + part) * 8 + k
+                    back_ref[peer, PULL_ROWS - 16 : PULL_ROWS - 4, 0:CH] = value[12 * k : 12 * k + 12]
+
+
+PULL_ROWS = TILES * 32 + 16
 WIRE = pl.BlockSpec((PEERS, TILES, 8, 128), lambda i: (0, 0, i, 0))
 LAT_TAB = pl.BlockSpec((2, 2, 256, 256), lambda i: (0, 0, 0, 0))
 MODES = pl.BlockSpec((1024, 256), lambda i: (i, 0))
@@ -349,7 +413,7 @@
         out_specs=MODES,
         out_shape=modes_shape(f32),
         scratch_shapes=[pltpu.VMEM((2, 2, 256, QB * 128), bf16)],
-        compiler_params=pltpu.CompilerParams(vmem_limit_bytes=40 * 2**20),
+        compiler_params=pltpu.CompilerParams(vmem_limit_bytes=56 * 2**20),
         cost_estimate=pl.CostEstimate(
             flops=6 * 2**31, bytes_accessed=8 * 2**20, transcendentals=0
         ),
@@ -362,47 +426,47 @@
         name="field_modes",
         grid=(STEPS,),
         in_specs=[WIRE, LAT_TAB, WEIGHT, BIAS, WEIGHT, BIAS],
-        out_specs=[WIRE, MODES, MODES, MODES],
-        out_shape=[WIRE_SHAPE, modes_shape(bf16), modes_shape(bf16), modes_shape(bf16)],
+        out_specs=[WIRE] + [MODES] * 5,
+        out_shape=[WIRE_SHAPE] + [modes_shape(bf16)] * 5,
         scratch_shapes=[
             pltpu.VMEM((2, 2, 256, QB * 128), bf16),
             pltpu.VMEM((256, 256), f32),
             pltpu.VMEM((2, 2, 256, 256), bf16),
             pltpu.VMEM((2, 8, 256), f32),
         ],
-        compiler_params=pltpu.CompilerParams(vmem_limit_bytes=48 * 2**20),
+        compiler_params=pltpu.CompilerParams(vmem_limit_bytes=56 * 2**20),
         cost_estimate=pl.CostEstimate(
             flops=12 * 2**31, bytes_accessed=14 * 2**20, transcendentals=0
         ),
     )(block, table, w_in, b_in, w_out, b_out)
 
 
-def pull_modes(grad, spec, act, mask, table, w_in, w_out):
+def pull_modes(grad, saved, table, w_in, w_out):
     return pl.pallas_call(
         pull_modes_kernel,
         name="pull_modes",
         grid=(STEPS,),
-        in_specs=[MODES, MODES, MODES, MODES, LAT_TAB, WEIGHT, WEIGHT],
-        out_specs=[WIRE, pl.BlockSpec((4, CH, CH), lambda i: (0, 0, 0))],
-        out_shape=[WIRE_SHAPE, jax.ShapeDtypeStruct((4, CH, CH), f32)],
+        in_specs=[MODES] * 6 + [LAT_TAB, WEIGHT, WEIGHT],
+        out_specs=pl.BlockSpec((PEERS, PULL_ROWS, 128), lambda i: (0, 0, 0)),
+        out_shape=jax.ShapeDtypeStruct((PEERS, PULL_ROWS, 128), f32),
         scratch_shapes=[
             pltpu.VMEM((256, 256), f32),
-            pltpu.VMEM((2, 256, 256), bf16),
+            pltpu.VMEM((2, 2, 256, 256), bf16),
             pltpu.VMEM((2, 256, 256), f32),
         ],
-        compiler_params=pltpu.CompilerParams(vmem_limit_bytes=48 * 2**20),
+        compiler_params=pltpu.CompilerParams(vmem_limit_bytes=56 * 2**20),
         cost_estimate=pl.CostEstimate(
             flops=8 * 2**31, bytes_accessed=14 * 2**20, transcendentals=0
         ),
-    )(grad, spec, act, mask, table, w_in, w_out)
-
-
-def lon_inverse(block_ref, tab_ref, rows_ref, weighted):
+    )(grad, *saved, table, w_in, w_out)
+
+
+def lon_inverse(take, tab_ref, rows_ref, weighted):
     sides = []
     for parity in range(2):
         value = jnp.concatenate(
             [
-                block_ref[pl.ds(parity * 16, 16), tile].reshape(HALF, 128)
+                take(slice(parity * 16, parity * 16 + 16), tile).reshape(HALF, 128)
                 for tile in range(TILES)
             ],
             axis=1,
@@ -412,7 +476,7 @@
             if parity == 0:
                 row = lax.broadcasted_iota(jnp.int32, (HALF, 1), 0)
                 value = value * jnp.where(row == 0, 0.5, 1.0)
-        sides.append(dot(value.astype(bf16), tab_ref[parity, 0], TN))
+        sides.append(dot(value.astype(bf16), tab_ref[parity], TN))
     first, second = sides[0] + sides[1], sides[0] - sides[1]
     for r in range(RW):
         at, rows = pl.ds(r, CH, stride=RW), slice(r * CH, (r + 1) * CH)
@@ -423,7 +487,7 @@
 
 
 def mixed_kernel(block_ref, tab_ref, tok_ref, stat_ref, gain_ref, shift_ref, out_ref, rows_ref):
-    lon_inverse(block_ref, tab_ref, rows_ref, True)
+    lon_inverse(lambda peers, tile: block_ref[peers, tile], tab_ref, rows_ref, True)
     for tile in range(8):
         lanes = slice(tile * 128, tile * 128 + 128)
         tok = tok_ref[:, :, lanes].astype(f32)
@@ -433,17 +497,59 @@
         out_ref[:, :, lanes] = (filtered + normal + tok).astype(bf16)
 
 
-def pulled_kernel(block_ref, tab_ref, tok_ref, cot_ref, stat_ref, gain_ref, out_ref, sum_ref, rows_ref):
-    lon_inverse(block_ref, tab_ref, rows_ref, False)
+def pulled_kernel(
+    block_ref, tab_ref, tok_ref, cot_ref, stat_ref, gain_ref,
+    out_ref, sum_ref, weight_ref,
+    rows_ref,
+):
+    def take(peers, tile):
+        return block_ref[peers, tile * 32 : tile * 32 + 32, :]
+
+    lon_inverse(take, tab_ref, rows_ref, False)
     for tile in range(8):
         lanes = slice(tile * 128, tile * 128 + 128)
         tok = tok_ref[:, :, lanes].astype(f32)
-        normed = (tok - stat_ref[0, :, lanes][None]) * stat_ref[1, :, lanes][None]
+        inv_std = stat_ref[1, :, lanes]
+        normed = (tok - stat_ref[0, :, lanes][None]) * inv_std[None]
         pulled = rows_ref[tile].reshape(CH, RW, 128)
-        dnorm = (pulled + cot_ref[:, :, lanes].astype(f32)) * gain_ref[...]
-        out_ref[:, :, lanes] = dnorm
+        cot = cot_ref[:, :, lanes].astype(f32)
+        dnorm = (pulled + cot) * gain_ref[...]
+        out_ref[:, :, lanes] = cot + inv_std[None] * dnorm
         sum_ref[0, :, lanes] = jnp.sum(dnorm, axis=0)
         sum_ref[1, :, lanes] = jnp.sum(dnorm * normed, axis=0)
+    share = jnp.sum(block_ref[:, PULL_ROWS - 16 :, :], axis=0)
+    for i in range(12):
+        weight_ref[0:1, i * CH : i * CH + CH] = share[i : i + 1, 0:CH]
+
+
+def finish_kernel(part_ref, tok_ref, sums_ref, stat_ref, out_ref):
+    count = 4.0 * CH
+    mean, inv_std = stat_ref[0], stat_ref[1]
+    one = (sums_ref[0, 0] + sums_ref[1, 0] + sums_ref[2, 0] + sums_ref[3, 0]) / count
+    two = (sums_ref[0, 1] + sums_ref[1, 1] + sums_ref[2, 1] + sums_ref[3, 1]) / count
+    normed = (tok_ref[...].astype(f32) - mean[None]) * inv_std[None]
+    out_ref[...] = (part_ref[...] - (inv_std * one)[None] - normed * (inv_std * two)[None]).astype(bf16)
+
+
+def finish(part, tokens, sums, stats):
+    block = pl.BlockSpec((CH // 4, RW, LON), lambda i: (i, 0, 0))
+    return pl.pallas_call(
+        finish_kernel,
+        name="finish",
+        grid=(4,),
+        in_specs=[
+            block,
+            block,
+            pl.BlockSpec((4, 2, RW, LON), lambda i: (0, 0, 0, 0)),
+            pl.BlockSpec((2, RW, LON), lambda i: (0, 0, 0)),
+        ],
+        out_specs=block,
+        out_shape=jax.ShapeDtypeStruct((CH, RW, LON), bf16),
+        compiler_params=pltpu.CompilerParams(vmem_limit_bytes=24 * 2**20),
+        cost_estimate=pl.CostEstimate(
+            flops=8 * CH * RW * LON, bytes_accessed=6 * 2**20, transcendentals=0
+        ),
+    )(part, tokens, sums, stats)
 
 
 def whole_call(kernel, name, out_shape):
@@ -452,7 +558,7 @@
         name=name,
         out_shape=out_shape,
         scratch_shapes=[pltpu.VMEM((8, LANES, 128), f32)],
-        compiler_params=pltpu.CompilerParams(vmem_limit_bytes=48 * 2**20),
+        compiler_params=pltpu.CompilerParams(vmem_limit_bytes=28 * 2**20),
         cost_estimate=pl.CostEstimate(
             flops=4 * LANES * LON * LON, bytes_accessed=10 * 2**20, transcendentals=0
         ),
@@ -463,52 +569,46 @@
     return lax.all_to_all(value, "lat", split_axis=0, concat_axis=0, tiled=True)
 
 
-def sum_groups(value):
-    return jnp.sum(lax.all_gather(value, "grp"), axis=0)
+def after(value, first):
+    mark = lax.slice(first, (0,) * first.ndim, (1,) * first.ndim)
+    return lax.optimization_barrier((value, mark))[0]
 
 
 def per_device(tokens, cotangent, gain, shift, w_in, b_in, w_out, b_out):
-    all_chans = CH * lax.axis_size("grp")
-    lon_tab, lat_tab = jnp.asarray(lon_table()), jnp.asarray(lat_table())
+    lon_host = lon_table()
+    lon_tab, lon_high = jnp.asarray(lon_host), jnp.asarray(lon_host[:, 0])
+    lat_tab = jnp.asarray(lat_table())
     tok_val = tokens.astype(f32)
-    sums = sum_groups(jnp.stack([jnp.sum(tok_val, axis=0), jnp.sum(tok_val * tok_val, axis=0)]))
-    token_mean = sums[0] / all_chans
-    inv_std = lax.rsqrt(sums[1] / all_chans - token_mean * token_mean + norm_eps)
-    stats = jnp.stack([token_mean, inv_std])
-    gain_col = gain.reshape(CH, 1)
+    sums = jnp.stack([jnp.sum(tok_val, axis=0), jnp.sum(tok_val * tok_val, axis=0)])
+    sums = lax.all_gather(sums, "grp")
+    spec_field, stats = lon_field(
+        tokens, sums, gain.reshape(1, CH), shift.reshape(1, CH), lon_tab
+    )
     gain_cube = jnp.broadcast_to(gain.reshape(CH, 1, 1), (CH, 1, 128))
     shift_cube = jnp.broadcast_to(shift.reshape(CH, 1, 1), (CH, 1, 128))
 
-    spec_grad = lon_forward_call(lon_grad_kernel, "lon_grad", [])(cotangent, lon_tab)
-    modes_grad = exchange(spec_grad)
-    small = [
-        pl.BlockSpec((2, RW, LON), lambda i: (0, 0, 0)),
-        pl.BlockSpec((CH, 1), lambda i: (0, 0)),
-        pl.BlockSpec((TILES, 1, 128), lambda i: (0, 0, 0)),
-    ]
-    spec_field = lon_forward_call(lon_field_kernel, "lon_field", small)(
-        tokens, stats, gain_col, jnp.tile(shift, RW).reshape(TILES, 1, 128), lon_tab
+    modes_field = exchange(spec_field)
+    spec_grad = lon_grad(after(cotangent, stats), lon_tab)
+    modes_grad = exchange(after(spec_grad, modes_field))
+    back_field, *saved = field_modes(modes_field, lat_tab, w_in, b_in, w_out, b_out)
+    rows_field = exchange(after(back_field, modes_grad))
+    grad_rows = grad_modes(modes_grad, lat_tab)
+    back_grad = pull_modes(grad_rows, saved, lat_tab, w_in, w_out)
+    rows_grad = exchange(after(back_grad, rows_field))
+    mixed = whole_call(mixed_kernel, "mixed", jax.ShapeDtypeStruct((CH, RW, LON), bf16))(
+        rows_field, lon_high, tokens, stats, gain_cube, shift_cube
     )
-    modes_field = exchange(spec_field)
-    grad_rows = grad_modes(modes_grad, lat_tab)
-    back_field, spec, act, mask = field_modes(modes_field, lat_tab, w_in, b_in, w_out, b_out)
-    rows_field = exchange(back_field)
-    back_grad, grads = pull_modes(grad_rows, spec, act, mask, lat_tab, w_in, w_out)
-    rows_grad = exchange(back_grad)
-    mixed = whole_call(mixed_kernel, "mixed", jax.ShapeDtypeStruct((CH, RW, LON), bf16))(
-        rows_field, lon_tab, tokens, stats, gain_cube, shift_cube
-    )
-    dnorm, back = whole_call(
+    part, back, grad_weights = whole_call(
         pulled_kernel,
         "pulled",
-        [jax.ShapeDtypeStruct((CH, RW, LON), f32), jax.ShapeDtypeStruct((2, RW, LON), f32)],
-    )(rows_grad, lon_tab, tokens, cotangent, stats, gain_cube)
-    back = sum_groups(back) / all_chans
-    normed = (tok_val - token_mean) * inv_std
-    grad_tokens = cotangent.astype(f32) + inv_std * (dnorm - back[0] - normed * back[1])
-    shares = exchange(grads.reshape(PEERS, 1152))
-    grad_weights = jnp.sum(shares, axis=0).reshape(1, 1152)
-    return (mixed, grad_tokens.astype(bf16), grad_weights)
+        [
+            jax.ShapeDtypeStruct((CH, RW, LON), f32),
+            jax.ShapeDtypeStruct((2, RW, LON), f32),
+            jax.ShapeDtypeStruct((1, 1152), f32),
+        ],
+    )(rows_grad, lon_high, tokens, cotangent, stats, gain_cube)
+    grad_tokens = finish(part, tokens, lax.all_gather(back, "grp"), stats)
+    return (mixed, grad_tokens, grad_weights)
 
 
 def solution(mesh):

time: 264 us -> 238 us (0.902)
  blocking collectives: 133 us -> 19.7 us
  waiting for transfers between devices: 34.1 us -> 110 us
  Pallas kernels: 47.7 us -> 64.1 us
  starting transfers between devices: 25.1 us -> 33.8 us
  local copies, waits for them, and re-layouts: 14.5 us -> 7.09 us
  other arithmetic: 6.76 us -> 1.86 us
    all_to_all x3 -> x4, waiting for transfers between devices: 34.1 us -> 110 us  [exchange(): return lax.all_to_all(value, 'lat', split_axis=0, concat_axis=0, tiled=True)]
    all_to_all x2 -> x0, blocking collectives: 56.5 us -> none  [exchange(): return lax.all_to_all(value, 'lat', split_axis=0, concat_axis=0, tiled=True)]
    all_gather x2, blocking collectives: 76.2 us -> 19.7 us  [the longest x1 11.1 us: per_device(): grad_tokens = finish(part, tokens, lax.all_gather(back, 'grp'), stats)]
    all_to_all x3 -> x4, starting transfers between devices: 25.1 us -> 33.8 us  [exchange(): return lax.all_to_all(value, 'lat', split_axis=0, concat_axis=0, tiled=True)]
    pallas_call x1, Pallas kernels: 7.75 us -> 15.4 us  [pull_modes(): pl.pallas_call(pull_modes_kernel, name='pull_modes', grid=(STEPS,), in_sp...]
    unnamed x36 -> x22, local copies, waits for them, and re-layouts: 13.2 us -> 6.77 us
    pallas_call x2 -> x3, Pallas kernels: 8.93 us -> 14.6 us  [the longest x1 7.85 us: lon_grad(): pl.pallas_call(lon_grad_kernel, name='lon_grad', grid=(2,), in_specs=[pl....]
    convert_element_type x1 -> x0, other arithmetic: 4.07 us -> none  [per_device(): return (mixed, grad_tokens.astype(bf16), grad_weights)]
  transfers between devices with their start and end apart: 3 -> 4, of which waited for: 1 -> 4; matrix products, arithmetic and copies ran while one was open for 3% -> 0% of each run, Pallas kernels for 6% -> 22%
where the time goes in v2:
time: 238 us; the launch traced here: 237 us
  waiting for transfers between devices  110 us (46%)
  Pallas kernels  64.1 us (27%)
  starting transfers between devices  33.8 us (14%)
  blocking collectives  19.7 us (8%)
  local copies, waits for them, and re-layouts  7.09 us (3%)
    all_to_all x4, waiting for transfers between devices, exchange(): return lax.all_to_all(value, 'lat', split_axis=0, concat_axis=0, tiled=True)  110 us
    all_to_all x4, starting transfers between devices, exchange(): return lax.all_to_all(value, 'lat', split_axis=0, concat_axis=0, tiled=True)  33.8 us
    pallas_call x1, Pallas kernels, field_modes(): pl.pallas_call(field_modes_kernel, name='field_modes', grid=(STEPS,), in_...  16 us
    pallas_call x1, Pallas kernels, pull_modes(): pl.pallas_call(pull_modes_kernel, name='pull_modes', grid=(STEPS,), in_sp...  15.4 us
    all_gather x1, blocking collectives, per_device(): grad_tokens = finish(part, tokens, lax.all_gather(back, 'grp'), stats)  11.1 us
    all_gather x1, blocking collectives, per_device(): sums = lax.all_gather(sums, 'grp')  8.62 us
    pallas_call x1, Pallas kernels, lon_grad(): pl.pallas_call(lon_grad_kernel, name='lon_grad', grid=(2,), in_specs=[pl....  7.85 us
    pallas_call x1, Pallas kernels, grad_modes(): pl.pallas_call(grad_modes_kernel, name='grad_modes', grid=(STEPS,), in_sp...  6.79 us
  transfers between devices with their start and end apart: 4, of which 4 were waited for; matrix products, arithmetic and copies ran while one was open for 0% of the time, Pallas kernels for 22%

profile of v2, /device:TPU:1, one launch (start us, length us, event | category | flops | bytes accessed | tf_op | source)
XLA Modules:
  0.0 237.4 jit_solution(1687971267757426512)
XLA Ops:
  0.6 1.9 convert_reduce_fusion
  2.5 8.6 %all-gather = f32[8,8,1024]{2,1,0:T(8,128)S(1)} all-gather(f32[2,8,1024]{2,1,0:T(8,128)S(1)} %pad_maximum_fusion), channel_id=2, replica_groups=mesh['lat'=32,'grp'=4] {'grp'}, dimensions={0}, use_global_device_ids=true | all-gather | bytes 327680 | tf_op jit(solution)/shard_map/all_gather | solution.py:583
  11.1 1.4 copy-done
  12.5 0.7 copy-done.2
  13.2 0.7 copy-done.4
  13.8 1.6 copy-done.7
  15.4 4.8 %lon_field.1 = (f32[32,6,32,128]{3,2,1,0:T(8,128)}, f32[2,8,1024]{2,1,0:T(8,128)S(1)}) custom-call(bf16[96,8,1024]{2,1,0:T(8,128)(2,1)S(1)} %copy-done, f32[4,2,8,1024]{3,2,1,0:T(8,128)S(1)} %bitcast.7, f32[1,96]{1,0:T(1,128)S(1)} %bitcast.8, f32[1,96]{1,0:T(1,128)S(1)} %bitcast.9, bf16[2,2,512,512]{3,2,1,0:T(8,128)(2,1)S(1)} %copy-done.7), custom_call_target="tpu_custom_call" | custom-call | flops 4831838208 | bytes 7340032 | tf_op jit(solution)/shard_map/lon_field/pallas_call | solution.py:200
  20.2 9.0 %all-to-all-start = ((f32[32,6,32,128]{3,2,1,0:T(8,128)}), f32[32,6,32,128]{3,2,1,0:T(8,128)S(1)}, u32[]{:S(2)}, u32[]{:S(2)}) async-start(f32[32,6,32,128]{3,2,1,0:T(8,128)} %get-tuple-element.14), calls=%async_computation | async-start | bytes 6291456 | tf_op jit(solution)/shard_map/all_to_all | solution.py:569
  29.2 7.9 %lon_grad.1 = f32[32,6,32,128]{3,2,1,0:T(8,128)} custom-call(bf16[96,8,1024]{2,1,0:T(8,128)(2,1)} %cot_ref.1, bf16[2,2,512,512]{3,2,1,0:T(8,128)(2,1)} %constant.8.clone.tab_ref), custom_call_target="tpu_custom_call" | custom-call | flops 4831838208 | bytes 7340032 | tf_op jit(solution)/shard_map/lon_grad/pallas_call | solution.py:177
  37.1 33.8 %all-to-all-done.block_ref = f32[32,6,32,128]{3,2,1,0:T(8,128)S(1)} async-done(((f32[32,6,32,128]{3,2,1,0:T(8,128)}), f32[32,6,32,128]{3,2,1,0:T(8,128)S(1)}, u32[]{:S(2)}, u32[]{:S(2)}) %all-to-all-start) | async-done | bytes 3145760 | tf_op jit(solution)/shard_map/all_to_all | solution.py:569
  70.8 7.5 %all-to-all-start.2 = ((f32[32,6,32,128]{3,2,1,0:T(8,128)}), f32[32,6,32,128]{3,2,1,0:T(8,128)}, u32[]{:S(2)}, u32[]{:S(2)}) async-start(f32[32,6,32,128]{3,2,1,0:T(8,128)} %lon_grad.1), calls=%async_computation.2 | async-start | bytes 6291456 | tf_op jit(solution)/shard_map/all_to_all | solution.py:569
  78.3 0.0 copy-done.10
  78.3 16.0 %field_modes.1 = (f32[32,6,32,128]{3,2,1,0:T(8,128)}, bf16[4096,256]{1,0:T(8,128)(2,1)}, bf16[4096,256]{1,0:T(8,128)(2,1)}, bf16[4096,256]{1,0:T(8,128)(2,1)}, b...) custom-call(f32[32,6,32,128]{3,2,1,0:T(8,128)} %copy-done.10, bf16[2,2,256,256]{3,2,1,0:T(8,128)(2,1)} %constant.10.clone.tab_ref, ...), custom_call_target="tpu_custom_call" | custom-call | flops 25769803776 | bytes 14680064 | tf_op jit(solution)/shard_map/field_modes/pallas_call | solution.py:424
  94.3 24.1 %all-to-all-done.2.block_ref = f32[32,6,32,128]{3,2,1,0:T(8,128)} async-done(((f32[32,6,32,128]{3,2,1,0:T(8,128)}), f32[32,6,32,128]{3,2,1,0:T(8,128)}, u32[]{:S(2)}, u32[]{:S(2)}) %all-to-all-start.2) | async-done | bytes 3145760 | tf_op jit(solution)/shard_map/all_to_all | solution.py:569
  118.4 8.3 %all-to-all-start.1 = ((f32[32,6,32,128]{3,2,1,0:T(8,128)}), f32[32,6,32,128]{3,2,1,0:T(8,128)}, u32[]{:S(2)}, u32[]{:S(2)}) async-start(f32[32,6,32,128]{3,2,1,0:T(8,128)} %get-tuple-element.15), calls=%async_computation.1 | async-start | bytes 6291456 | tf_op jit(solution)/shard_map/all_to_all | solution.py:569
  126.7 6.8 %grad_modes.1.grad_ref = f32[4096,256]{1,0:T(8,128)} custom-call(f32[32,6,32,128]{3,2,1,0:T(8,128)} %all-to-all-done.2.block_ref, bf16[2,2,256,256]{3,2,1,0:T(8,128)(2,1)} %constant.10.clone.tab_ref), custom_call_target="tpu_custom_call" | custom-call | flops 12884901888 | bytes 8388608 | tf_op jit(solution)/shard_map/grad_modes/pallas_call | solution.py:408
  133.5 15.4 %pull_modes.1 = f32[32,208,128]{2,1,0:T(8,128)} custom-call(f32[4096,256]{1,0:T(8,128)} %grad_modes.1.grad_ref, bf16[4096,256]{1,0:T(8,128)(2,1)} %get-tuple-element.17.spec_ref, bf16[4096,256]{1,0:T(8,128)(2,1)} %get-tuple-element.18.spec_low_ref, bf16[4096,256]{1,0:T(8,128)(2,1)} %get-tuple-element.19.act_ref, ...), custom_call_target="tpu_custom_call" | custom-call | flops 17179869184 | bytes 14680064 | tf_op jit(solution)/shard_map/pull_modes/pallas_call | solution.py:445
  148.9 0.0 copy-start.1
  148.9 17.2 %all-to-all-done.1.block_ref = f32[32,6,32,128]{3,2,1,0:T(8,128)} async-done(((f32[32,6,32,128]{3,2,1,0:T(8,128)}), f32[32,6,32,128]{3,2,1,0:T(8,128)}, u32[]{:S(2)}, u32[]{:S(2)}) %all-to-all-start.1) | async-done | bytes 3145760 | tf_op jit(solution)/shard_map/all_to_all | solution.py:569
  166.2 9.0 %all-to-all-start.3 = ((f32[32,208,128]{2,1,0:T(8,128)}), f32[32,208,128]{2,1,0:T(8,128)}, u32[]{:S(2)}, u32[]{:S(2)}) async-start(f32[32,208,128]{2,1,0:T(8,128)} %pull_modes.1), calls=%async_computation.3 | async-start | bytes 6815744 | tf_op jit(solution)/shard_map/all_to_all | solution.py:569
  175.2 0.0 copy-done.3
  175.2 0.2 broadcast_in_dim.4.gain_ref
  175.4 0.2 broadcast_in_dim.5.shift_ref
  175.6 0.0 copy-start.8
  175.6 1.2 copy-done.8
  176.8 5.7 %mixed.1 = bf16[96,8,1024]{2,1,0:T(8,128)(2,1)} custom-call(f32[32,6,32,128]{3,2,1,0:T(8,128)} %all-to-all-done.1.block_ref, bf16[2,512,512]{2,1,0:T(8,128)(2,1)S(1)} %copy-done.8, bf16[96,8,1024]{2,1,0:T(8,128)(2,1)S(1)} %copy-done.1, f32[2,8,1024]{2,1,0:T(8,128)S(1)} %get-tuple-element.16.stat_ref, f32[96,1,128]{2,1,0:T(1,128)S(1)} %broadcast_in_dim.4.gain_ref, ...), custom_call_target="tpu_custom_call" | custom-call | flops 3221225472 | bytes 10485760 | tf_op jit(solution)/shard_map/mixed/pallas_call | solution.py:598
  182.5 35.0 %all-to-all-done.3.block_ref = f32[32,208,128]{2,1,0:T(8,128)} async-done(((f32[32,208,128]{2,1,0:T(8,128)}), f32[32,208,128]{2,1,0:T(8,128)}, u32[]{:S(2)}, u32[]{:S(2)}) %all-to-all-start.3) | async-done | bytes 3407904 | tf_op jit(solution)/shard_map/all_to_all | solution.py:569
  217.5 0.0 copy-done.6
  217.5 1.2 copy-done.9
  218.7 5.6 %pulled.1 = (f32[96,8,1024]{2,1,0:T(8,128)S(1)}, f32[2,8,1024]{2,1,0:T(8,128)S(1)}, f32[1,1152]{1,0:T(1,128)}) custom-call(f32[32,208,128]{2,1,0:T(8,128)} %all-to-all-done.3.block_ref, bf16[2,512,512]{2,1,0:T(8,128)(2,1)S(1)} %copy-done.9, bf16[96,8,1024]{2,1,0:T(8,128)(2,1)S(1)} %copy-done.1, bf16[96,8,1024]{2,1,0:T(8,128)(2,1)S(1)} %copy-done.6, ...), custom_call_target="tpu_custom_call" | custom-call | flops 3221225472 | bytes 10485760 | tf_op jit(solution)/shard_map/pulled/pallas_call | solution.py:601
  224.3 11.1 %all-gather.1 = f32[8,8,1024]{2,1,0:T(8,128)S(1)} all-gather(f32[2,8,1024]{2,1,0:T(8,128)S(1)} %get-tuple-element.23), channel_id=3, replica_groups=mesh['lat'=32,'grp'=4] {'grp'}, dimensions={0}, use_global_device_ids=true | all-gather | bytes 327680 | tf_op jit(solution)/shard_map/all_gather | solution.py:610
  235.4 2.0 finish.1
  (12 shorter events, 0.0 us)
Async XLA Ops:
  11.1 1.4 copy-start
  12.5 0.7 copy-start.2
  13.2 0.7 copy-start.4
  13.8 1.6 copy-start.7
  20.2 50.6 %all-to-all-start = ((f32[32,6,32,128]{3,2,1,0:T(8,128)}), f32[32,6,32,128]{3,2,1,0:T(8,128)S(1)}, u32[]{:S(2)}, u32[]{:S(2)}) async-start(f32[32,6,32,128]{3,2,1,0:T(8,128)} %get-tuple-element.14), calls=%async_computation | async-start | bytes 6291456 | tf_op jit(solution)/shard_map/all_to_all | solution.py:569
  70.8 7.5 %copy-start.10 = (f32[32,6,32,128]{3,2,1,0:T(8,128)}, f32[32,6,32,128]{3,2,1,0:T(8,128)S(1)}, u32[]{:S(2)}) copy-start(f32[32,6,32,128]{3,2,1,0:T(8,128)S(1)} %all-to-all-done.block_ref) | copy-start | bytes 9437188
  70.8 47.6 %all-to-all-start.2 = ((f32[32,6,32,128]{3,2,1,0:T(8,128)}), f32[32,6,32,128]{3,2,1,0:T(8,128)}, u32[]{:S(2)}, u32[]{:S(2)}) async-start(f32[32,6,32,128]{3,2,1,0:T(8,128)} %lon_grad.1), calls=%async_computation.2 | async-start | bytes 6291456 | tf_op jit(solution)/shard_map/all_to_all | solution.py:569
  118.4 47.8 %all-to-all-start.1 = ((f32[32,6,32,128]{3,2,1,0:T(8,128)}), f32[32,6,32,128]{3,2,1,0:T(8,128)}, u32[]{:S(2)}, u32[]{:S(2)}) async-start(f32[32,6,32,128]{3,2,1,0:T(8,128)} %get-tuple-element.15), calls=%async_computation.1 | async-start | bytes 6291456 | tf_op jit(solution)/shard_map/all_to_all | solution.py:569
  148.9 26.3 %copy-start.3 = (f32[96]{0:T(128)S(1)}, f32[96]{0:T(128)}, u32[]{:S(2)}) copy-start(f32[96]{0:T(128)} %param.13) | copy-start | bytes 1156
  148.9 26.5 %copy-start.5 = (f32[96]{0:T(128)S(1)}, f32[96]{0:T(128)}, u32[]{:S(2)}) copy-start(f32[96]{0:T(128)} %param.14) | copy-start | bytes 1156
  148.9 26.7 %copy-start.1 = (bf16[96,8,1024]{2,1,0:T(8,128)(2,1)S(1)}, bf16[96,8,1024]{2,1,0:T(8,128)(2,1)}, u32[]{:S(2)}) copy-start(bf16[96,8,1024]{2,1,0:T(8,128)(2,1)} %tok_ref.5) | copy-start | bytes 4718596
  166.2 51.3 %all-to-all-start.3 = ((f32[32,208,128]{2,1,0:T(8,128)}), f32[32,208,128]{2,1,0:T(8,128)}, u32[]{:S(2)}, u32[]{:S(2)}) async-start(f32[32,208,128]{2,1,0:T(8,128)} %pull_modes.1), calls=%async_computation.3 | async-start | bytes 6815744 | tf_op jit(solution)/shard_map/all_to_all | solution.py:569
  175.6 1.2 copy-start.8
  176.8 40.7 %copy-start.6 = (bf16[96,8,1024]{2,1,0:T(8,128)(2,1)S(1)}, bf16[96,8,1024]{2,1,0:T(8,128)(2,1)}, u32[]{:S(2)}) copy-start(bf16[96,8,1024]{2,1,0:T(8,128)(2,1)} %cot_ref.1) | copy-start | bytes 4718596
  217.5 1.2 copy-start.9

commit v3 on v2

v3 whole, which is shorter than its diff:
```python
import functools
import math

import jax
import jax.numpy as jnp
import ml_dtypes
import numpy as np
from jax import lax
from jax.experimental import pallas as pl
from jax.experimental.pallas import tpu as pltpu
from jax.sharding import PartitionSpec as P

shrink_level = 0.01
norm_eps = 1e-05
f32 = jnp.float32
bf16 = jnp.bfloat16

CH = 96
RW = 8
LON = 1024
HALF = 512
PEERS = 32
LANES = RW * CH
QB = 4
KB = 128
STEPS = 4
TILES = LANES // 128
WIRE_SHAPE = jax.ShapeDtypeStruct((PEERS, TILES, 32, 128), jnp.float32)


def host_split(table):
    high = table.astype(ml_dtypes.bfloat16)
    low = (table - high.astype(np.float64)).astype(ml_dtypes.bfloat16)
    return np.stack([high, low])


def lon_table():
    parts = []
    n = np.arange(HALF)
    for parity in range(2):
        m = 2 * np.arange(256) + parity
        theta = 2.0 * np.pi * ((m[:, None] * n[None, :]) % LON) / LON
        table = np.stack([np.cos(theta), -np.sin(theta)], axis=1).reshape(HALF, HALF)
        parts.append(host_split(table / 32.0))
    return np.stack(parts)


def lat_table():
    parts = []
    row = np.arange(RW)[:, None]
    peer = np.arange(16)[None, :]
    place = (8 * peer + row).reshape(-1)
    for parity in range(2):
        k = 2 * np.arange(KB) + parity
        theta = 2.0 * np.pi * ((k[:, None] * place[None, :]) % 256) / 256
        c, s = np.cos(theta), np.sin(theta)
        table = np.concatenate(
            [np.concatenate([c, s], axis=1), np.concatenate([-s, c], axis=1)], axis=0
        )
        parts.append(host_split(table / 16.0))
    return np.stack(parts)


def spread_table():
    table = np.zeros((LANES, RW * 128), ml_dtypes.bfloat16)
    channel, row = np.divmod(np.arange(LANES), RW)
    table[np.arange(LANES), row * 128 + channel] = 1
    return table


def split(value):
    high = value.astype(bf16)
    low = (value - high.astype(f32)).astype(bf16)
    return high, low


def dot(left, right, dims=((1,), (0,))):
    return lax.dot_general(left, right, (dims, ((), ())), preferred_element_type=f32)


NT = ((1,), (1,))
TN = ((0,), (0,))


def dot3(left, right, dims=((1,), (0,))):
    return (
        dot(left[0], right[0], dims) + dot(left[0], right[1], dims) + dot(left[1], right[0], dims)
    )


CHUNKS = 4
GROUP = CH // CHUNKS


def bring(pairs, sems):
    copies = [pltpu.make_async_copy(src, dst, sems.at[i]) for i, (src, dst) in enumerate(pairs)]
    for copy in copies:
        copy.start()
    return copies


def lon_transform(prepare, finish_rows, x_ref, tab_hbm, out_hbm, scratch):
    tab_ref, halves_ref, wire_ref, tab_sems, sems = scratch
    tab_copies = bring([(tab_hbm.at[p], tab_ref.at[p]) for p in range(2)], tab_sems)
    for tile in range(4):
        pair = []
        for lanes in (slice(tile * 128, tile * 128 + 128), slice(HALF + tile * 128, HALF + tile * 128 + 128)):
            pair.append(prepare(x_ref[:, :, lanes].astype(f32), lanes).reshape(LANES, 128))
        for parity, value in enumerate((pair[0] + pair[1], pair[0] - pair[1])):
            high, low = split(value)
            halves_ref[parity, 0, :, tile * 128 : tile * 128 + 128] = high
            halves_ref[parity, 1, :, tile * 128 : tile * 128 + 128] = low
    peers = PEERS // 2
    copies = []
    for parity in range(2):
        tab_copies[parity].wait()
        both = dot(tab_ref[parity].reshape(2 * HALF, HALF), halves_ref[parity, 0], NT)
        value = both[:HALF] + both[HALF:] + dot(tab_ref[parity, 0], halves_ref[parity, 1], NT)
        own = pl.ds(parity * peers, peers)
        for tile in range(TILES):
            piece = finish_rows(value[:, tile * 128 : tile * 128 + 128], tile)
            wire_ref[own, tile] = piece.reshape(peers, 32, 128)
        if parity == 0:
            finish_rows(None, wire_ref)
        copy = pltpu.make_async_copy(wire_ref.at[own], out_hbm.at[own], sems.at[parity])
        copy.start()
        copies.append(copy)
    for copy in copies:
        copy.wait()


def lon_grad_kernel(x_ref, tab_hbm, sums_hbm, out_hbm, mark_ref, *scratch):
    mark_ref[...] = jnp.zeros((8, 128), f32)

    def finish_rows(value, at):
        if value is not None:
            return value
        at[0, :, 0:2, :] = at[0, :, 0:2, :] * 0.5

    lon_transform(lambda value, lanes: value * 2.0, finish_rows, x_ref, tab_hbm, out_hbm, scratch)


def total(terms, at):
    return terms[0][at] + terms[1][at] + terms[2][at] + terms[3][at]


def lon_field_kernel(
    x_ref, tab_hbm, gain_ref, shift_ref, one_ref, two_ref, three_ref, four_ref,
    mark_hbm,
    out_hbm, stat_ref,
    *scratch,
):
    terms = (one_ref, two_ref, three_ref, four_ref)
    count = 4.0 * CH
    mean = total(terms, 0) / count
    inv_std = lax.rsqrt(total(terms, 1) / count - mean * mean + norm_eps)
    stat_ref[0], stat_ref[1] = mean, inv_std

    def prepare(value, lanes):
        return (value - mean[:, lanes][None]) * inv_std[:, lanes][None]

    def finish_rows(value, at):
        if value is not None:
            return value * gain_ref[at]
        for tile in range(TILES):
            at[0, tile, 0:1, :] = at[0, tile, 0:1, :] + shift_ref[tile] * 32.0

    lon_transform(prepare, finish_rows, x_ref, tab_hbm, out_hbm, scratch)


VMEM = pl.BlockSpec(memory_space=pltpu.VMEM)
HBM = pl.BlockSpec(memory_space=pltpu.HBM)
STATS_SHAPE = jax.ShapeDtypeStruct((2, RW, LON), f32)


def lon_call(kernel, name, more, unread):
    return pl.pallas_call(
        kernel,
        name=name,
        in_specs=[VMEM, HBM] + [VMEM] * (more + unread),
        out_specs=[HBM, VMEM],
        out_shape=[WIRE_SHAPE, STATS_SHAPE]
        if more
        else [pltpu.HBM(WIRE_SHAPE.shape, f32), jax.ShapeDtypeStruct((8, 128), f32)],
        scratch_shapes=[
            pltpu.VMEM((2, 2, HALF, HALF), bf16),
            pltpu.VMEM((2, 2, LANES, HALF), bf16),
            pltpu.VMEM((PEERS, TILES, 32, 128), f32),
            pltpu.SemaphoreType.DMA((2,)),
            pltpu.SemaphoreType.DMA((2,)),
        ],
        compiler_params=pltpu.CompilerParams(vmem_limit_bytes=24 * 2**20),
        cost_estimate=pl.CostEstimate(
            flops=6 * LANES * LON * LON, bytes_accessed=7 * 2**20, transcendentals=0
        ),
    )


def unpack_rows(block_ref, spread_ref, rows_ref, halves_ref, terms):
    left = jnp.concatenate([block_ref[:, t].reshape(PEERS * 8, 128) for t in range(TILES)], axis=1)
    value = None
    for _ in range(terms):
        part = left.astype(bf16)
        left = left - part.astype(f32)
        moved = dot(part, spread_ref[...])
        value = moved if value is None else value + moved
    for r in range(RW):
        rows_ref[r, 0 : PEERS * 8] = value[:, r * 128 : r * 128 + 128]
    for q in range(QB):
        for part in range(2):
            for r in range(RW):
                first = rows_ref[r, pl.ds(2 * q + part, 16, stride=8), :]
                second = rows_ref[r, pl.ds(128 + 2 * q + part, 16, stride=8), :]
                for parity, value in enumerate((first + second, first - second)):
                    high, low = split(value)
                    at = (pl.ds((part * RW + r) * 16, 16), pl.ds(q * 128, 128))
                    halves_ref[(parity, 0) + at] = high
                    halves_ref[(parity, 1) + at] = low


def pack_rows(even, odd, spread_ref, rows_ref):
    for q in range(QB):
        lanes = slice(q * 128, q * 128 + 128)
        for part in range(2):
            for r in range(RW):
                at = slice((part * RW + r) * 16, (part * RW + r + 1) * 16)
                first, second = even[at, lanes], odd[at, lanes]
                rows_ref[r, pl.ds(2 * q + part, 16, stride=8), :] = first + second
                rows_ref[r, pl.ds(128 + 2 * q + part, 16, stride=8), :] = first - second
    high, low = split(jnp.concatenate([rows_ref[r, 0 : PEERS * 8] for r in range(RW)], axis=1))
    return dot(high, spread_ref[...], NT) + dot(low, spread_ref[...], NT)


def by_frequency(even, odd):
    rows = []
    for q in range(QB):
        for value in (even, odd):
            lanes = slice(q * 128, q * 128 + 128)
            rows.append(jnp.concatenate([value[0:KB, lanes], value[KB : 2 * KB, lanes]], axis=1))
    return jnp.concatenate(rows, axis=0)


def by_part(rows):
    out = []
    for parity in range(2):
        parts = []
        for part in range(2):
            lanes = slice(part * 128, part * 128 + 128)
            parts.append(
                jnp.concatenate(
                    [rows[(2 * q + parity) * KB : (2 * q + parity + 1) * KB, lanes] for q in range(QB)],
                    axis=1,
                )
            )
        out.append(jnp.concatenate(parts, axis=0))
    return out


def lat_forward(block_ref, tab_ref, spread_ref, rows_ref, halves_ref, terms):
    unpack_rows(block_ref, spread_ref, rows_ref, halves_ref, terms)
    out = [
        dot3(
            (tab_ref[parity, 0], tab_ref[parity, 1]),
            (halves_ref[parity, 0], halves_ref[parity, 1]),
        )
        for parity in range(2)
    ]
    return by_frequency(out[0], out[1])


def lat_inverse(rows, tab_ref, spread_ref, rows_ref):
    high, low = by_part(rows[0]), by_part(rows[1])
    even, odd = [
        dot3((tab_ref[parity, 0], tab_ref[parity, 1]), (high[parity], low[parity]), TN)
        for parity in range(2)
    ]
    wire = pack_rows(even, odd, spread_ref, rows_ref)
    return [wire[:, t * 128 : t * 128 + 128].reshape(PEERS, 8, 128) for t in range(TILES)]


def fill_weight(w_ref, out_ref):
    full = jnp.zeros((256, 256), f32)
    out_ref[...] = full
    real, imag = w_ref[0, 0], w_ref[0, 1]
    out_ref[0:CH, 0:CH] = real
    out_ref[0:CH, 128 : 128 + CH] = imag
    out_ref[128 : 128 + CH, 0:CH] = -imag
    out_ref[128 : 128 + CH, 128 : 128 + CH] = real


def fill_bias(b_ref, out_ref):
    out_ref[...] = jnp.zeros((8, 256), f32)
    out_ref[0:1, 0:CH] = b_ref[0, 0:1, :]
    out_ref[0:1, 128 : 128 + CH] = b_ref[0, 1:2, :]


def grad_modes_kernel(block_ref, tab_ref, spread_ref, out_ref, rows_ref, halves_ref):
    out_ref[...] = lat_forward(block_ref, tab_ref, spread_ref, rows_ref, halves_ref, 2)


def field_modes_kernel(
    block_ref, tab_ref, spread_ref, w_in_ref, b_in_ref, w_out_ref, b_out_ref,
    back_ref, spec_ref, spec_low_ref, act_ref, act_low_ref, mask_ref,
    rows_ref, halves_ref, full_ref, weight_ref, bias_ref,
):
    @pl.when(pl.program_id(0) == 0)
    def _():
        for at, (w_ref, b_ref) in enumerate(((w_in_ref, b_in_ref), (w_out_ref, b_out_ref))):
            fill_weight(w_ref, full_ref)
            weight_ref[at, 0], weight_ref[at, 1] = split(full_ref[...])
            fill_bias(b_ref, bias_ref.at[at])

    spec = split(lat_forward(block_ref, tab_ref, spread_ref, rows_ref, halves_ref, 3))
    spec_ref[...], spec_low_ref[...] = spec
    act = dot3(spec, (weight_ref[0, 0], weight_ref[0, 1])) + bias_ref[0, 0:1, :]
    act = split(jnp.maximum(act, 0.0))
    act_ref[...], act_low_ref[...] = act
    post = dot3(act, (weight_ref[1, 0], weight_ref[1, 1])) + bias_ref[1, 0:1, :]
    mask_ref[...] = jnp.where(jnp.abs(post) > shrink_level, 1.0, 0.0).astype(bf16)
    shrunk = post - jnp.clip(post, -shrink_level, shrink_level)
    for tile, piece in enumerate(lat_inverse(split(shrunk), tab_ref, spread_ref, rows_ref)):
        back_ref[:, tile] = piece


def pull_modes_kernel(
    grad_ref, spec_ref, spec_low_ref, act_ref, act_low_ref, mask_ref, tab_ref, spread_ref,
    w_in_ref, w_out_ref, cubes_hbm,
    back_ref,
    rows_ref, full_ref, weight_ref, sum_ref,
):
    step = pl.program_id(0)

    @pl.when(step == 0)
    def _():
        for at, w_ref in enumerate((w_in_ref, w_out_ref)):
            fill_weight(w_ref, full_ref)
            weight_ref[at, 0], weight_ref[at, 1] = split(full_ref[...])
        sum_ref[...] = jnp.zeros_like(sum_ref)
        back_ref[:, PULL_ROWS - 16 :, :] = jnp.zeros((PEERS, 16, 128), f32)

    spec, act = (spec_ref[...], spec_low_ref[...]), (act_ref[...], act_low_ref[...])
    d_post = split(jnp.where(mask_ref[...].astype(f32) > 0.5, grad_ref[...], 0.0))
    sum_ref[1] += dot3(act, d_post, TN)
    d_act = dot3(d_post, (weight_ref[1, 0], weight_ref[1, 1]), NT)
    d_pre = split(jnp.where(act[0].astype(f32) > 0.0, d_act, 0.0))
    sum_ref[0] += dot3(spec, d_pre, TN)
    d_spec = dot3(d_pre, (weight_ref[0, 0], weight_ref[0, 1]), NT)
    for tile, piece in enumerate(lat_inverse(split(d_spec), tab_ref, spread_ref, rows_ref)):
        back_ref[:, pl.ds(pl.multiple_of(tile * 32 + step * 8, 8), 8), :] = piece

    @pl.when(step == STEPS - 1)
    def _():
        scale = 1.0 / math.sqrt(131072.0)
        for at in range(2):
            total = sum_ref[at] * scale
            rr, ri = total[0:CH, 0:CH], total[0:CH, 128 : 128 + CH]
            ir, ii = total[128 : 128 + CH, 0:CH], total[128 : 128 + CH, 128 : 128 + CH]
            for part, value in enumerate((rr + ii, ri - ir)):
                for k in range(8):
                    peer = (2 * at + part) * 8 + k
                    back_ref[peer, PULL_ROWS - 16 : PULL_ROWS - 4, 0:CH] = value[12 * k : 12 * k + 12]


PULL_ROWS = TILES * 32 + 16
WIRE = pl.BlockSpec((PEERS, TILES, 8, 128), lambda i: (0, 0, i, 0))
LAT_TAB = pl.BlockSpec((2, 2, 256, 256), lambda i: (0, 0, 0, 0))
MODES = pl.BlockSpec((1024, 256), lambda i: (i, 0))
SPREAD = pl.BlockSpec((LANES, RW * 128), lambda i: (0, 0))
ROWS = pltpu.VMEM((RW, PEERS * 8 + 8, 128), f32)
WEIGHT = pl.BlockSpec((1, 2, CH, CH), lambda i: (0, 0, 0, 0))
BIAS = pl.BlockSpec((1, 2, CH), lambda i: (0, 0, 0))


def modes_shape(dtype):
    return jax.ShapeDtypeStruct((4096, 256), dtype)


def grad_modes(block, table, spread):
    return pl.pallas_call(
        grad_modes_kernel,
        name="grad_modes",
        grid=(STEPS,),
        in_specs=[WIRE, LAT_TAB, SPREAD],
        out_specs=MODES,
        out_shape=modes_shape(f32),
        scratch_shapes=[ROWS, pltpu.VMEM((2, 2, 256, QB * 128), bf16)],
        compiler_params=pltpu.CompilerParams(vmem_limit_bytes=36 * 2**20),
        cost_estimate=pl.CostEstimate(
            flops=6 * 2**31, bytes_accessed=8 * 2**20, transcendentals=0
        ),
    )(block, table, spread)


def field_modes(block, table, spread, w_in, b_in, w_out, b_out):
    return pl.pallas_call(
        field_modes_kernel,
        name="field_modes",
        grid=(STEPS,),
        in_specs=[WIRE, LAT_TAB, SPREAD, WEIGHT, BIAS, WEIGHT, BIAS],
        out_specs=[WIRE] + [MODES] * 5,
        out_shape=[WIRE_SHAPE] + [modes_shape(bf16)] * 5,
        scratch_shapes=[
            ROWS,
            pltpu.VMEM((2, 2, 256, QB * 128), bf16),
            pltpu.VMEM((256, 256), f32),
            pltpu.VMEM((2, 2, 256, 256), bf16),
            pltpu.VMEM((2, 8, 256), f32),
        ],
        compiler_params=pltpu.CompilerParams(vmem_limit_bytes=36 * 2**20),
        cost_estimate=pl.CostEstimate(
            flops=12 * 2**31, bytes_accessed=14 * 2**20, transcendentals=0
        ),
    )(block, table, spread, w_in, b_in, w_out, b_out)


def pull_modes(grad, saved, table, spread, w_in, w_out, cubes):
    return pl.pallas_call(
        pull_modes_kernel,
        name="pull_modes",
        grid=(STEPS,),
        in_specs=[MODES] * 6 + [LAT_TAB, SPREAD, WEIGHT, WEIGHT, HBM],
        out_specs=pl.BlockSpec((PEERS, PULL_ROWS, 128), lambda i: (0, 0, 0)),
        out_shape=jax.ShapeDtypeStruct((PEERS, PULL_ROWS, 128), f32),
        scratch_shapes=[
            ROWS,
            pltpu.VMEM((256, 256), f32),
            pltpu.VMEM((2, 2, 256, 256), bf16),
            pltpu.VMEM((2, 256, 256), f32),
        ],
        compiler_params=pltpu.CompilerParams(vmem_limit_bytes=36 * 2**20),
        cost_estimate=pl.CostEstimate(
            flops=8 * 2**31, bytes_accessed=14 * 2**20, transcendentals=0
        ),
    )(grad, *saved, table, spread, w_in, w_out, cubes)


def lon_inverse(take, tab_ref, weighted):
    sides = []
    for parity in range(2):
        value = jnp.concatenate(
            [
                take(slice(parity * 16, parity * 16 + 16), tile).reshape(HALF, 128)
                for tile in range(TILES)
            ],
            axis=1,
        )
        if weighted:
            value = value * 2.0
            if parity == 0:
                row = lax.broadcasted_iota(jnp.int32, (HALF, 1), 0)
                value = value * jnp.where(row == 0, 0.5, 1.0)
        sides.append(dot(value.astype(bf16), tab_ref[parity], TN))
    sums, differences = sides[0] + sides[1], sides[0] - sides[1]
    return [v[:, t * 128 : t * 128 + 128] for v in (sums, differences) for t in range(4)]


def mixed_kernel(
    block_ref, tab_hbm, tok_hbm, stat_ref, cubes_ref, back_hbm,
    out_hbm,
    tab_ref, tok_ref, mix_ref, sems, out_sems,
):
    copies = bring(((tab_hbm, tab_ref), (tok_hbm, tok_ref)), sems)
    copies[0].wait()
    tiles = lon_inverse(lambda peers, tile: block_ref[peers, tile], tab_ref, True)
    copies[1].wait()
    out_copies = []
    for g in range(CHUNKS):
        own = pl.ds(g * GROUP, GROUP)
        gain, shift = cubes_ref[0, own], cubes_ref[1, own]
        for tile in range(8):
            lanes = slice(tile * 128, tile * 128 + 128)
            tok = tok_ref[own, :, lanes].astype(f32)
            normed = (tok - stat_ref[0, :, lanes][None]) * stat_ref[1, :, lanes][None]
            filtered = tiles[tile][g * GROUP * RW : (g + 1) * GROUP * RW].reshape(GROUP, RW, 128)
            mix_ref[own, :, lanes] = (filtered + (normed * gain + shift) + tok).astype(bf16)
        copy = pltpu.make_async_copy(mix_ref.at[own], out_hbm.at[own], out_sems.at[g])
        copy.start()
        out_copies.append(copy)
    for copy in out_copies:
        copy.wait()


def pulled_kernel(
    block_ref, tab_hbm, tok_hbm, cot_hbm, stat_ref, cubes_ref,
    out_ref, sum_ref, weight_ref,
    tab_ref, tok_ref, cot_ref, sems,
):
    copies = bring(((tab_hbm, tab_ref), (tok_hbm, tok_ref), (cot_hbm, cot_ref)), sems)

    def take(peers, tile):
        return block_ref[peers, tile * 32 : tile * 32 + 32, :]

    copies[0].wait()
    tiles = lon_inverse(take, tab_ref, False)
    share = jnp.sum(block_ref[:, PULL_ROWS - 16 :, :], axis=0)
    for i in range(12):
        weight_ref[0:1, i * CH : i * CH + CH] = share[i : i + 1, 0:CH]
    copies[1].wait()
    copies[2].wait()
    for tile in range(8):
        lanes = slice(tile * 128, tile * 128 + 128)
        tok = tok_ref[:, :, lanes].astype(f32)
        inv_std = stat_ref[1, :, lanes]
        normed = (tok - stat_ref[0, :, lanes][None]) * inv_std[None]
        pulled = tiles[tile].reshape(CH, RW, 128)
        cot = cot_ref[:, :, lanes].astype(f32)
        dnorm = (pulled + cot) * cubes_ref[0]
        out_ref[:, :, lanes] = cot + inv_std[None] * dnorm
        sum_ref[0, :, lanes] = jnp.sum(dnorm, axis=0)
        sum_ref[1, :, lanes] = jnp.sum(dnorm * normed, axis=0)


def inverse_call(kernel, name, in_specs, out_specs, out_shape, scratch):
    return pl.pallas_call(
        kernel,
        name=name,
        in_specs=in_specs,
        out_specs=out_specs,
        out_shape=out_shape,
        scratch_shapes=[
            pltpu.VMEM((2, HALF, HALF), bf16),
            pltpu.VMEM((CH, RW, LON), bf16),
            pltpu.VMEM((CH, RW, LON), bf16),
        ]
        + scratch,
        compiler_params=pltpu.CompilerParams(vmem_limit_bytes=28 * 2**20),
        cost_estimate=pl.CostEstimate(
            flops=4 * LANES * LON * LON, bytes_accessed=10 * 2**20, transcendentals=0
        ),
    )


def finish_kernel(part_ref, tok_ref, stat_ref, one_ref, two_ref, three_ref, four_ref, out_ref):
    terms = (one_ref, two_ref, three_ref, four_ref)
    count = 4.0 * CH
    mean, inv_std = stat_ref[0], stat_ref[1]
    one, two = total(terms, 0) / count, total(terms, 1) / count
    normed = (tok_ref[...].astype(f32) - mean[None]) * inv_std[None]
    out_ref[...] = (part_ref[...] - (inv_std * one)[None] - normed * (inv_std * two)[None]).astype(bf16)


def finish(part, tokens, stats, terms):
    block = pl.BlockSpec((CH // 4, RW, LON), lambda i: (i, 0, 0))
    return pl.pallas_call(
        finish_kernel,
        name="finish",
        grid=(4,),
        in_specs=[block, block] + [pl.BlockSpec((2, RW, LON), lambda i: (0, 0, 0))] * 5,
        out_specs=block,
        out_shape=jax.ShapeDtypeStruct((CH, RW, LON), bf16),
        compiler_params=pltpu.CompilerParams(vmem_limit_bytes=24 * 2**20),
        cost_estimate=pl.CostEstimate(
            flops=8 * CH * RW * LON, bytes_accessed=6 * 2**20, transcendentals=0
        ),
    )(part, tokens, stats, *terms)


def exchange(value):
    return lax.all_to_all(value, "lat", split_axis=0, concat_axis=0, tiled=True)


def group_terms(value):
    return [value] + [
        lax.ppermute(value, "grp", [(j, j ^ step) for j in range(4)]) for step in (1, 2, 3)
    ]


def per_device(tokens, cotangent, gain, shift, w_in, b_in, w_out, b_out):
    lon_host = lon_table()
    lon_tab, lon_high = jnp.asarray(lon_host), jnp.asarray(lon_host[:, 0])
    lon_tab = pltpu.with_memory_space_constraint(lon_tab, pltpu.HBM)
    lat_tab, spread = jnp.asarray(lat_table()), jnp.asarray(spread_table())
    tok_val = tokens.astype(f32)
    sums = jnp.stack([jnp.sum(tok_val, axis=0), jnp.sum(tok_val * tok_val, axis=0)])
    terms = group_terms(sums)
    spec_grad, grad_mark = lon_call(lon_grad_kernel, "lon_grad", 0, 1)(cotangent, lon_tab, sums)
    spec_field, stats = lon_call(lon_field_kernel, "lon_field", 6, 1)(
        tokens, lon_tab, jnp.repeat(gain, RW).reshape(TILES, 1, 128),
        jnp.repeat(shift, RW).reshape(TILES, 1, 128), *terms, grad_mark
    )

    modes_field = exchange(spec_field)
    modes_grad = exchange(spec_grad)
    back_field, *saved = field_modes(modes_field, lat_tab, spread, w_in, b_in, w_out, b_out)
    gain_now, shift_now, saved[0] = lax.optimization_barrier((gain, shift, saved[0]))
    cubes = jnp.stack([gain_now, shift_now]).reshape(2, CH, 1, 1)
    cubes = jnp.broadcast_to(cubes, (2, CH, 1, 128))
    rows_field = exchange(back_field)
    grad_rows = grad_modes(modes_grad, lat_tab, spread)
    back_grad = pull_modes(grad_rows, saved, lat_tab, spread, w_in, w_out, cubes)
    back_grad, rows_field = lax.optimization_barrier((back_grad, rows_field))
    rows_grad = exchange(back_grad)
    part, back, grad_weights = inverse_call(
        pulled_kernel,
        "pulled",
        [VMEM, HBM, HBM, HBM, VMEM, VMEM],
        [VMEM] * 3,
        [
            jax.ShapeDtypeStruct((CH, RW, LON), f32),
            STATS_SHAPE,
            jax.ShapeDtypeStruct((1, 1152), f32),
        ],
        [pltpu.SemaphoreType.DMA((3,))],
    )(rows_grad, lon_high, tokens, cotangent, stats, cubes)
    back_terms = group_terms(back)
    mixed = inverse_call(
        mixed_kernel,
        "mixed",
        [VMEM, HBM, HBM, VMEM, VMEM, HBM],
        HBM,
        jax.ShapeDtypeStruct((CH, RW, LON), bf16),
        [pltpu.SemaphoreType.DMA((2,)), pltpu.SemaphoreType.DMA((CHUNKS,))],
    )(rows_field, lon_high, tokens, stats, cubes, back)
    grad_tokens = finish(part, tokens, stats, back_terms)
    return (mixed, grad_tokens, grad_weights)


def solution(mesh):
    in_specs = (
        P("grp", "lat", None),
        P("grp", "lat", None),
        P("grp"),
        P("grp"),
        P("grp", None, None, None),
        P("grp", None, None),
        P("grp", None, None, None),
        P("grp", None, None),
    )
    out_specs = (P("grp", "lat", None), P("grp", "lat", None), P("grp", "lat"))
    return jax.shard_map(
        per_device, mesh=mesh, in_specs=in_specs, out_specs=out_specs, check_vma=False
    )
```

time: 238 us -> 228 us (0.958)
  waiting for transfers between devices: 110 us -> 15.5 us
  blocking collectives: 19.7 us -> 97.1 us
  local copies, waits for them, and re-layouts: 7.09 us -> 16.3 us
  starting transfers between devices: 33.8 us -> 26.6 us
  Pallas kernels: 64.1 us -> 69 us
    all_to_all x0 -> x2, blocking collectives: none -> 97.1 us  [exchange(): return lax.all_to_all(value, 'lat', split_axis=0, concat_axis=0, tiled=True)]
    all_to_all x4 -> x2, waiting for transfers between devices: 110 us -> 15.4 us  [exchange(): return lax.all_to_all(value, 'lat', split_axis=0, concat_axis=0, tiled=True)]
    all_gather x2 -> x0, blocking collectives: 19.7 us -> none  [the longest x1 11.1 us: per_device(): grad_tokens = finish(part, tokens, lax.all_gather(back, 'grp'), stats)]
    all_to_all x4 -> x2, starting transfers between devices: 33.8 us -> 15.8 us  [exchange(): return lax.all_to_all(value, 'lat', split_axis=0, concat_axis=0, tiled=True)]
    ppermute x0 -> x6, starting transfers between devices: none -> 10.8 us  [group_terms(): lax.ppermute(value, 'grp', [(j, j ^ step) for j in range(4)])]
    unnamed x22 -> x54, local copies, waits for them, and re-layouts: 6.77 us -> 15.5 us
    pallas_call x1, Pallas kernels: 16 us -> 22.6 us  [field_modes(): pl.pallas_call(field_modes_kernel, name='field_modes', grid=(STEPS,), in_...]
    pallas_call x4, Pallas kernels: 23.9 us -> 18.6 us  [the longest x1 6.06 us: per_device(): lon_call(lon_grad_kernel, 'lon_grad', 0, 1)(cotangent, lon_tab, sums)]
  transfers between devices with their start and end apart: 4 -> 8, of which waited for: 4 -> 2; matrix products, arithmetic and copies ran while one was open for 0% -> 0% of each run, Pallas kernels for 22% -> 26%
where the time goes in v3:
time: 228 us; the launch traced here: 227 us
  blocking collectives  97.1 us (43%)
  Pallas kernels  69 us (30%)
  starting transfers between devices  26.6 us (12%)
  local copies, waits for them, and re-layouts  16.3 us (7%)
  waiting for transfers between devices  15.5 us (7%)
    all_to_all x2, blocking collectives, exchange(): return lax.all_to_all(value, 'lat', split_axis=0, concat_axis=0, tiled=True)  97.1 us
    pallas_call x1, Pallas kernels, field_modes(): pl.pallas_call(field_modes_kernel, name='field_modes', grid=(STEPS,), in_...  22.6 us
    pallas_call x1, Pallas kernels, pull_modes(): pl.pallas_call(pull_modes_kernel, name='pull_modes', grid=(STEPS,), in_sp...  17.4 us
    all_to_all x2, starting transfers between devices, exchange(): return lax.all_to_all(value, 'lat', split_axis=0, concat_axis=0, tiled=True)  15.8 us
    unnamed x54, local copies, waits for them, and re-layouts  15.5 us
    all_to_all x2, waiting for transfers between devices, exchange(): return lax.all_to_all(value, 'lat', split_axis=0, concat_axis=0, tiled=True)  15.4 us
    ppermute x6, starting transfers between devices, group_terms(): lax.ppermute(value, 'grp', [(j, j ^ step) for j in range(4)])  10.8 us
    pallas_call x1, Pallas kernels, grad_modes(): pl.pallas_call(grad_modes_kernel, name='grad_modes', grid=(STEPS,), in_sp...  8.3 us
  transfers between devices with their start and end apart: 8, of which 2 were waited for; matrix products, arithmetic and copies ran while one was open for 0% of the time, Pallas kernels for 26%

profile of v3, /device:TPU:1, one launch (start us, length us, event | category | flops | bytes accessed | tf_op | source)
XLA Modules:
  0.0 227.3 jit_solution(17454310895750683754)
XLA Ops:
  0.6 1.9 convert_reduce_fusion
  2.5 4.2 %collective-permute-start.2 = (f32[2,8,1024]{2,1,0:T(8,128)S(1)}, f32[2,8,1024]{2,1,0:T(8,128)S(1)}, u32[]{:S(2)}, u32[]{:S(2)}) collective-permute-start(f32[2,8,1024]{2,1,0:T(8,128)S(1)} %pad_maximum_fusion.sums_hbm.one_ref), channel_id=1, source_target_pairs={{0,3},{1,2},{2,1},{3,0},{4,7},{5,6},{6,5},{7,4},{8,11},{9,10},{10,... | collective-permute-start | bytes 196616 | tf_op jit(solution)/shard_map/ppermute | solution.py:564
  6.7 0.1 collective-permute-start.1
  6.9 0.3 collective-permute-start
  7.2 1.4 copy-done.3
  8.6 6.1 %lon_grad.1 = (f32[32,6,32,128]{3,2,1,0:T(8,128)}, f32[8,128]{1,0:T(8,128)S(1)}) custom-call(bf16[96,8,1024]{2,1,0:T(8,128)(2,1)S(1)} %copy-done.3, bf16[2,2,512,512]{3,2,1,0:T(8,128)(2,1)} %constant.10.clone.tab_hbm, f32[2,8,1024]{2,1,0:T(8,128)S(1)} %pad_maximum_fusion.sums_hbm.one_ref), custom_call_target="tpu_custom_call" | custom-call | flops 4831838208 | bytes 7340032 | tf_op jit(solution)/shard_map/lon_grad/pallas_call | solution.py:576
  15.3 5.1 %lon_field.1 = (f32[32,6,32,128]{3,2,1,0:T(8,128)S(1)}, f32[2,8,1024]{2,1,0:T(8,128)S(1)}) custom-call(bf16[96,8,1024]{2,1,0:T(8,128)(2,1)S(1)} %copy-done, bf16[2,2,512,512]{3,2,1,0:T(8,128)(2,1)} %constant.10.clone.tab_hbm, f32[6,1,128]{2,1,0:T(1,128)S(1)} %broadcast_in_dim.26.gain_ref, f32[6,1,128]{2,1,0:T(1,128)S(1)} %broadcast_in_dim.27.shift_ref, ...), custom_call_target="tpu_custom_call" | custom-call | flops 4831838208 | bytes 7340032 | tf_op jit(solution)/shard_map/lon_field/pallas_call | solution.py:577
  20.4 46.8 %all_to_all.20.block_ref = f32[32,6,32,128]{3,2,1,0:T(8,128)} all-to-all(f32[32,6,32,128]{3,2,1,0:T(8,128)S(1)} %get-tuple-element.23), channel_id=1, replica_groups=mesh['lat'=32,'grp'=4] {'lat'}, dimensions={0} | all-to-all | bytes 6291456 | tf_op jit(solution)/shard_map/all_to_all | solution.py:559
  67.3 6.7 %all-to-all-start = ((f32[32,6,32,128]{3,2,1,0:T(8,128)}), f32[32,6,32,128]{3,2,1,0:T(8,128)}, u32[]{:S(2)}, u32[]{:S(2)}) async-start(f32[32,6,32,128]{3,2,1,0:T(8,128)} %get-tuple-element.21), calls=%async_computation | async-start | bytes 6291456 | tf_op jit(solution)/shard_map/all_to_all | solution.py:559
  74.1 1.0 copy-done.11
  75.1 22.6 %field_modes.1 = (f32[32,6,32,128]{3,2,1,0:T(8,128)S(1)}, bf16[4096,256]{1,0:T(8,128)(2,1)S(1)}, bf16[4096,256]{1,0:T(8,128)(2,1)S(1)}, bf16[4096,256]{1,0:T(8,1...) custom-call(f32[32,6,32,128]{3,2,1,0:T(8,128)} %all_to_all.20.block_ref, ...), custom_call_target="tpu_custom_call" | custom-call | flops 25769803776 | bytes 14680064 | tf_op jit(solution)/shard_map/field_modes/pallas_call | solution.py:395
  97.7 1.6 copy-done.2
  99.4 1.4 copy-done.15
  100.7 1.3 copy-done.17
  102.1 1.3 copy-done.19
  103.4 1.3 copy-done.21
  104.7 1.3 copy-done.23
  106.0 7.4 %all-to-all-done.block_ref = f32[32,6,32,128]{3,2,1,0:T(8,128)} async-done(((f32[32,6,32,128]{3,2,1,0:T(8,128)}), f32[32,6,32,128]{3,2,1,0:T(8,128)}, u32[]{:S(2)}, u32[]{:S(2)}) %all-to-all-start) | async-done | bytes 3145760 | tf_op jit(solution)/shard_map/all_to_all | solution.py:559
  113.4 9.1 %all-to-all-start.2 = ((f32[32,6,32,128]{3,2,1,0:T(8,128)}), f32[32,6,32,128]{3,2,1,0:T(8,128)}, u32[]{:S(2)}, u32[]{:S(2)}) async-start(f32[32,6,32,128]{3,2,1,0:T(8,128)} %copy-done.2), calls=%async_computation.2 | async-start | bytes 6291456 | tf_op jit(solution)/shard_map/all_to_all | solution.py:559
  122.5 1.0 copy-done.12
  123.6 8.3 %grad_modes.1.grad_ref = f32[4096,256]{1,0:T(8,128)S(1)} custom-call(f32[32,6,32,128]{3,2,1,0:T(8,128)} %all-to-all-done.block_ref, bf16[2,2,256,256]{3,2,1,0:T(8,128)(2,1)S(1)} %copy-done.12, bf16[768,1024]{1,0:T(8,128)(2,1)S(1)} %copy-done.9), custom_call_target="tpu_custom_call" | custom-call | flops 12884901888 | bytes 8388608 | tf_op jit(solution)/shard_map/grad_modes/pallas_call | solution.py:379
  131.9 2.0 copy-done.14
  133.9 0.3 broadcast_in_dim.25.cubes_hbm.cubes_ref
  134.2 17.4 %pull_modes.1 = f32[32,208,128]{2,1,0:T(8,128)S(1)} custom-call(f32[4096,256]{1,0:T(8,128)} %copy-done.14, bf16[4096,256]{1,0:T(8,128)(2,1)S(1)} %copy-done.16, bf16[4096,256]{1,0:T(8,128)(2,1)S(1)} %copy-done.18, bf16[4096,256]{1,0:T(8,128)(2,1)S(1)} %copy-done.20, bf16[4096,256]{1,0:T(8,128)(2,1)S(1)} %copy-done.22, bf16[4096,256]{1,0:T(8,128)(2,1)S(1)} %copy-done.24, ...), custom_call_target="tpu_custom_call" | custom-call | flops 17179869184 | bytes 14680064 | tf_op jit(solution)/shard_map/pull_modes/pallas_call | solution.py:417
  151.6 1.7 copy-done.1
  153.3 8.1 %all-to-all-done.2.block_ref = f32[32,6,32,128]{3,2,1,0:T(8,128)} async-done(((f32[32,6,32,128]{3,2,1,0:T(8,128)}), f32[32,6,32,128]{3,2,1,0:T(8,128)}, u32[]{:S(2)}, u32[]{:S(2)}) %all-to-all-start.2) | async-done | bytes 3145760 | tf_op jit(solution)/shard_map/all_to_all | solution.py:559
  161.4 50.3 %all_to_all.21.block_ref = f32[32,208,128]{2,1,0:T(8,128)S(1)} all-to-all(f32[32,208,128]{2,1,0:T(8,128)} %copy-done.1), channel_id=1, replica_groups=mesh['lat'=32,'grp'=4] {'lat'}, dimensions={0} | all-to-all | bytes 6815744 | tf_op jit(solution)/shard_map/all_to_all | solution.py:559
  211.7 2.5 %pulled.1 = (f32[96,8,1024]{2,1,0:T(8,128)S(1)}, f32[2,8,1024]{2,1,0:T(8,128)S(1)}, f32[1,1152]{1,0:T(1,128)}) custom-call(f32[32,208,128]{2,1,0:T(8,128)S(1)} %all_to_all.21.block_ref, bf16[2,512,512]{2,1,0:T(8,128)(2,1)S(1)} %copy-done.10, bf16[96,8,1024]{2,1,0:T(8,128)(2,1)S(1)} %copy-done, bf16[96,8,1024]{2,1,0:T(8,128)(2,1)S(1)} %copy-done.4, ...), custom_call_target="tpu_custom_call" | custom-call | flops 3221225472 | bytes 10485760 | tf_op jit(solution)/shard_map/pulled/pallas_call | solution.py:593
  214.3 5.6 %collective-permute-start.5 = (f32[2,8,1024]{2,1,0:T(8,128)S(1)}, f32[2,8,1024]{2,1,0:T(8,128)S(1)}, u32[]{:S(2)}, u32[]{:S(2)}) collective-permute-start(f32[2,8,1024]{2,1,0:T(8,128)S(1)} %get-tuple-element.36.back_hbm.one_ref), channel_id=1, source_target_pairs={{0,3},{1,2},{2,1},{3,0},{4,7},{5,6},{6,5},{7,4},{8,11},{9,10},{10,... | collective-permute-start | bytes 196616 | tf_op jit(solution)/shard_map/ppermute | solution.py:564
  219.8 0.5 collective-permute-start.4
  220.4 4.8 %mixed.1 = bf16[96,8,1024]{2,1,0:T(8,128)(2,1)} custom-call(f32[32,6,32,128]{3,2,1,0:T(8,128)} %all-to-all-done.2.block_ref, bf16[2,512,512]{2,1,0:T(8,128)(2,1)S(1)} %copy-done.10, bf16[96,8,1024]{2,1,0:T(8,128)(2,1)S(1)} %copy-done, f32[2,8,1024]{2,1,0:T(8,128)S(1)} %get-tuple-element.34.stat_ref, ...), custom_call_target="tpu_custom_call" | custom-call | flops 3221225472 | bytes 10485760 | tf_op jit(solution)/shard_map/mixed/pallas_call | solution.py:606
  225.2 2.1 finish.1
  (58 shorter events, 0.6 us)
Async XLA Ops:
  2.5 12.2 %copy-start.25 = (f32[96]{0:T(128)S(1)}, f32[96]{0:T(128)}, u32[]{:S(2)}) copy-start(f32[96]{0:T(128)} %param.14) | copy-start | bytes 1156
  2.5 12.3 %copy-start.26 = (f32[96]{0:T(128)S(1)}, f32[96]{0:T(128)}, u32[]{:S(2)}) copy-start(f32[96]{0:T(128)} %param.15) | copy-start | bytes 1156
  2.5 12.8 %copy-start = (bf16[96,8,1024]{2,1,0:T(8,128)(2,1)S(1)}, bf16[96,8,1024]{2,1,0:T(8,128)(2,1)}, u32[]{:S(2)}) copy-start(bf16[96,8,1024]{2,1,0:T(8,128)(2,1)} %tok_ref.1) | copy-start | bytes 4718596
  2.5 12.7 %collective-permute-start.2 = (f32[2,8,1024]{2,1,0:T(8,128)S(1)}, f32[2,8,1024]{2,1,0:T(8,128)S(1)}, u32[]{:S(2)}, u32[]{:S(2)}) collective-permute-start(f32[2,8,1024]{2,1,0:T(8,128)S(1)} %pad_maximum_fusion.sums_hbm.one_ref), channel_id=1, source_target_pairs={{0,3},{1,2},{2,1},{3,0},{4,7},{5,6},{6,5},{7,4},{8,11},{9,10},{10,... | collective-permute-start | bytes 196616 | tf_op jit(solution)/shard_map/ppermute | solution.py:564
  6.7 8.5 %collective-permute-start.1 = (f32[2,8,1024]{2,1,0:T(8,128)S(1)}, f32[2,8,1024]{2,1,0:T(8,128)S(1)}, u32[]{:S(2)}, u32[]{:S(2)}) collective-permute-start(f32[2,8,1024]{2,1,0:T(8,128)S(1)} %pad_maximum_fusion.sums_hbm.one_ref), channel_id=1, source_target_pairs={{0,2},{1,3},{2,0},{3,1},{4,6},{5,7},{6,4},{7,5},{8,10},{9,11},{10,... | collective-permute-start | bytes 196616 | tf_op jit(solution)/shard_map/ppermute | solution.py:564
  6.9 8.4 %collective-permute-start = (f32[2,8,1024]{2,1,0:T(8,128)S(1)}, f32[2,8,1024]{2,1,0:T(8,128)S(1)}, u32[]{:S(2)}, u32[]{:S(2)}) collective-permute-start(f32[2,8,1024]{2,1,0:T(8,128)S(1)} %pad_maximum_fusion.sums_hbm.one_ref), channel_id=1, source_target_pairs={{0,1},{1,0},{2,3},{3,2},{4,5},{5,4},{6,7},{7,6},{8,9},{9,8},{10,11... | collective-permute-start | bytes 196616 | tf_op jit(solution)/shard_map/ppermute | solution.py:564
  7.2 1.4 copy-start.3
  67.3 6.8 %copy-start.5 = (f32[1,2,96,96]{3,2,1,0:T(8,128)S(1)}, f32[1,2,96,96]{3,2,1,0:T(8,128)}, u32[]{:S(2)}) copy-start(f32[1,2,96,96]{3,2,1,0:T(8,128)} %w_in_ref.3) | copy-start | bytes 221188
  67.3 6.8 %copy-start.6 = (f32[1,2,96,96]{3,2,1,0:T(8,128)S(1)}, f32[1,2,96,96]{3,2,1,0:T(8,128)}, u32[]{:S(2)}) copy-start(f32[1,2,96,96]{3,2,1,0:T(8,128)} %w_out_ref.3) | copy-start | bytes 221188
  67.3 6.8 %copy-start.7 = (f32[1,2,96]{2,1,0:T(2,128)S(1)}, f32[1,2,96]{2,1,0:T(2,128)}, u32[]{:S(2)}) copy-start(f32[1,2,96]{2,1,0:T(2,128)} %b_in_ref.1) | copy-start | bytes 2308
  67.3 6.8 %copy-start.8 = (f32[1,2,96]{2,1,0:T(2,128)S(1)}, f32[1,2,96]{2,1,0:T(2,128)}, u32[]{:S(2)}) copy-start(f32[1,2,96]{2,1,0:T(2,128)} %b_out_ref.1) | copy-start | bytes 2308
  67.3 6.8 %copy-start.9 = (bf16[768,1024]{1,0:T(8,128)(2,1)S(1)}, bf16[768,1024]{1,0:T(8,128)(2,1)}, u32[]{:S(2)}) copy-start(bf16[768,1024]{1,0:T(8,128)(2,1)} %constant.13.clone.spread_ref) | copy-start | bytes 4718596
  67.3 46.1 %all-to-all-start = ((f32[32,6,32,128]{3,2,1,0:T(8,128)}), f32[32,6,32,128]{3,2,1,0:T(8,128)}, u32[]{:S(2)}, u32[]{:S(2)}) async-start(f32[32,6,32,128]{3,2,1,0:T(8,128)} %get-tuple-element.21), calls=%async_computation | async-start | bytes 6291456 | tf_op jit(solution)/shard_map/all_to_all | solution.py:559
  97.7 1.7 copy-start.2
  99.4 1.4 copy-start.15
  100.7 1.3 copy-start.17
  103.4 1.3 copy-start.21
  104.7 1.3 copy-start.23
  113.4 48.0 %all-to-all-start.2 = ((f32[32,6,32,128]{3,2,1,0:T(8,128)}), f32[32,6,32,128]{3,2,1,0:T(8,128)}, u32[]{:S(2)}, u32[]{:S(2)}) async-start(f32[32,6,32,128]{3,2,1,0:T(8,128)} %copy-done.2), calls=%async_computation.2 | async-start | bytes 6291456 | tf_op jit(solution)/shard_map/all_to_all | solution.py:559
  123.6 10.6 %copy-start.13 = (bf16[2,2,256,256]{3,2,1,0:T(8,128)(2,1)S(1)}, bf16[2,2,256,256]{3,2,1,0:T(8,128)(2,1)}, u32[]{:S(2)}) copy-start(bf16[2,2,256,256]{3,2,1,0:T(8,128)(2,1)} %constant.12.clone.tab_ref) | copy-start | bytes 1572868
  123.6 10.6 %copy-start.16 = (bf16[4096,256]{1,0:T(8,128)(2,1)S(1)}, bf16[4096,256]{1,0:T(8,128)(2,1)}, u32[]{:S(2)}) copy-start(bf16[4096,256]{1,0:T(8,128)(2,1)} %copy-done.15) | copy-start | bytes 6291460
  123.6 10.6 %copy-start.18 = (bf16[4096,256]{1,0:T(8,128)(2,1)S(1)}, bf16[4096,256]{1,0:T(8,128)(2,1)}, u32[]{:S(2)}) copy-start(bf16[4096,256]{1,0:T(8,128)(2,1)} %copy-done.17) | copy-start | bytes 6291460
  123.6 10.6 %copy-start.20 = (bf16[4096,256]{1,0:T(8,128)(2,1)S(1)}, bf16[4096,256]{1,0:T(8,128)(2,1)}, u32[]{:S(2)}) copy-start(bf16[4096,256]{1,0:T(8,128)(2,1)} %copy-done.19) | copy-start | bytes 6291460
  123.6 10.6 %copy-start.22 = (bf16[4096,256]{1,0:T(8,128)(2,1)S(1)}, bf16[4096,256]{1,0:T(8,128)(2,1)}, u32[]{:S(2)}) copy-start(bf16[4096,256]{1,0:T(8,128)(2,1)} %copy-done.21) | copy-start | bytes 6291460
  123.6 10.6 %copy-start.24 = (bf16[4096,256]{1,0:T(8,128)(2,1)S(1)}, bf16[4096,256]{1,0:T(8,128)(2,1)}, u32[]{:S(2)}) copy-start(bf16[4096,256]{1,0:T(8,128)(2,1)} %copy-done.23) | copy-start | bytes 6291460
  131.9 2.0 copy-start.14
  151.6 1.7 copy-start.1
  153.3 58.4 %copy-start.4 = (bf16[96,8,1024]{2,1,0:T(8,128)(2,1)S(1)}, bf16[96,8,1024]{2,1,0:T(8,128)(2,1)}, u32[]{:S(2)}) copy-start(bf16[96,8,1024]{2,1,0:T(8,128)(2,1)} %cot_hbm.1) | copy-start | bytes 4718596
  161.4 50.3 %copy-start.10 = (bf16[2,512,512]{2,1,0:T(8,128)(2,1)S(1)}, bf16[2,512,512]{2,1,0:T(8,128)(2,1)}, u32[]{:S(2)}) copy-start(bf16[2,512,512]{2,1,0:T(8,128)(2,1)} %constant.11.clone.tab_hbm) | copy-start | bytes 3145732
  214.3 10.9 %collective-permute-start.5 = (f32[2,8,1024]{2,1,0:T(8,128)S(1)}, f32[2,8,1024]{2,1,0:T(8,128)S(1)}, u32[]{:S(2)}, u32[]{:S(2)}) collective-permute-start(f32[2,8,1024]{2,1,0:T(8,128)S(1)} %get-tuple-element.36.back_hbm.one_ref), channel_id=1, source_target_pairs={{0,3},{1,2},{2,1},{3,0},{4,7},{5,6},{6,5},{7,4},{8,11},{9,10},{10,... | collective-permute-start | bytes 196616 | tf_op jit(solution)/shard_map/ppermute | solution.py:564
  219.8 5.4 %collective-permute-start.4 = (f32[2,8,1024]{2,1,0:T(8,128)S(1)}, f32[2,8,1024]{2,1,0:T(8,128)S(1)}, u32[]{:S(2)}, u32[]{:S(2)}) collective-permute-start(f32[2,8,1024]{2,1,0:T(8,128)S(1)} %get-tuple-element.36.back_hbm.one_ref), channel_id=1, source_target_pairs={{0,2},{1,3},{2,0},{3,1},{4,6},{5,7},{6,4},{7,5},{8,10},{9,11},{10,... | collective-permute-start | bytes 196616 | tf_op jit(solution)/shard_map/ppermute | solution.py:564
  220.4 4.9 %collective-permute-start.3 = (f32[2,8,1024]{2,1,0:T(8,128)S(1)}, f32[2,8,1024]{2,1,0:T(8,128)S(1)}, u32[]{:S(2)}, u32[]{:S(2)}) collective-permute-start(f32[2,8,1024]{2,1,0:T(8,128)S(1)} %get-tuple-element.36.back_hbm.one_ref), channel_id=1, source_target_pairs={{0,1},{1,0},{2,3},{3,2},{4,5},{5,4},{6,7},{7,6},{8,9},{9,8},{10,11... | collective-permute-start | bytes 196616 | tf_op jit(solution)/shard_map/ppermute | solution.py:564
  (3 other events, 3.4 us)

commit v4 on v3

--- a/solution.py
+++ b/solution.py
@@ -42,6 +42,18 @@
         theta = 2.0 * np.pi * ((m[:, None] * n[None, :]) % LON) / LON
         table = np.stack([np.cos(theta), -np.sin(theta)], axis=1).reshape(HALF, HALF)
         parts.append(host_split(table / 32.0))
+    return np.stack(parts)
+
+
+def grad_table():
+    parts = []
+    n = np.arange(LON)
+    for parity in range(2):
+        m = 2 * np.arange(256) + parity
+        theta = 2.0 * np.pi * ((m[:, None] * n[None, :]) % LON) / LON
+        table = np.stack([np.cos(theta), -np.sin(theta)], axis=1)
+        table = table * np.where(m == 0, 1.0, 2.0)[:, None, None]
+        parts.append(host_split(table.reshape(HALF, LON) / 32.0)[0])
     return np.stack(parts)
 
 
@@ -88,6 +100,10 @@
     )
 
 
+def in_hbm(value):
+    return pltpu.with_memory_space_constraint(value, pltpu.HBM)
+
+
 CHUNKS = 4
 GROUP = CH // CHUNKS
 
@@ -99,45 +115,29 @@
     return copies
 
 
-def lon_transform(prepare, finish_rows, x_ref, tab_hbm, out_hbm, scratch):
-    tab_ref, halves_ref, wire_ref, tab_sems, sems = scratch
-    tab_copies = bring([(tab_hbm.at[p], tab_ref.at[p]) for p in range(2)], tab_sems)
-    for tile in range(4):
-        pair = []
-        for lanes in (slice(tile * 128, tile * 128 + 128), slice(HALF + tile * 128, HALF + tile * 128 + 128)):
-            pair.append(prepare(x_ref[:, :, lanes].astype(f32), lanes).reshape(LANES, 128))
-        for parity, value in enumerate((pair[0] + pair[1], pair[0] - pair[1])):
-            high, low = split(value)
-            halves_ref[parity, 0, :, tile * 128 : tile * 128 + 128] = high
-            halves_ref[parity, 1, :, tile * 128 : tile * 128 + 128] = low
-    peers = PEERS // 2
-    copies = []
+def lon_grad_kernel(
+    x_hbm, tab_hbm, sums_ref,
+    out_hbm, mark_ref,
+    x_ref, tab_ref, wire_ref, in_sems, out_sems,
+):
+    copies = bring(
+        [(x_hbm, x_ref)] + [(tab_hbm.at[p], tab_ref.at[p]) for p in range(2)], in_sems
+    )
+    mark_ref[...] = jnp.zeros((8, 128), f32)
+    out_copies = []
+    copies[0].wait()
     for parity in range(2):
-        tab_copies[parity].wait()
-        both = dot(tab_ref[parity].reshape(2 * HALF, HALF), halves_ref[parity, 0], NT)
-        value = both[:HALF] + both[HALF:] + dot(tab_ref[parity, 0], halves_ref[parity, 1], NT)
-        own = pl.ds(parity * peers, peers)
+        copies[1 + parity].wait()
+        value = dot(tab_ref[parity], x_ref[...].reshape(LANES, LON), NT)
+        own = pl.ds(parity * 16, 16)
         for tile in range(TILES):
-            piece = finish_rows(value[:, tile * 128 : tile * 128 + 128], tile)
-            wire_ref[own, tile] = piece.reshape(peers, 32, 128)
-        if parity == 0:
-            finish_rows(None, wire_ref)
-        copy = pltpu.make_async_copy(wire_ref.at[own], out_hbm.at[own], sems.at[parity])
+            piece = value[:, tile * 128 : tile * 128 + 128]
+            wire_ref[own, tile] = piece.reshape(16, 32, 128)
+        copy = pltpu.make_async_copy(wire_ref.at[own], out_hbm.at[own], out_sems.at[parity])
         copy.start()
-        copies.append(copy)
-    for copy in copies:
+        out_copies.append(copy)
+    for copy in out_copies:
         copy.wait()
-
-
-def lon_grad_kernel(x_ref, tab_hbm, sums_hbm, out_hbm, mark_ref, *scratch):
-    mark_ref[...] = jnp.zeros((8, 128), f32)
-
-    def finish_rows(value, at):
-        if value is not None:
-            return value
-        at[0, :, 0:2, :] = at[0, :, 0:2, :] * 0.5
-
-    lon_transform(lambda value, lanes: value * 2.0, finish_rows, x_ref, tab_hbm, out_hbm, scratch)
 
 
 def total(terms, at):
@@ -145,55 +145,83 @@
 
 
 def lon_field_kernel(
-    x_ref, tab_hbm, gain_ref, shift_ref, one_ref, two_ref, three_ref, four_ref,
-    mark_hbm,
-    out_hbm, stat_ref,
-    *scratch,
+    x_ref, tab_hbm, gain_ref, shift_ref, one_ref, two_ref, three_ref, four_ref, mark_ref,
+    out_ref, stat_ref,
+    tab_ref, halves_ref, tab_sems,
 ):
+    tab_copies = bring([(tab_hbm.at[p], tab_ref.at[p]) for p in range(2)], tab_sems)
     terms = (one_ref, two_ref, three_ref, four_ref)
     count = 4.0 * CH
     mean = total(terms, 0) / count
     inv_std = lax.rsqrt(total(terms, 1) / count - mean * mean + norm_eps)
     stat_ref[0], stat_ref[1] = mean, inv_std
-
-    def prepare(value, lanes):
-        return (value - mean[:, lanes][None]) * inv_std[:, lanes][None]
-
-    def finish_rows(value, at):
-        if value is not None:
-            return value * gain_ref[at]
+    for tile in range(4):
+        pair = []
+        for start in (tile * 128, HALF + tile * 128):
+            lanes = slice(start, start + 128)
+            value = x_ref[:, :, lanes].astype(f32)
+            value = (value - mean[:, lanes][None]) * inv_std[:, lanes][None]
+            pair.append(value.reshape(LANES, 128))
+        for parity, value in enumerate((pair[0] + pair[1], pair[0] - pair[1])):
+            high, low = split(value)
+            halves_ref[parity, 0, :, tile * 128 : tile * 128 + 128] = high
+            halves_ref[parity, 1, :, tile * 128 : tile * 128 + 128] = low
+    for parity in range(2):
+        tab_copies[parity].wait()
+        both = dot(tab_ref[parity].reshape(2 * HALF, HALF), halves_ref[parity, 0], NT)
+        value = both[:HALF] + both[HALF:] + dot(tab_ref[parity, 0], halves_ref[parity, 1], NT)
         for tile in range(TILES):
-            at[0, tile, 0:1, :] = at[0, tile, 0:1, :] + shift_ref[tile] * 32.0
-
-    lon_transform(prepare, finish_rows, x_ref, tab_hbm, out_hbm, scratch)
+            piece = value[:, tile * 128 : tile * 128 + 128] * gain_ref[tile]
+            out_ref[pl.ds(parity * 16, 16), tile] = piece.reshape(16, 32, 128)
+    for tile in range(TILES):
+        out_ref[0, tile, 0:1, :] = out_ref[0, tile, 0:1, :] + shift_ref[tile] * 32.0
 
 
 VMEM = pl.BlockSpec(memory_space=pltpu.VMEM)
 HBM = pl.BlockSpec(memory_space=pltpu.HBM)
 STATS_SHAPE = jax.ShapeDtypeStruct((2, RW, LON), f32)
-
-
-def lon_call(kernel, name, more, unread):
+LON_COST = pl.CostEstimate(
+    flops=6 * LANES * LON * LON, bytes_accessed=7 * 2**20, transcendentals=0
+)
+
+
+def lon_grad(cotangent, table, sums):
     return pl.pallas_call(
-        kernel,
-        name=name,
-        in_specs=[VMEM, HBM] + [VMEM] * (more + unread),
+        lon_grad_kernel,
+        name="lon_grad",
+        in_specs=[HBM, HBM, VMEM],
         out_specs=[HBM, VMEM],
-        out_shape=[WIRE_SHAPE, STATS_SHAPE]
-        if more
-        else [pltpu.HBM(WIRE_SHAPE.shape, f32), jax.ShapeDtypeStruct((8, 128), f32)],
+        out_shape=[
+            pltpu.HBM(WIRE_SHAPE.shape, f32),
+            jax.ShapeDtypeStruct((8, 128), f32),
+        ],
+        scratch_shapes=[
+            pltpu.VMEM((CH, RW, LON), bf16),
+            pltpu.VMEM((2, HALF, LON), bf16),
+            pltpu.VMEM((PEERS, TILES, 32, 128), f32),
+            pltpu.SemaphoreType.DMA((3,)),
+            pltpu.SemaphoreType.DMA((2,)),
+        ],
+        compiler_params=pltpu.CompilerParams(vmem_limit_bytes=28 * 2**20),
+        cost_estimate=LON_COST,
+    )(in_hbm(cotangent), in_hbm(table), sums)
+
+
+def lon_field(tokens, table, *small):
+    return pl.pallas_call(
+        lon_field_kernel,
+        name="lon_field",
+        in_specs=[VMEM, HBM] + [VMEM] * len(small),
+        out_specs=[VMEM, VMEM],
+        out_shape=[WIRE_SHAPE, STATS_SHAPE],
         scratch_shapes=[
             pltpu.VMEM((2, 2, HALF, HALF), bf16),
             pltpu.VMEM((2, 2, LANES, HALF), bf16),
-            pltpu.VMEM((PEERS, TILES, 32, 128), f32),
-            pltpu.SemaphoreType.DMA((2,)),
             pltpu.SemaphoreType.DMA((2,)),
         ],
         compiler_params=pltpu.CompilerParams(vmem_limit_bytes=24 * 2**20),
-        cost_estimate=pl.CostEstimate(
-            flops=6 * LANES * LON * LON, bytes_accessed=7 * 2**20, transcendentals=0
-        ),
-    )
+        cost_estimate=LON_COST,
+    )(tokens, in_hbm(table), *small)
 
 
 def unpack_rows(block_ref, spread_ref, rows_ref, halves_ref, terms):
@@ -455,14 +483,23 @@
 
 
 def mixed_kernel(
-    block_ref, tab_hbm, tok_hbm, stat_ref, cubes_ref, back_hbm,
+    block_hbm, tab_hbm, tok_hbm, stat_ref, cubes_ref, back_hbm,
     out_hbm,
-    tab_ref, tok_ref, mix_ref, sems, out_sems,
+    tab_ref, tok_ref, mix_ref, block_ref, sems, out_sems,
 ):
-    copies = bring(((tab_hbm, tab_ref), (tok_hbm, tok_ref)), sems)
+    halves = [
+        (block_hbm.at[pl.ds(p * 16, 16)], block_ref.at[pl.ds(p * 16, 16)]) for p in range(2)
+    ]
+    copies = bring([(tab_hbm, tab_ref)] + halves + [(tok_hbm, tok_ref)], sems)
     copies[0].wait()
-    tiles = lon_inverse(lambda peers, tile: block_ref[peers, tile], tab_ref, True)
-    copies[1].wait()
+
+    def take(peers, tile):
+        if tile == 0:
+            copies[1 if peers.start == 0 else 2].wait()
+        return block_ref[peers, tile]
+
+    tiles = lon_inverse(take, tab_ref, True)
+    copies[3].wait()
     out_copies = []
     for g in range(CHUNKS):
         own = pl.ds(g * GROUP, GROUP)
@@ -568,15 +605,18 @@
 def per_device(tokens, cotangent, gain, shift, w_in, b_in, w_out, b_out):
     lon_host = lon_table()
     lon_tab, lon_high = jnp.asarray(lon_host), jnp.asarray(lon_host[:, 0])
-    lon_tab = pltpu.with_memory_space_constraint(lon_tab, pltpu.HBM)
     lat_tab, spread = jnp.asarray(lat_table()), jnp.asarray(spread_table())
     tok_val = tokens.astype(f32)
     sums = jnp.stack([jnp.sum(tok_val, axis=0), jnp.sum(tok_val * tok_val, axis=0)])
     terms = group_terms(sums)
-    spec_grad, grad_mark = lon_call(lon_grad_kernel, "lon_grad", 0, 1)(cotangent, lon_tab, sums)
-    spec_field, stats = lon_call(lon_field_kernel, "lon_field", 6, 1)(
-        tokens, lon_tab, jnp.repeat(gain, RW).reshape(TILES, 1, 128),
-        jnp.repeat(shift, RW).reshape(TILES, 1, 128), *terms, grad_mark
+    spec_grad, grad_mark = lon_grad(cotangent, jnp.asarray(grad_table()), sums)
+    spec_field, stats = lon_field(
+        tokens,
+        lon_tab,
+        jnp.repeat(gain, RW).reshape(TILES, 1, 128),
+        jnp.repeat(shift, RW).reshape(TILES, 1, 128),
+        *terms,
+        grad_mark,
     )
 
     modes_field = exchange(spec_field)
@@ -606,11 +646,15 @@
     mixed = inverse_call(
         mixed_kernel,
         "mixed",
-        [VMEM, HBM, HBM, VMEM, VMEM, HBM],
+        [HBM, HBM, HBM, VMEM, VMEM, HBM],
         HBM,
         jax.ShapeDtypeStruct((CH, RW, LON), bf16),
-        [pltpu.SemaphoreType.DMA((2,)), pltpu.SemaphoreType.DMA((CHUNKS,))],
-    )(rows_field, lon_high, tokens, stats, cubes, back)
+        [
+            pltpu.VMEM((PEERS, TILES, 32, 128), f32),
+            pltpu.SemaphoreType.DMA((4,)),
+            pltpu.SemaphoreType.DMA((CHUNKS,)),
+        ],
+    )(in_hbm(rows_field), lon_high, tokens, stats, cubes, back)
     grad_tokens = finish(part, tokens, stats, back_terms)
     return (mixed, grad_tokens, grad_weights)
 

time: 228 us -> 225 us (0.987)
    unnamed x54 -> x52, local copies, waits for them, and re-layouts: 15.5 us -> 14.1 us
where the time goes in v4:
time: 225 us
  blocking collectives  97.1 us (43%)
  Pallas kernels  67.8 us (30%)
  starting transfers between devices  26.4 us (12%)
  waiting for transfers between devices  15.6 us (7%)
  local copies, waits for them, and re-layouts  14.9 us (7%)
    all_to_all x2, blocking collectives, exchange(): return lax.all_to_all(value, 'lat', split_axis=0, concat_axis=0, tiled=True)  97.1 us
    pallas_call x1, Pallas kernels, field_modes(): pl.pallas_call(field_modes_kernel, name='field_modes', grid=(STEPS,), in_...  22.6 us
    pallas_call x1, Pallas kernels, pull_modes(): pl.pallas_call(pull_modes_kernel, name='pull_modes', grid=(STEPS,), in_sp...  17.4 us
    all_to_all x2, starting transfers between devices, exchange(): return lax.all_to_all(value, 'lat', split_axis=0, concat_axis=0, tiled=True)  15.7 us
    all_to_all x2, waiting for transfers between devices, exchange(): return lax.all_to_all(value, 'lat', split_axis=0, concat_axis=0, tiled=True)  15.6 us
    unnamed x52, local copies, waits for them, and re-layouts  14.1 us
    ppermute x6, starting transfers between devices, group_terms(): lax.ppermute(value, 'grp', [(j, j ^ step) for j in range(4)])  10.8 us
    pallas_call x1, Pallas kernels, grad_modes(): pl.pallas_call(grad_modes_kernel, name='grad_modes', grid=(STEPS,), in_sp...  8.3 us
  transfers between devices with their start and end apart: 8, of which 2 were waited for; matrix products, arithmetic and copies ran while one was open for 0% of the time, Pallas kernels for 26%

profile of v4, /device:TPU:1, one launch (start us, length us, event | category | flops | bytes accessed | tf_op | source)
XLA Modules:
  0.0 224.7 jit_solution(14190650705586257425)
XLA Ops:
  0.6 1.9 convert_reduce_fusion
  2.5 4.2 %collective-permute-start.2 = (f32[2,8,1024]{2,1,0:T(8,128)S(1)}, f32[2,8,1024]{2,1,0:T(8,128)S(1)}, u32[]{:S(2)}, u32[]{:S(2)}) collective-permute-start(f32[2,8,1024]{2,1,0:T(8,128)S(1)} %pad_maximum_fusion.sums_ref.one_ref), channel_id=1, source_target_pairs={{0,3},{1,2},{2,1},{3,0},{4,7},{5,6},{6,5},{7,4},{8,11},{9,10},{10,... | collective-permute-start | bytes 196616 | tf_op jit(solution)/shard_map/ppermute | solution.py:601
  6.7 0.1 collective-permute-start.1
  6.9 0.3 collective-permute-start
  7.2 5.4 %lon_grad.1 = (f32[32,6,32,128]{3,2,1,0:T(8,128)}, f32[8,128]{1,0:T(8,128)S(1)}) custom-call(bf16[96,8,1024]{2,1,0:T(8,128)(2,1)} %cot_hbm.1, bf16[2,512,1024]{2,1,0:T(8,128)(2,1)} %constant.16.clone.tab_hbm, f32[2,8,1024]{2,1,0:T(8,128)S(1)} %pad_maximum_fusion.sums_ref.one_ref), custom_call_target="tpu_custom_call" | custom-call | flops 4831838208 | bytes 7340032 | tf_op jit(solution)/shard_map/lon_grad/pallas_call | solution.py:189
  12.9 0.1 broadcast_in_dim.27.shift_ref
  13.3 4.9 %lon_field.1 = (f32[32,6,32,128]{3,2,1,0:T(8,128)S(1)}, f32[2,8,1024]{2,1,0:T(8,128)S(1)}) custom-call(bf16[96,8,1024]{2,1,0:T(8,128)(2,1)S(1)} %copy-done, bf16[2,2,512,512]{3,2,1,0:T(8,128)(2,1)} %constant.12.clone.tab_hbm, f32[6,1,128]{2,1,0:T(1,128)S(1)} %broadcast_in_dim.26.gain_ref, f32[6,1,128]{2,1,0:T(1,128)S(1)} %broadcast_in_dim.27.shift_ref, ...), custom_call_target="tpu_custom_call" | custom-call | flops 4831838208 | bytes 7340032 | tf_op jit(solution)/shard_map/lon_field/pallas_call | solution.py:211
  18.1 46.8 %all_to_all.20.block_ref = f32[32,6,32,128]{3,2,1,0:T(8,128)} all-to-all(f32[32,6,32,128]{3,2,1,0:T(8,128)S(1)} %get-tuple-element.23), channel_id=1, replica_groups=mesh['lat'=32,'grp'=4] {'lat'}, dimensions={0} | all-to-all | bytes 6291456 | tf_op jit(solution)/shard_map/all_to_all | solution.py:596
  65.0 6.5 %all-to-all-start = ((f32[32,6,32,128]{3,2,1,0:T(8,128)}), f32[32,6,32,128]{3,2,1,0:T(8,128)}, u32[]{:S(2)}, u32[]{:S(2)}) async-start(f32[32,6,32,128]{3,2,1,0:T(8,128)} %get-tuple-element.21), calls=%async_computation | async-start | bytes 6291456 | tf_op jit(solution)/shard_map/all_to_all | solution.py:596
  71.6 1.0 copy-done.10
  72.7 22.6 %field_modes.1 = (f32[32,6,32,128]{3,2,1,0:T(8,128)S(1)}, bf16[4096,256]{1,0:T(8,128)(2,1)S(1)}, bf16[4096,256]{1,0:T(8,128)(2,1)S(1)}, bf16[4096,256]{1,0:T(8,1...) custom-call(f32[32,6,32,128]{3,2,1,0:T(8,128)} %all_to_all.20.block_ref, ...), custom_call_target="tpu_custom_call" | custom-call | flops 25769803776 | bytes 14680064 | tf_op jit(solution)/shard_map/field_modes/pallas_call | solution.py:423
  95.3 1.7 copy-done.2
  96.9 1.4 copy-done.14
  98.3 1.3 copy-done.16
  99.6 1.3 copy-done.18
  100.9 1.3 copy-done.20
  102.3 1.3 copy-done.22
  103.6 7.5 %all-to-all-done.block_ref = f32[32,6,32,128]{3,2,1,0:T(8,128)} async-done(((f32[32,6,32,128]{3,2,1,0:T(8,128)}), f32[32,6,32,128]{3,2,1,0:T(8,128)}, u32[]{:S(2)}, u32[]{:S(2)}) %all-to-all-start) | async-done | bytes 3145760 | tf_op jit(solution)/shard_map/all_to_all | solution.py:596
  111.1 9.1 %all-to-all-start.2 = ((f32[32,6,32,128]{3,2,1,0:T(8,128)}), f32[32,6,32,128]{3,2,1,0:T(8,128)}, u32[]{:S(2)}, u32[]{:S(2)}) async-start(f32[32,6,32,128]{3,2,1,0:T(8,128)} %copy-done.2), calls=%async_computation.2 | async-start | bytes 6291456 | tf_op jit(solution)/shard_map/all_to_all | solution.py:596
  120.3 1.0 copy-done.11
  121.3 8.3 %grad_modes.1.grad_ref = f32[4096,256]{1,0:T(8,128)S(1)} custom-call(f32[32,6,32,128]{3,2,1,0:T(8,128)} %all-to-all-done.block_ref, bf16[2,2,256,256]{3,2,1,0:T(8,128)(2,1)S(1)} %copy-done.11, bf16[768,1024]{1,0:T(8,128)(2,1)S(1)} %copy-done.8), custom_call_target="tpu_custom_call" | custom-call | flops 12884901888 | bytes 8388608 | tf_op jit(solution)/shard_map/grad_modes/pallas_call | solution.py:407
  129.6 2.0 copy-done.13
  131.6 0.3 broadcast_in_dim.25.cubes_hbm.cubes_ref
  131.9 17.4 %pull_modes.1 = f32[32,208,128]{2,1,0:T(8,128)S(1)} custom-call(f32[4096,256]{1,0:T(8,128)} %copy-done.13, bf16[4096,256]{1,0:T(8,128)(2,1)S(1)} %copy-done.15, bf16[4096,256]{1,0:T(8,128)(2,1)S(1)} %copy-done.17, bf16[4096,256]{1,0:T(8,128)(2,1)S(1)} %copy-done.19, bf16[4096,256]{1,0:T(8,128)(2,1)S(1)} %copy-done.21, bf16[4096,256]{1,0:T(8,128)(2,1)S(1)} %copy-done.23, ...), custom_call_target="tpu_custom_call" | custom-call | flops 17179869184 | bytes 14680064 | tf_op jit(solution)/shard_map/pull_modes/pallas_call | solution.py:445
  149.4 1.7 copy-done.1
  151.1 8.1 %all-to-all-done.2.block_hbm = f32[32,6,32,128]{3,2,1,0:T(8,128)} async-done(((f32[32,6,32,128]{3,2,1,0:T(8,128)}), f32[32,6,32,128]{3,2,1,0:T(8,128)}, u32[]{:S(2)}, u32[]{:S(2)}) %all-to-all-start.2) | async-done | bytes 3145760 | tf_op jit(solution)/shard_map/all_to_all | solution.py:596
  159.1 50.3 %all_to_all.21.block_ref = f32[32,208,128]{2,1,0:T(8,128)S(1)} all-to-all(f32[32,208,128]{2,1,0:T(8,128)} %copy-done.1), channel_id=1, replica_groups=mesh['lat'=32,'grp'=4] {'lat'}, dimensions={0} | all-to-all | bytes 6815744 | tf_op jit(solution)/shard_map/all_to_all | solution.py:596
  209.4 2.5 %pulled.1 = (f32[96,8,1024]{2,1,0:T(8,128)S(1)}, f32[2,8,1024]{2,1,0:T(8,128)S(1)}, f32[1,1152]{1,0:T(1,128)}) custom-call(f32[32,208,128]{2,1,0:T(8,128)S(1)} %all_to_all.21.block_ref, bf16[2,512,512]{2,1,0:T(8,128)(2,1)S(1)} %copy-done.9, bf16[96,8,1024]{2,1,0:T(8,128)(2,1)S(1)} %copy-done, bf16[96,8,1024]{2,1,0:T(8,128)(2,1)S(1)} %copy-done.3, ...), custom_call_target="tpu_custom_call" | custom-call | flops 3221225472 | bytes 10485760 | tf_op jit(solution)/shard_map/pulled/pallas_call | solution.py:633
  212.0 5.6 %collective-permute-start.5 = (f32[2,8,1024]{2,1,0:T(8,128)S(1)}, f32[2,8,1024]{2,1,0:T(8,128)S(1)}, u32[]{:S(2)}, u32[]{:S(2)}) collective-permute-start(f32[2,8,1024]{2,1,0:T(8,128)S(1)} %get-tuple-element.36.back_hbm.one_ref), channel_id=1, source_target_pairs={{0,3},{1,2},{2,1},{3,0},{4,7},{5,6},{6,5},{7,4},{8,11},{9,10},{10,... | collective-permute-start | bytes 196616 | tf_op jit(solution)/shard_map/ppermute | solution.py:601
  217.6 0.5 collective-permute-start.4
  218.1 4.5 %mixed.1 = bf16[96,8,1024]{2,1,0:T(8,128)(2,1)} custom-call(f32[32,6,32,128]{3,2,1,0:T(8,128)} %all-to-all-done.2.block_hbm, bf16[2,512,512]{2,1,0:T(8,128)(2,1)S(1)} %copy-done.9, bf16[96,8,1024]{2,1,0:T(8,128)(2,1)S(1)} %copy-done, f32[2,8,1024]{2,1,0:T(8,128)S(1)} %get-tuple-element.34.stat_ref, ...), custom_call_target="tpu_custom_call" | custom-call | flops 3221225472 | bytes 10485760 | tf_op jit(solution)/shard_map/mixed/pallas_call | solution.py:646
  222.6 2.1 finish.1
  (56 shorter events, 0.5 us)
Async XLA Ops:
  2.5 10.2 %copy-start.24 = (f32[96]{0:T(128)S(1)}, f32[96]{0:T(128)}, u32[]{:S(2)}) copy-start(f32[96]{0:T(128)} %param.15) | copy-start | bytes 1156
  2.5 10.3 %copy-start.25 = (f32[96]{0:T(128)S(1)}, f32[96]{0:T(128)}, u32[]{:S(2)}) copy-start(f32[96]{0:T(128)} %param.16) | copy-start | bytes 1156
  2.5 10.7 %copy-start = (bf16[96,8,1024]{2,1,0:T(8,128)(2,1)S(1)}, bf16[96,8,1024]{2,1,0:T(8,128)(2,1)}, u32[]{:S(2)}) copy-start(bf16[96,8,1024]{2,1,0:T(8,128)(2,1)} %tok_ref.1) | copy-start | bytes 4718596
  2.5 10.7 %collective-permute-start.2 = (f32[2,8,1024]{2,1,0:T(8,128)S(1)}, f32[2,8,1024]{2,1,0:T(8,128)S(1)}, u32[]{:S(2)}, u32[]{:S(2)}) collective-permute-start(f32[2,8,1024]{2,1,0:T(8,128)S(1)} %pad_maximum_fusion.sums_ref.one_ref), channel_id=1, source_target_pairs={{0,3},{1,2},{2,1},{3,0},{4,7},{5,6},{6,5},{7,4},{8,11},{9,10},{10,... | collective-permute-start | bytes 196616 | tf_op jit(solution)/shard_map/ppermute | solution.py:601
  6.7 6.5 %collective-permute-start.1 = (f32[2,8,1024]{2,1,0:T(8,128)S(1)}, f32[2,8,1024]{2,1,0:T(8,128)S(1)}, u32[]{:S(2)}, u32[]{:S(2)}) collective-permute-start(f32[2,8,1024]{2,1,0:T(8,128)S(1)} %pad_maximum_fusion.sums_ref.one_ref), channel_id=1, source_target_pairs={{0,2},{1,3},{2,0},{3,1},{4,6},{5,7},{6,4},{7,5},{8,10},{9,11},{10,... | collective-permute-start | bytes 196616 | tf_op jit(solution)/shard_map/ppermute | solution.py:601
  6.9 6.4 %collective-permute-start = (f32[2,8,1024]{2,1,0:T(8,128)S(1)}, f32[2,8,1024]{2,1,0:T(8,128)S(1)}, u32[]{:S(2)}, u32[]{:S(2)}) collective-permute-start(f32[2,8,1024]{2,1,0:T(8,128)S(1)} %pad_maximum_fusion.sums_ref.one_ref), channel_id=1, source_target_pairs={{0,1},{1,0},{2,3},{3,2},{4,5},{5,4},{6,7},{7,6},{8,9},{9,8},{10,11... | collective-permute-start | bytes 196616 | tf_op jit(solution)/shard_map/ppermute | solution.py:601
  65.0 6.6 %copy-start.4 = (f32[1,2,96,96]{3,2,1,0:T(8,128)S(1)}, f32[1,2,96,96]{3,2,1,0:T(8,128)}, u32[]{:S(2)}) copy-start(f32[1,2,96,96]{3,2,1,0:T(8,128)} %w_in_ref.3) | copy-start | bytes 221188
  65.0 6.6 %copy-start.5 = (f32[1,2,96,96]{3,2,1,0:T(8,128)S(1)}, f32[1,2,96,96]{3,2,1,0:T(8,128)}, u32[]{:S(2)}) copy-start(f32[1,2,96,96]{3,2,1,0:T(8,128)} %w_out_ref.3) | copy-start | bytes 221188
  65.0 6.6 %copy-start.6 = (f32[1,2,96]{2,1,0:T(2,128)S(1)}, f32[1,2,96]{2,1,0:T(2,128)}, u32[]{:S(2)}) copy-start(f32[1,2,96]{2,1,0:T(2,128)} %b_in_ref.1) | copy-start | bytes 2308
  65.0 6.6 %copy-start.7 = (f32[1,2,96]{2,1,0:T(2,128)S(1)}, f32[1,2,96]{2,1,0:T(2,128)}, u32[]{:S(2)}) copy-start(f32[1,2,96]{2,1,0:T(2,128)} %b_out_ref.1) | copy-start | bytes 2308
  65.0 6.6 %copy-start.8 = (bf16[768,1024]{1,0:T(8,128)(2,1)S(1)}, bf16[768,1024]{1,0:T(8,128)(2,1)}, u32[]{:S(2)}) copy-start(bf16[768,1024]{1,0:T(8,128)(2,1)} %constant.15.clone.spread_ref) | copy-start | bytes 4718596
  65.0 46.1 %all-to-all-start = ((f32[32,6,32,128]{3,2,1,0:T(8,128)}), f32[32,6,32,128]{3,2,1,0:T(8,128)}, u32[]{:S(2)}, u32[]{:S(2)}) async-start(f32[32,6,32,128]{3,2,1,0:T(8,128)} %get-tuple-element.21), calls=%async_computation | async-start | bytes 6291456 | tf_op jit(solution)/shard_map/all_to_all | solution.py:596
  95.3 1.7 copy-start.2
  96.9 1.4 copy-start.14
  98.3 1.3 copy-start.16
  99.6 1.3 copy-start.18
  100.9 1.3 copy-start.20
  102.3 1.3 copy-start.22
  111.1 48.0 %all-to-all-start.2 = ((f32[32,6,32,128]{3,2,1,0:T(8,128)}), f32[32,6,32,128]{3,2,1,0:T(8,128)}, u32[]{:S(2)}, u32[]{:S(2)}) async-start(f32[32,6,32,128]{3,2,1,0:T(8,128)} %copy-done.2), calls=%async_computation.2 | async-start | bytes 6291456 | tf_op jit(solution)/shard_map/all_to_all | solution.py:596
  121.3 10.6 %copy-start.12 = (bf16[2,2,256,256]{3,2,1,0:T(8,128)(2,1)S(1)}, bf16[2,2,256,256]{3,2,1,0:T(8,128)(2,1)}, u32[]{:S(2)}) copy-start(bf16[2,2,256,256]{3,2,1,0:T(8,128)(2,1)} %constant.14.clone.tab_ref) | copy-start | bytes 1572868
  121.3 10.6 %copy-start.15 = (bf16[4096,256]{1,0:T(8,128)(2,1)S(1)}, bf16[4096,256]{1,0:T(8,128)(2,1)}, u32[]{:S(2)}) copy-start(bf16[4096,256]{1,0:T(8,128)(2,1)} %copy-done.14) | copy-start | bytes 6291460
  121.3 10.6 %copy-start.17 = (bf16[4096,256]{1,0:T(8,128)(2,1)S(1)}, bf16[4096,256]{1,0:T(8,128)(2,1)}, u32[]{:S(2)}) copy-start(bf16[4096,256]{1,0:T(8,128)(2,1)} %copy-done.16) | copy-start | bytes 6291460
  121.3 10.6 %copy-start.19 = (bf16[4096,256]{1,0:T(8,128)(2,1)S(1)}, bf16[4096,256]{1,0:T(8,128)(2,1)}, u32[]{:S(2)}) copy-start(bf16[4096,256]{1,0:T(8,128)(2,1)} %copy-done.18) | copy-start | bytes 6291460
  121.3 10.6 %copy-start.21 = (bf16[4096,256]{1,0:T(8,128)(2,1)S(1)}, bf16[4096,256]{1,0:T(8,128)(2,1)}, u32[]{:S(2)}) copy-start(bf16[4096,256]{1,0:T(8,128)(2,1)} %copy-done.20) | copy-start | bytes 6291460
  121.3 10.6 %copy-start.23 = (bf16[4096,256]{1,0:T(8,128)(2,1)S(1)}, bf16[4096,256]{1,0:T(8,128)(2,1)}, u32[]{:S(2)}) copy-start(bf16[4096,256]{1,0:T(8,128)(2,1)} %copy-done.22) | copy-start | bytes 6291460
  129.6 2.0 copy-start.13
  149.4 1.7 copy-start.1
  151.1 58.4 %copy-start.3 = (bf16[96,8,1024]{2,1,0:T(8,128)(2,1)S(1)}, bf16[96,8,1024]{2,1,0:T(8,128)(2,1)}, u32[]{:S(2)}) copy-start(bf16[96,8,1024]{2,1,0:T(8,128)(2,1)} %cot_hbm.1) | copy-start | bytes 4718596
  159.1 50.3 %copy-start.9 = (bf16[2,512,512]{2,1,0:T(8,128)(2,1)S(1)}, bf16[2,512,512]{2,1,0:T(8,128)(2,1)}, u32[]{:S(2)}) copy-start(bf16[2,512,512]{2,1,0:T(8,128)(2,1)} %constant.13.clone.tab_hbm) | copy-start | bytes 3145732
  212.0 10.6 %collective-permute-start.5 = (f32[2,8,1024]{2,1,0:T(8,128)S(1)}, f32[2,8,1024]{2,1,0:T(8,128)S(1)}, u32[]{:S(2)}, u32[]{:S(2)}) collective-permute-start(f32[2,8,1024]{2,1,0:T(8,128)S(1)} %get-tuple-element.36.back_hbm.one_ref), channel_id=1, source_target_pairs={{0,3},{1,2},{2,1},{3,0},{4,7},{5,6},{6,5},{7,4},{8,11},{9,10},{10,... | collective-permute-start | bytes 196616 | tf_op jit(solution)/shard_map/ppermute | solution.py:601
  217.6 5.0 %collective-permute-start.4 = (f32[2,8,1024]{2,1,0:T(8,128)S(1)}, f32[2,8,1024]{2,1,0:T(8,128)S(1)}, u32[]{:S(2)}, u32[]{:S(2)}) collective-permute-start(f32[2,8,1024]{2,1,0:T(8,128)S(1)} %get-tuple-element.36.back_hbm.one_ref), channel_id=1, source_target_pairs={{0,2},{1,3},{2,0},{3,1},{4,6},{5,7},{6,4},{7,5},{8,10},{9,11},{10,... | collective-permute-start | bytes 196616 | tf_op jit(solution)/shard_map/ppermute | solution.py:601
  218.1 4.5 %collective-permute-start.3 = (f32[2,8,1024]{2,1,0:T(8,128)S(1)}, f32[2,8,1024]{2,1,0:T(8,128)S(1)}, u32[]{:S(2)}, u32[]{:S(2)}) collective-permute-start(f32[2,8,1024]{2,1,0:T(8,128)S(1)} %get-tuple-element.36.back_hbm.one_ref), channel_id=1, source_target_pairs={{0,1},{1,0},{2,3},{3,2},{4,5},{5,4},{6,7},{7,6},{8,9},{9,8},{10,11... | collective-permute-start | bytes 196616 | tf_op jit(solution)/shard_map/ppermute | solution.py:601
  (2 other events, 2.1 us)

commit v5 on v4

--- a/solution.py
+++ b/solution.py
@@ -483,23 +483,21 @@
 
 
 def mixed_kernel(
-    block_hbm, tab_hbm, tok_hbm, stat_ref, cubes_ref, back_hbm,
+    block_hbm, tab_ref, tok_ref, stat_ref, cubes_ref, back_hbm,
     out_hbm,
-    tab_ref, tok_ref, mix_ref, block_ref, sems, out_sems,
+    mix_ref, block_ref, sems, out_sems,
 ):
     halves = [
         (block_hbm.at[pl.ds(p * 16, 16)], block_ref.at[pl.ds(p * 16, 16)]) for p in range(2)
     ]
-    copies = bring([(tab_hbm, tab_ref)] + halves + [(tok_hbm, tok_ref)], sems)
-    copies[0].wait()
+    copies = bring(halves, sems)
 
     def take(peers, tile):
         if tile == 0:
-            copies[1 if peers.start == 0 else 2].wait()
+            copies[0 if peers.start == 0 else 1].wait()
         return block_ref[peers, tile]
 
     tiles = lon_inverse(take, tab_ref, True)
-    copies[3].wait()
     out_copies = []
     for g in range(CHUNKS):
         own = pl.ds(g * GROUP, GROUP)
@@ -518,22 +516,16 @@
 
 
 def pulled_kernel(
-    block_ref, tab_hbm, tok_hbm, cot_hbm, stat_ref, cubes_ref,
+    block_ref, tab_ref, tok_ref, cot_ref, stat_ref, cubes_ref,
     out_ref, sum_ref, weight_ref,
-    tab_ref, tok_ref, cot_ref, sems,
 ):
-    copies = bring(((tab_hbm, tab_ref), (tok_hbm, tok_ref), (cot_hbm, cot_ref)), sems)
-
     def take(peers, tile):
         return block_ref[peers, tile * 32 : tile * 32 + 32, :]
 
-    copies[0].wait()
     tiles = lon_inverse(take, tab_ref, False)
     share = jnp.sum(block_ref[:, PULL_ROWS - 16 :, :], axis=0)
     for i in range(12):
         weight_ref[0:1, i * CH : i * CH + CH] = share[i : i + 1, 0:CH]
-    copies[1].wait()
-    copies[2].wait()
     for tile in range(8):
         lanes = slice(tile * 128, tile * 128 + 128)
         tok = tok_ref[:, :, lanes].astype(f32)
@@ -554,12 +546,7 @@
         in_specs=in_specs,
         out_specs=out_specs,
         out_shape=out_shape,
-        scratch_shapes=[
-            pltpu.VMEM((2, HALF, HALF), bf16),
-            pltpu.VMEM((CH, RW, LON), bf16),
-            pltpu.VMEM((CH, RW, LON), bf16),
-        ]
-        + scratch,
+        scratch_shapes=scratch,
         compiler_params=pltpu.CompilerParams(vmem_limit_bytes=28 * 2**20),
         cost_estimate=pl.CostEstimate(
             flops=4 * LANES * LON * LON, bytes_accessed=10 * 2**20, transcendentals=0
@@ -567,25 +554,38 @@
     )
 
 
-def finish_kernel(part_ref, tok_ref, stat_ref, one_ref, two_ref, three_ref, four_ref, out_ref):
+def finish_kernel(
+    part_ref, tok_ref, stat_ref, one_ref, two_ref, three_ref, four_ref,
+    out_hbm,
+    own_ref, sems,
+):
     terms = (one_ref, two_ref, three_ref, four_ref)
     count = 4.0 * CH
     mean, inv_std = stat_ref[0], stat_ref[1]
-    one, two = total(terms, 0) / count, total(terms, 1) / count
-    normed = (tok_ref[...].astype(f32) - mean[None]) * inv_std[None]
-    out_ref[...] = (part_ref[...] - (inv_std * one)[None] - normed * (inv_std * two)[None]).astype(bf16)
+    one, two = inv_std * total(terms, 0) / count, inv_std * total(terms, 1) / count
+    scale = inv_std * two
+    level = one - mean * scale
+    copies = []
+    for g in range(CHUNKS):
+        own = pl.ds(g * GROUP, GROUP)
+        value = part_ref[own] - level[None] - tok_ref[own].astype(f32) * scale[None]
+        own_ref[own] = value.astype(bf16)
+        copy = pltpu.make_async_copy(own_ref.at[own], out_hbm.at[own], sems.at[g])
+        copy.start()
+        copies.append(copy)
+    for copy in copies:
+        copy.wait()
 
 
 def finish(part, tokens, stats, terms):
-    block = pl.BlockSpec((CH // 4, RW, LON), lambda i: (i, 0, 0))
     return pl.pallas_call(
         finish_kernel,
         name="finish",
-        grid=(4,),
-        in_specs=[block, block] + [pl.BlockSpec((2, RW, LON), lambda i: (0, 0, 0))] * 5,
-        out_specs=block,
+        in_specs=[VMEM] * 7,
+        out_specs=HBM,
         out_shape=jax.ShapeDtypeStruct((CH, RW, LON), bf16),
-        compiler_params=pltpu.CompilerParams(vmem_limit_bytes=24 * 2**20),
+        scratch_shapes=[pltpu.VMEM((CH, RW, LON), bf16), pltpu.SemaphoreType.DMA((CHUNKS,))],
+        compiler_params=pltpu.CompilerParams(vmem_limit_bytes=20 * 2**20),
         cost_estimate=pl.CostEstimate(
             flops=8 * CH * RW * LON, bytes_accessed=6 * 2**20, transcendentals=0
         ),
@@ -633,25 +633,26 @@
     part, back, grad_weights = inverse_call(
         pulled_kernel,
         "pulled",
-        [VMEM, HBM, HBM, HBM, VMEM, VMEM],
+        [VMEM] * 6,
         [VMEM] * 3,
         [
             jax.ShapeDtypeStruct((CH, RW, LON), f32),
             STATS_SHAPE,
             jax.ShapeDtypeStruct((1, 1152), f32),
         ],
-        [pltpu.SemaphoreType.DMA((3,))],
+        [],
     )(rows_grad, lon_high, tokens, cotangent, stats, cubes)
     back_terms = group_terms(back)
     mixed = inverse_call(
         mixed_kernel,
         "mixed",
-        [HBM, HBM, HBM, VMEM, VMEM, HBM],
+        [HBM, VMEM, VMEM, VMEM, VMEM, HBM],
         HBM,
         jax.ShapeDtypeStruct((CH, RW, LON), bf16),
         [
+            pltpu.VMEM((CH, RW, LON), bf16),
             pltpu.VMEM((PEERS, TILES, 32, 128), f32),
-            pltpu.SemaphoreType.DMA((4,)),
+            pltpu.SemaphoreType.DMA((2,)),
             pltpu.SemaphoreType.DMA((CHUNKS,)),
         ],
     )(in_hbm(rows_field), lon_high, tokens, stats, cubes, back)

time: 225 us -> 224 us (level)
  no operation moved by 1% of the time
where the time goes in v5:
time: 224 us
  blocking collectives  97.1 us (43%)
  Pallas kernels  66.7 us (30%)
  starting transfers between devices  26.4 us (12%)
  waiting for transfers between devices  15.6 us (7%)
  local copies, waits for them, and re-layouts  14.9 us (7%)
    all_to_all x2, blocking collectives, exchange(): return lax.all_to_all(value, 'lat', split_axis=0, concat_axis=0, tiled=True)  97.1 us
    pallas_call x1, Pallas kernels, field_modes(): pl.pallas_call(field_modes_kernel, name='field_modes', grid=(STEPS,), in_...  22.6 us
    pallas_call x1, Pallas kernels, pull_modes(): pl.pallas_call(pull_modes_kernel, name='pull_modes', grid=(STEPS,), in_sp...  17.4 us
    all_to_all x2, starting transfers between devices, exchange(): return lax.all_to_all(value, 'lat', split_axis=0, concat_axis=0, tiled=True)  15.7 us
    all_to_all x2, waiting for transfers between devices, exchange(): return lax.all_to_all(value, 'lat', split_axis=0, concat_axis=0, tiled=True)  15.6 us
    unnamed x52, local copies, waits for them, and re-layouts  14.1 us
    ppermute x6, starting transfers between devices, group_terms(): lax.ppermute(value, 'grp', [(j, j ^ step) for j in range(4)])  10.7 us
    pallas_call x1, Pallas kernels, grad_modes(): pl.pallas_call(grad_modes_kernel, name='grad_modes', grid=(STEPS,), in_sp...  8.3 us
  transfers between devices with their start and end apart: 8, of which 2 were waited for; matrix products, arithmetic and copies ran while one was open for 0% of the time, Pallas kernels for 26%

profile of v5, /device:TPU:1, one launch (start us, length us, event | category | flops | bytes accessed | tf_op | source)
XLA Modules:
  0.0 223.7 jit_solution(9144600464356404737)
XLA Ops:
  0.6 1.9 convert_reduce_fusion
  2.5 4.2 %collective-permute-start.2 = (f32[2,8,1024]{2,1,0:T(8,128)S(1)}, f32[2,8,1024]{2,1,0:T(8,128)S(1)}, u32[]{:S(2)}, u32[]{:S(2)}) collective-permute-start(f32[2,8,1024]{2,1,0:T(8,128)S(1)} %pad_maximum_fusion.sums_ref.one_ref), channel_id=1, source_target_pairs={{0,3},{1,2},{2,1},{3,0},{4,7},{5,6},{6,5},{7,4},{8,11},{9,10},{10,... | collective-permute-start | bytes 196616 | tf_op jit(solution)/shard_map/ppermute | solution.py:601
  6.7 0.1 collective-permute-start.1
  6.9 0.3 collective-permute-start
  7.2 5.4 %lon_grad.1 = (f32[32,6,32,128]{3,2,1,0:T(8,128)}, f32[8,128]{1,0:T(8,128)S(1)}) custom-call(bf16[96,8,1024]{2,1,0:T(8,128)(2,1)} %cot_ref.1, bf16[2,512,1024]{2,1,0:T(8,128)(2,1)} %constant.16.clone.tab_hbm, f32[2,8,1024]{2,1,0:T(8,128)S(1)} %pad_maximum_fusion.sums_ref.one_ref), custom_call_target="tpu_custom_call" | custom-call | flops 4831838208 | bytes 7340032 | tf_op jit(solution)/shard_map/lon_grad/pallas_call | solution.py:189
  12.9 0.1 broadcast_in_dim.27.shift_ref
  13.3 4.9 %lon_field.1 = (f32[32,6,32,128]{3,2,1,0:T(8,128)S(1)}, f32[2,8,1024]{2,1,0:T(8,128)S(1)}) custom-call(bf16[96,8,1024]{2,1,0:T(8,128)(2,1)S(1)} %copy-done, bf16[2,2,512,512]{3,2,1,0:T(8,128)(2,1)} %constant.12.clone.tab_hbm, f32[6,1,128]{2,1,0:T(1,128)S(1)} %broadcast_in_dim.26.gain_ref, f32[6,1,128]{2,1,0:T(1,128)S(1)} %broadcast_in_dim.27.shift_ref, ...), custom_call_target="tpu_custom_call" | custom-call | flops 4831838208 | bytes 7340032 | tf_op jit(solution)/shard_map/lon_field/pallas_call | solution.py:211
  18.1 46.8 %all_to_all.20.block_ref = f32[32,6,32,128]{3,2,1,0:T(8,128)} all-to-all(f32[32,6,32,128]{3,2,1,0:T(8,128)S(1)} %get-tuple-element.23), channel_id=1, replica_groups=mesh['lat'=32,'grp'=4] {'lat'}, dimensions={0} | all-to-all | bytes 6291456 | tf_op jit(solution)/shard_map/all_to_all | solution.py:596
  65.0 6.5 %all-to-all-start = ((f32[32,6,32,128]{3,2,1,0:T(8,128)}), f32[32,6,32,128]{3,2,1,0:T(8,128)}, u32[]{:S(2)}, u32[]{:S(2)}) async-start(f32[32,6,32,128]{3,2,1,0:T(8,128)} %get-tuple-element.21), calls=%async_computation | async-start | bytes 6291456 | tf_op jit(solution)/shard_map/all_to_all | solution.py:596
  71.6 1.0 copy-done.10
  72.7 22.6 %field_modes.1 = (f32[32,6,32,128]{3,2,1,0:T(8,128)S(1)}, bf16[4096,256]{1,0:T(8,128)(2,1)S(1)}, bf16[4096,256]{1,0:T(8,128)(2,1)S(1)}, bf16[4096,256]{1,0:T(8,1...) custom-call(f32[32,6,32,128]{3,2,1,0:T(8,128)} %all_to_all.20.block_ref, ...), custom_call_target="tpu_custom_call" | custom-call | flops 25769803776 | bytes 14680064 | tf_op jit(solution)/shard_map/field_modes/pallas_call | solution.py:423
  95.3 1.7 copy-done.2
  96.9 1.4 copy-done.14
  98.3 1.3 copy-done.16
  99.6 1.3 copy-done.18
  100.9 1.3 copy-done.20
  102.3 1.3 copy-done.22
  103.6 7.5 %all-to-all-done.block_ref = f32[32,6,32,128]{3,2,1,0:T(8,128)} async-done(((f32[32,6,32,128]{3,2,1,0:T(8,128)}), f32[32,6,32,128]{3,2,1,0:T(8,128)}, u32[]{:S(2)}, u32[]{:S(2)}) %all-to-all-start) | async-done | bytes 3145760 | tf_op jit(solution)/shard_map/all_to_all | solution.py:596
  111.1 9.1 %all-to-all-start.2 = ((f32[32,6,32,128]{3,2,1,0:T(8,128)}), f32[32,6,32,128]{3,2,1,0:T(8,128)}, u32[]{:S(2)}, u32[]{:S(2)}) async-start(f32[32,6,32,128]{3,2,1,0:T(8,128)} %copy-done.2), calls=%async_computation.2 | async-start | bytes 6291456 | tf_op jit(solution)/shard_map/all_to_all | solution.py:596
  120.3 1.0 copy-done.11
  121.3 8.3 %grad_modes.1.grad_ref = f32[4096,256]{1,0:T(8,128)S(1)} custom-call(f32[32,6,32,128]{3,2,1,0:T(8,128)} %all-to-all-done.block_ref, bf16[2,2,256,256]{3,2,1,0:T(8,128)(2,1)S(1)} %copy-done.11, bf16[768,1024]{1,0:T(8,128)(2,1)S(1)} %copy-done.8), custom_call_target="tpu_custom_call" | custom-call | flops 12884901888 | bytes 8388608 | tf_op jit(solution)/shard_map/grad_modes/pallas_call | solution.py:407
  129.6 2.0 copy-done.13
  131.6 0.3 broadcast_in_dim.25.cubes_hbm.cubes_ref
  131.9 17.4 %pull_modes.1 = f32[32,208,128]{2,1,0:T(8,128)S(1)} custom-call(f32[4096,256]{1,0:T(8,128)} %copy-done.13, bf16[4096,256]{1,0:T(8,128)(2,1)S(1)} %copy-done.15, bf16[4096,256]{1,0:T(8,128)(2,1)S(1)} %copy-done.17, bf16[4096,256]{1,0:T(8,128)(2,1)S(1)} %copy-done.19, bf16[4096,256]{1,0:T(8,128)(2,1)S(1)} %copy-done.21, bf16[4096,256]{1,0:T(8,128)(2,1)S(1)} %copy-done.23, ...), custom_call_target="tpu_custom_call" | custom-call | flops 17179869184 | bytes 14680064 | tf_op jit(solution)/shard_map/pull_modes/pallas_call | solution.py:445
  149.4 1.7 copy-done.1
  151.1 8.1 %all-to-all-done.2.block_hbm = f32[32,6,32,128]{3,2,1,0:T(8,128)} async-done(((f32[32,6,32,128]{3,2,1,0:T(8,128)}), f32[32,6,32,128]{3,2,1,0:T(8,128)}, u32[]{:S(2)}, u32[]{:S(2)}) %all-to-all-start.2) | async-done | bytes 3145760 | tf_op jit(solution)/shard_map/all_to_all | solution.py:596
  159.1 50.3 %all_to_all.21.block_ref = f32[32,208,128]{2,1,0:T(8,128)S(1)} all-to-all(f32[32,208,128]{2,1,0:T(8,128)} %copy-done.1), channel_id=1, replica_groups=mesh['lat'=32,'grp'=4] {'lat'}, dimensions={0} | all-to-all | bytes 6815744 | tf_op jit(solution)/shard_map/all_to_all | solution.py:596
  209.4 2.6 %pulled.1 = (f32[96,8,1024]{2,1,0:T(8,128)S(1)}, f32[2,8,1024]{2,1,0:T(8,128)S(1)}, f32[1,1152]{1,0:T(1,128)}) custom-call(f32[32,208,128]{2,1,0:T(8,128)S(1)} %all_to_all.21.block_ref, bf16[2,512,512]{2,1,0:T(8,128)(2,1)S(1)} %copy-done.9, bf16[96,8,1024]{2,1,0:T(8,128)(2,1)S(1)} %copy-done, bf16[96,8,1024]{2,1,0:T(8,128)(2,1)S(1)} %copy-done.3, ...), custom_call_target="tpu_custom_call" | custom-call | flops 3221225472 | bytes 10485760 | tf_op jit(solution)/shard_map/pulled/pallas_call | solution.py:633
  212.1 5.5 %collective-permute-start.5 = (f32[2,8,1024]{2,1,0:T(8,128)S(1)}, f32[2,8,1024]{2,1,0:T(8,128)S(1)}, u32[]{:S(2)}, u32[]{:S(2)}) collective-permute-start(f32[2,8,1024]{2,1,0:T(8,128)S(1)} %get-tuple-element.36.back_hbm.one_ref), channel_id=1, source_target_pairs={{0,3},{1,2},{2,1},{3,0},{4,7},{5,6},{6,5},{7,4},{8,11},{9,10},{10,... | collective-permute-start | bytes 196616 | tf_op jit(solution)/shard_map/ppermute | solution.py:601
  217.6 0.5 collective-permute-start.4
  218.1 4.1 %mixed.1 = bf16[96,8,1024]{2,1,0:T(8,128)(2,1)} custom-call(f32[32,6,32,128]{3,2,1,0:T(8,128)} %all-to-all-done.2.block_hbm, bf16[2,512,512]{2,1,0:T(8,128)(2,1)S(1)} %copy-done.9, bf16[96,8,1024]{2,1,0:T(8,128)(2,1)S(1)} %copy-done, f32[2,8,1024]{2,1,0:T(8,128)S(1)} %get-tuple-element.34.stat_ref, ...), custom_call_target="tpu_custom_call" | custom-call | flops 3221225472 | bytes 10485760 | tf_op jit(solution)/shard_map/mixed/pallas_call | solution.py:646
  222.2 1.3 finish.1
  (56 shorter events, 0.5 us)
Async XLA Ops:
  2.5 10.2 %copy-start.24 = (f32[96]{0:T(128)S(1)}, f32[96]{0:T(128)}, u32[]{:S(2)}) copy-start(f32[96]{0:T(128)} %param.15) | copy-start | bytes 1156
  2.5 10.3 %copy-start.25 = (f32[96]{0:T(128)S(1)}, f32[96]{0:T(128)}, u32[]{:S(2)}) copy-start(f32[96]{0:T(128)} %param.16) | copy-start | bytes 1156
  2.5 10.7 %copy-start = (bf16[96,8,1024]{2,1,0:T(8,128)(2,1)S(1)}, bf16[96,8,1024]{2,1,0:T(8,128)(2,1)}, u32[]{:S(2)}) copy-start(bf16[96,8,1024]{2,1,0:T(8,128)(2,1)} %tok_ref.5) | copy-start | bytes 4718596
  2.5 10.7 %collective-permute-start.2 = (f32[2,8,1024]{2,1,0:T(8,128)S(1)}, f32[2,8,1024]{2,1,0:T(8,128)S(1)}, u32[]{:S(2)}, u32[]{:S(2)}) collective-permute-start(f32[2,8,1024]{2,1,0:T(8,128)S(1)} %pad_maximum_fusion.sums_ref.one_ref), channel_id=1, source_target_pairs={{0,3},{1,2},{2,1},{3,0},{4,7},{5,6},{6,5},{7,4},{8,11},{9,10},{10,... | collective-permute-start | bytes 196616 | tf_op jit(solution)/shard_map/ppermute | solution.py:601
  6.7 6.5 %collective-permute-start.1 = (f32[2,8,1024]{2,1,0:T(8,128)S(1)}, f32[2,8,1024]{2,1,0:T(8,128)S(1)}, u32[]{:S(2)}, u32[]{:S(2)}) collective-permute-start(f32[2,8,1024]{2,1,0:T(8,128)S(1)} %pad_maximum_fusion.sums_ref.one_ref), channel_id=1, source_target_pairs={{0,2},{1,3},{2,0},{3,1},{4,6},{5,7},{6,4},{7,5},{8,10},{9,11},{10,... | collective-permute-start | bytes 196616 | tf_op jit(solution)/shard_map/ppermute | solution.py:601
  6.9 6.4 %collective-permute-start = (f32[2,8,1024]{2,1,0:T(8,128)S(1)}, f32[2,8,1024]{2,1,0:T(8,128)S(1)}, u32[]{:S(2)}, u32[]{:S(2)}) collective-permute-start(f32[2,8,1024]{2,1,0:T(8,128)S(1)} %pad_maximum_fusion.sums_ref.one_ref), channel_id=1, source_target_pairs={{0,1},{1,0},{2,3},{3,2},{4,5},{5,4},{6,7},{7,6},{8,9},{9,8},{10,11... | collective-permute-start | bytes 196616 | tf_op jit(solution)/shard_map/ppermute | solution.py:601
  65.0 6.6 %copy-start.4 = (f32[1,2,96,96]{3,2,1,0:T(8,128)S(1)}, f32[1,2,96,96]{3,2,1,0:T(8,128)}, u32[]{:S(2)}) copy-start(f32[1,2,96,96]{3,2,1,0:T(8,128)} %w_in_ref.3) | copy-start | bytes 221188
  65.0 6.6 %copy-start.5 = (f32[1,2,96,96]{3,2,1,0:T(8,128)S(1)}, f32[1,2,96,96]{3,2,1,0:T(8,128)}, u32[]{:S(2)}) copy-start(f32[1,2,96,96]{3,2,1,0:T(8,128)} %w_out_ref.3) | copy-start | bytes 221188
  65.0 6.6 %copy-start.6 = (f32[1,2,96]{2,1,0:T(2,128)S(1)}, f32[1,2,96]{2,1,0:T(2,128)}, u32[]{:S(2)}) copy-start(f32[1,2,96]{2,1,0:T(2,128)} %b_in_ref.1) | copy-start | bytes 2308
  65.0 6.6 %copy-start.7 = (f32[1,2,96]{2,1,0:T(2,128)S(1)}, f32[1,2,96]{2,1,0:T(2,128)}, u32[]{:S(2)}) copy-start(f32[1,2,96]{2,1,0:T(2,128)} %b_out_ref.1) | copy-start | bytes 2308
  65.0 6.6 %copy-start.8 = (bf16[768,1024]{1,0:T(8,128)(2,1)S(1)}, bf16[768,1024]{1,0:T(8,128)(2,1)}, u32[]{:S(2)}) copy-start(bf16[768,1024]{1,0:T(8,128)(2,1)} %constant.15.clone.spread_ref) | copy-start | bytes 4718596
  65.0 46.1 %all-to-all-start = ((f32[32,6,32,128]{3,2,1,0:T(8,128)}), f32[32,6,32,128]{3,2,1,0:T(8,128)}, u32[]{:S(2)}, u32[]{:S(2)}) async-start(f32[32,6,32,128]{3,2,1,0:T(8,128)} %get-tuple-element.21), calls=%async_computation | async-start | bytes 6291456 | tf_op jit(solution)/shard_map/all_to_all | solution.py:596
  95.3 1.7 copy-start.2
  96.9 1.4 copy-start.14
  98.3 1.3 copy-start.16
  99.6 1.3 copy-start.18
  100.9 1.3 copy-start.20
  102.3 1.3 copy-start.22
  111.1 48.0 %all-to-all-start.2 = ((f32[32,6,32,128]{3,2,1,0:T(8,128)}), f32[32,6,32,128]{3,2,1,0:T(8,128)}, u32[]{:S(2)}, u32[]{:S(2)}) async-start(f32[32,6,32,128]{3,2,1,0:T(8,128)} %copy-done.2), calls=%async_computation.2 | async-start | bytes 6291456 | tf_op jit(solution)/shard_map/all_to_all | solution.py:596
  121.3 10.6 %copy-start.12 = (bf16[2,2,256,256]{3,2,1,0:T(8,128)(2,1)S(1)}, bf16[2,2,256,256]{3,2,1,0:T(8,128)(2,1)}, u32[]{:S(2)}) copy-start(bf16[2,2,256,256]{3,2,1,0:T(8,128)(2,1)} %constant.14.clone.tab_ref) | copy-start | bytes 1572868
  121.3 10.6 %copy-start.15 = (bf16[4096,256]{1,0:T(8,128)(2,1)S(1)}, bf16[4096,256]{1,0:T(8,128)(2,1)}, u32[]{:S(2)}) copy-start(bf16[4096,256]{1,0:T(8,128)(2,1)} %copy-done.14) | copy-start | bytes 6291460
  121.3 10.6 %copy-start.17 = (bf16[4096,256]{1,0:T(8,128)(2,1)S(1)}, bf16[4096,256]{1,0:T(8,128)(2,1)}, u32[]{:S(2)}) copy-start(bf16[4096,256]{1,0:T(8,128)(2,1)} %copy-done.16) | copy-start | bytes 6291460
  121.3 10.6 %copy-start.19 = (bf16[4096,256]{1,0:T(8,128)(2,1)S(1)}, bf16[4096,256]{1,0:T(8,128)(2,1)}, u32[]{:S(2)}) copy-start(bf16[4096,256]{1,0:T(8,128)(2,1)} %copy-done.18) | copy-start | bytes 6291460
  121.3 10.6 %copy-start.21 = (bf16[4096,256]{1,0:T(8,128)(2,1)S(1)}, bf16[4096,256]{1,0:T(8,128)(2,1)}, u32[]{:S(2)}) copy-start(bf16[4096,256]{1,0:T(8,128)(2,1)} %copy-done.20) | copy-start | bytes 6291460
  121.3 10.6 %copy-start.23 = (bf16[4096,256]{1,0:T(8,128)(2,1)S(1)}, bf16[4096,256]{1,0:T(8,128)(2,1)}, u32[]{:S(2)}) copy-start(bf16[4096,256]{1,0:T(8,128)(2,1)} %copy-done.22) | copy-start | bytes 6291460
  129.6 2.0 copy-start.13
  149.4 1.7 copy-start.1
  151.1 58.4 %copy-start.3 = (bf16[96,8,1024]{2,1,0:T(8,128)(2,1)S(1)}, bf16[96,8,1024]{2,1,0:T(8,128)(2,1)}, u32[]{:S(2)}) copy-start(bf16[96,8,1024]{2,1,0:T(8,128)(2,1)} %cot_ref.1) | copy-start | bytes 4718596
  159.1 50.3 %copy-start.9 = (bf16[2,512,512]{2,1,0:T(8,128)(2,1)S(1)}, bf16[2,512,512]{2,1,0:T(8,128)(2,1)}, u32[]{:S(2)}) copy-start(bf16[2,512,512]{2,1,0:T(8,128)(2,1)} %constant.13.clone.tab_ref) | copy-start | bytes 3145732
  212.1 10.1 %collective-permute-start.5 = (f32[2,8,1024]{2,1,0:T(8,128)S(1)}, f32[2,8,1024]{2,1,0:T(8,128)S(1)}, u32[]{:S(2)}, u32[]{:S(2)}) collective-permute-start(f32[2,8,1024]{2,1,0:T(8,128)S(1)} %get-tuple-element.36.back_hbm.one_ref), channel_id=1, source_target_pairs={{0,3},{1,2},{2,1},{3,0},{4,7},{5,6},{6,5},{7,4},{8,11},{9,10},{10,... | collective-permute-start | bytes 196616 | tf_op jit(solution)/shard_map/ppermute | solution.py:601
  217.6 4.6 %collective-permute-start.4 = (f32[2,8,1024]{2,1,0:T(8,128)S(1)}, f32[2,8,1024]{2,1,0:T(8,128)S(1)}, u32[]{:S(2)}, u32[]{:S(2)}) collective-permute-start(f32[2,8,1024]{2,1,0:T(8,128)S(1)} %get-tuple-element.36.back_hbm.one_ref), channel_id=1, source_target_pairs={{0,2},{1,3},{2,0},{3,1},{4,6},{5,7},{6,4},{7,5},{8,10},{9,11},{10,... | collective-permute-start | bytes 196616 | tf_op jit(solution)/shard_map/ppermute | solution.py:601
  218.1 4.1 %collective-permute-start.3 = (f32[2,8,1024]{2,1,0:T(8,128)S(1)}, f32[2,8,1024]{2,1,0:T(8,128)S(1)}, u32[]{:S(2)}, u32[]{:S(2)}) collective-permute-start(f32[2,8,1024]{2,1,0:T(8,128)S(1)} %get-tuple-element.36.back_hbm.one_ref), channel_id=1, source_target_pairs={{0,1},{1,0},{2,3},{3,2},{4,5},{5,4},{6,7},{7,6},{8,9},{9,8},{10,11... | collective-permute-start | bytes 196616 | tf_op jit(solution)/shard_map/ppermute | solution.py:601
  (2 other events, 2.1 us)

commit v6 on v5

--- a/solution.py
+++ b/solution.py
@@ -113,6 +113,19 @@
     for copy in copies:
         copy.start()
     return copies
+
+
+def sums_kernel(x_hbm, out_ref, x_ref, sems):
+    parts = [pl.ds(g * GROUP, GROUP) for g in range(CHUNKS)]
+    copies = bring([(x_hbm.at[own], x_ref.at[own]) for own in parts], sems)
+    for g, own in enumerate(parts):
+        copies[g].wait()
+        for tile in range(8):
+            lanes = slice(tile * 128, tile * 128 + 128)
+            value = x_ref[own, :, lanes].astype(f32)
+            for at, term in enumerate((value, value * value)):
+                term = jnp.sum(term, axis=0)
+                out_ref[at, :, lanes] = term if g == 0 else out_ref[at, :, lanes] + term
 
 
 def lon_grad_kernel(
@@ -185,6 +198,21 @@
 )
 
 
+def token_sums(tokens):
+    return pl.pallas_call(
+        sums_kernel,
+        name="token_sums",
+        in_specs=[HBM],
+        out_specs=VMEM,
+        out_shape=STATS_SHAPE,
+        scratch_shapes=[pltpu.VMEM((CH, RW, LON), bf16), pltpu.SemaphoreType.DMA((CHUNKS,))],
+        compiler_params=pltpu.CompilerParams(vmem_limit_bytes=16 * 2**20),
+        cost_estimate=pl.CostEstimate(
+            flops=3 * CH * RW * LON, bytes_accessed=2 * CH * RW * LON, transcendentals=0
+        ),
+    )(in_hbm(tokens))
+
+
 def lon_grad(cotangent, table, sums):
     return pl.pallas_call(
         lon_grad_kernel,
@@ -606,8 +634,7 @@
     lon_host = lon_table()
     lon_tab, lon_high = jnp.asarray(lon_host), jnp.asarray(lon_host[:, 0])
     lat_tab, spread = jnp.asarray(lat_table()), jnp.asarray(spread_table())
-    tok_val = tokens.astype(f32)
-    sums = jnp.stack([jnp.sum(tok_val, axis=0), jnp.sum(tok_val * tok_val, axis=0)])
+    sums = token_sums(tokens)
     terms = group_terms(sums)
     spec_grad, grad_mark = lon_grad(cotangent, jnp.asarray(grad_table()), sums)
     spec_field, stats = lon_field(

time: 224 us -> 224 us (level)
  no operation moved by 1% of the time
where the time goes in v6:
time: 224 us; the launch traced here: 223 us
  blocking collectives  97.1 us (43%)
  Pallas kernels  68.2 us (30%)
  starting transfers between devices  26.4 us (12%)
  waiting for transfers between devices  15.6 us (7%)
  local copies, waits for them, and re-layouts  14.9 us (7%)
    all_to_all x2, blocking collectives, exchange(): return lax.all_to_all(value, 'lat', split_axis=0, concat_axis=0, tiled=True)  97.1 us
    pallas_call x1, Pallas kernels, field_modes(): pl.pallas_call(field_modes_kernel, name='field_modes', grid=(STEPS,), in_...  22.6 us
    pallas_call x1, Pallas kernels, pull_modes(): pl.pallas_call(pull_modes_kernel, name='pull_modes', grid=(STEPS,), in_sp...  17.4 us
    all_to_all x2, starting transfers between devices, exchange(): return lax.all_to_all(value, 'lat', split_axis=0, concat_axis=0, tiled=True)  15.7 us
    all_to_all x2, waiting for transfers between devices, exchange(): return lax.all_to_all(value, 'lat', split_axis=0, concat_axis=0, tiled=True)  15.6 us
    unnamed x52, local copies, waits for them, and re-layouts  14.1 us
    ppermute x6, starting transfers between devices, group_terms(): lax.ppermute(value, 'grp', [(j, j ^ step) for j in range(4)])  10.7 us
    pallas_call x1, Pallas kernels, grad_modes(): pl.pallas_call(grad_modes_kernel, name='grad_modes', grid=(STEPS,), in_sp...  8.3 us
  transfers between devices with their start and end apart: 8, of which 2 were waited for; matrix products, arithmetic and copies ran while one was open for 0% of the time, Pallas kernels for 26%

profile of v6, /device:TPU:1, one launch (start us, length us, event | category | flops | bytes accessed | tf_op | source)
XLA Modules:
  0.0 223.3 jit_solution(6808409869610155013)
XLA Ops:
  0.6 1.5 token_sums.1.sums_ref.one_ref
  2.2 4.2 %collective-permute-start.2 = (f32[2,8,1024]{2,1,0:T(8,128)S(1)}, f32[2,8,1024]{2,1,0:T(8,128)S(1)}, u32[]{:S(2)}, u32[]{:S(2)}) collective-permute-start(f32[2,8,1024]{2,1,0:T(8,128)S(1)} %token_sums.1.sums_ref.one_ref), channel_id=1, source_target_pairs={{0,3},{1,2},{2,1},{3,0},{4,7},{5,6},{6,5},{7,4},{8,11},{9,10},{10,... | collective-permute-start | bytes 196616 | tf_op jit(solution)/shard_map/ppermute | solution.py:629
  6.4 0.1 collective-permute-start.1
  6.5 0.3 collective-permute-start
  6.9 5.4 %lon_grad.1 = (f32[32,6,32,128]{3,2,1,0:T(8,128)}, f32[8,128]{1,0:T(8,128)S(1)}) custom-call(bf16[96,8,1024]{2,1,0:T(8,128)(2,1)} %cot_ref.1, bf16[2,512,1024]{2,1,0:T(8,128)(2,1)} %constant.14.clone.tab_hbm, f32[2,8,1024]{2,1,0:T(8,128)S(1)} %token_sums.1.sums_ref.one_ref), custom_call_target="tpu_custom_call" | custom-call | flops 4831838208 | bytes 7340032 | tf_op jit(solution)/shard_map/lon_grad/pallas_call | solution.py:217
  12.6 0.1 broadcast_in_dim.27.shift_ref
  12.9 4.9 %lon_field.1 = (f32[32,6,32,128]{3,2,1,0:T(8,128)S(1)}, f32[2,8,1024]{2,1,0:T(8,128)S(1)}) custom-call(bf16[96,8,1024]{2,1,0:T(8,128)(2,1)S(1)} %copy-done, bf16[2,2,512,512]{3,2,1,0:T(8,128)(2,1)} %constant.10.clone.tab_hbm, f32[6,1,128]{2,1,0:T(1,128)S(1)} %broadcast_in_dim.26.gain_ref, f32[6,1,128]{2,1,0:T(1,128)S(1)} %broadcast_in_dim.27.shift_ref, ...), custom_call_target="tpu_custom_call" | custom-call | flops 4831838208 | bytes 7340032 | tf_op jit(solution)/shard_map/lon_field/pallas_call | solution.py:239
  17.8 46.8 %all_to_all.20.block_ref = f32[32,6,32,128]{3,2,1,0:T(8,128)} all-to-all(f32[32,6,32,128]{3,2,1,0:T(8,128)S(1)} %get-tuple-element.23), channel_id=1, replica_groups=mesh['lat'=32,'grp'=4] {'lat'}, dimensions={0} | all-to-all | bytes 6291456 | tf_op jit(solution)/shard_map/all_to_all | solution.py:624
  64.6 6.5 %all-to-all-start = ((f32[32,6,32,128]{3,2,1,0:T(8,128)}), f32[32,6,32,128]{3,2,1,0:T(8,128)}, u32[]{:S(2)}, u32[]{:S(2)}) async-start(f32[32,6,32,128]{3,2,1,0:T(8,128)} %get-tuple-element.21), calls=%async_computation | async-start | bytes 6291456 | tf_op jit(solution)/shard_map/all_to_all | solution.py:624
  71.3 1.0 copy-done.10
  72.3 22.6 %field_modes.1 = (f32[32,6,32,128]{3,2,1,0:T(8,128)S(1)}, bf16[4096,256]{1,0:T(8,128)(2,1)S(1)}, bf16[4096,256]{1,0:T(8,128)(2,1)S(1)}, bf16[4096,256]{1,0:T(8,1...) custom-call(f32[32,6,32,128]{3,2,1,0:T(8,128)} %all_to_all.20.block_ref, ...), custom_call_target="tpu_custom_call" | custom-call | flops 25769803776 | bytes 14680064 | tf_op jit(solution)/shard_map/field_modes/pallas_call | solution.py:451
  94.9 1.6 copy-done.2
  96.6 1.4 copy-done.14
  97.9 1.3 copy-done.16
  99.2 1.3 copy-done.18
  100.5 1.4 copy-done.20
  101.9 1.3 copy-done.22
  103.2 7.5 %all-to-all-done.block_ref = f32[32,6,32,128]{3,2,1,0:T(8,128)} async-done(((f32[32,6,32,128]{3,2,1,0:T(8,128)}), f32[32,6,32,128]{3,2,1,0:T(8,128)}, u32[]{:S(2)}, u32[]{:S(2)}) %all-to-all-start) | async-done | bytes 3145760 | tf_op jit(solution)/shard_map/all_to_all | solution.py:624
  110.8 9.1 %all-to-all-start.2 = ((f32[32,6,32,128]{3,2,1,0:T(8,128)}), f32[32,6,32,128]{3,2,1,0:T(8,128)}, u32[]{:S(2)}, u32[]{:S(2)}) async-start(f32[32,6,32,128]{3,2,1,0:T(8,128)} %copy-done.2), calls=%async_computation.2 | async-start | bytes 6291456 | tf_op jit(solution)/shard_map/all_to_all | solution.py:624
  119.9 1.0 copy-done.11
  121.0 8.3 %grad_modes.1.grad_ref = f32[4096,256]{1,0:T(8,128)S(1)} custom-call(f32[32,6,32,128]{3,2,1,0:T(8,128)} %all-to-all-done.block_ref, bf16[2,2,256,256]{3,2,1,0:T(8,128)(2,1)S(1)} %copy-done.11, bf16[768,1024]{1,0:T(8,128)(2,1)S(1)} %copy-done.8), custom_call_target="tpu_custom_call" | custom-call | flops 12884901888 | bytes 8388608 | tf_op jit(solution)/shard_map/grad_modes/pallas_call | solution.py:435
  129.3 2.0 copy-done.13
  131.3 0.3 broadcast_in_dim.25.cubes_hbm.cubes_ref
  131.6 17.4 %pull_modes.1 = f32[32,208,128]{2,1,0:T(8,128)S(1)} custom-call(f32[4096,256]{1,0:T(8,128)} %copy-done.13, bf16[4096,256]{1,0:T(8,128)(2,1)S(1)} %copy-done.15, bf16[4096,256]{1,0:T(8,128)(2,1)S(1)} %copy-done.17, bf16[4096,256]{1,0:T(8,128)(2,1)S(1)} %copy-done.19, bf16[4096,256]{1,0:T(8,128)(2,1)S(1)} %copy-done.21, bf16[4096,256]{1,0:T(8,128)(2,1)S(1)} %copy-done.23, ...), custom_call_target="tpu_custom_call" | custom-call | flops 17179869184 | bytes 14680064 | tf_op jit(solution)/shard_map/pull_modes/pallas_call | solution.py:473
  149.0 1.7 copy-done.1
  150.7 8.0 %all-to-all-done.2.block_hbm = f32[32,6,32,128]{3,2,1,0:T(8,128)} async-done(((f32[32,6,32,128]{3,2,1,0:T(8,128)}), f32[32,6,32,128]{3,2,1,0:T(8,128)}, u32[]{:S(2)}, u32[]{:S(2)}) %all-to-all-start.2) | async-done | bytes 3145760 | tf_op jit(solution)/shard_map/all_to_all | solution.py:624
  158.8 50.3 %all_to_all.21.block_ref = f32[32,208,128]{2,1,0:T(8,128)S(1)} all-to-all(f32[32,208,128]{2,1,0:T(8,128)} %copy-done.1), channel_id=1, replica_groups=mesh['lat'=32,'grp'=4] {'lat'}, dimensions={0} | all-to-all | bytes 6815744 | tf_op jit(solution)/shard_map/all_to_all | solution.py:624
  209.1 2.6 %pulled.1 = (f32[96,8,1024]{2,1,0:T(8,128)S(1)}, f32[2,8,1024]{2,1,0:T(8,128)S(1)}, f32[1,1152]{1,0:T(1,128)}) custom-call(f32[32,208,128]{2,1,0:T(8,128)S(1)} %all_to_all.21.block_ref, bf16[2,512,512]{2,1,0:T(8,128)(2,1)S(1)} %copy-done.9, bf16[96,8,1024]{2,1,0:T(8,128)(2,1)S(1)} %copy-done, bf16[96,8,1024]{2,1,0:T(8,128)(2,1)S(1)} %copy-done.3, ...), custom_call_target="tpu_custom_call" | custom-call | flops 3221225472 | bytes 10485760 | tf_op jit(solution)/shard_map/pulled/pallas_call | solution.py:660
  211.7 5.5 %collective-permute-start.5 = (f32[2,8,1024]{2,1,0:T(8,128)S(1)}, f32[2,8,1024]{2,1,0:T(8,128)S(1)}, u32[]{:S(2)}, u32[]{:S(2)}) collective-permute-start(f32[2,8,1024]{2,1,0:T(8,128)S(1)} %get-tuple-element.36.back_hbm.one_ref), channel_id=1, source_target_pairs={{0,3},{1,2},{2,1},{3,0},{4,7},{5,6},{6,5},{7,4},{8,11},{9,10},{10,... | collective-permute-start | bytes 196616 | tf_op jit(solution)/shard_map/ppermute | solution.py:629
  217.2 0.5 collective-permute-start.4
  217.7 4.1 %mixed.1 = bf16[96,8,1024]{2,1,0:T(8,128)(2,1)} custom-call(f32[32,6,32,128]{3,2,1,0:T(8,128)} %all-to-all-done.2.block_hbm, bf16[2,512,512]{2,1,0:T(8,128)(2,1)S(1)} %copy-done.9, bf16[96,8,1024]{2,1,0:T(8,128)(2,1)S(1)} %copy-done, f32[2,8,1024]{2,1,0:T(8,128)S(1)} %get-tuple-element.34.stat_ref, ...), custom_call_target="tpu_custom_call" | custom-call | flops 3221225472 | bytes 10485760 | tf_op jit(solution)/shard_map/mixed/pallas_call | solution.py:673
  221.9 1.3 finish.1
  (55 shorter events, 0.5 us)
Async XLA Ops:
  2.1 10.2 %copy-start.24 = (f32[96]{0:T(128)S(1)}, f32[96]{0:T(128)}, u32[]{:S(2)}) copy-start(f32[96]{0:T(128)} %param.15) | copy-start | bytes 1156
  2.2 10.3 %copy-start.25 = (f32[96]{0:T(128)S(1)}, f32[96]{0:T(128)}, u32[]{:S(2)}) copy-start(f32[96]{0:T(128)} %param.16) | copy-start | bytes 1156
  2.2 10.7 %copy-start = (bf16[96,8,1024]{2,1,0:T(8,128)(2,1)S(1)}, bf16[96,8,1024]{2,1,0:T(8,128)(2,1)}, u32[]{:S(2)}) copy-start(bf16[96,8,1024]{2,1,0:T(8,128)(2,1)} %tok_ref.5) | copy-start | bytes 4718596
  2.2 10.7 %collective-permute-start.2 = (f32[2,8,1024]{2,1,0:T(8,128)S(1)}, f32[2,8,1024]{2,1,0:T(8,128)S(1)}, u32[]{:S(2)}, u32[]{:S(2)}) collective-permute-start(f32[2,8,1024]{2,1,0:T(8,128)S(1)} %token_sums.1.sums_ref.one_ref), channel_id=1, source_target_pairs={{0,3},{1,2},{2,1},{3,0},{4,7},{5,6},{6,5},{7,4},{8,11},{9,10},{10,... | collective-permute-start | bytes 196616 | tf_op jit(solution)/shard_map/ppermute | solution.py:629
  6.4 6.5 %collective-permute-start.1 = (f32[2,8,1024]{2,1,0:T(8,128)S(1)}, f32[2,8,1024]{2,1,0:T(8,128)S(1)}, u32[]{:S(2)}, u32[]{:S(2)}) collective-permute-start(f32[2,8,1024]{2,1,0:T(8,128)S(1)} %token_sums.1.sums_ref.one_ref), channel_id=1, source_target_pairs={{0,2},{1,3},{2,0},{3,1},{4,6},{5,7},{6,4},{7,5},{8,10},{9,11},{10,... | collective-permute-start | bytes 196616 | tf_op jit(solution)/shard_map/ppermute | solution.py:629
  6.5 6.3 %collective-permute-start = (f32[2,8,1024]{2,1,0:T(8,128)S(1)}, f32[2,8,1024]{2,1,0:T(8,128)S(1)}, u32[]{:S(2)}, u32[]{:S(2)}) collective-permute-start(f32[2,8,1024]{2,1,0:T(8,128)S(1)} %token_sums.1.sums_ref.one_ref), channel_id=1, source_target_pairs={{0,1},{1,0},{2,3},{3,2},{4,5},{5,4},{6,7},{7,6},{8,9},{9,8},{10,11... | collective-permute-start | bytes 196616 | tf_op jit(solution)/shard_map/ppermute | solution.py:629
  64.6 6.6 %copy-start.4 = (f32[1,2,96,96]{3,2,1,0:T(8,128)S(1)}, f32[1,2,96,96]{3,2,1,0:T(8,128)}, u32[]{:S(2)}) copy-start(f32[1,2,96,96]{3,2,1,0:T(8,128)} %w_in_ref.3) | copy-start | bytes 221188
  64.6 6.6 %copy-start.5 = (f32[1,2,96,96]{3,2,1,0:T(8,128)S(1)}, f32[1,2,96,96]{3,2,1,0:T(8,128)}, u32[]{:S(2)}) copy-start(f32[1,2,96,96]{3,2,1,0:T(8,128)} %w_out_ref.3) | copy-start | bytes 221188
  64.6 6.6 %copy-start.6 = (f32[1,2,96]{2,1,0:T(2,128)S(1)}, f32[1,2,96]{2,1,0:T(2,128)}, u32[]{:S(2)}) copy-start(f32[1,2,96]{2,1,0:T(2,128)} %b_in_ref.1) | copy-start | bytes 2308
  64.6 6.6 %copy-start.7 = (f32[1,2,96]{2,1,0:T(2,128)S(1)}, f32[1,2,96]{2,1,0:T(2,128)}, u32[]{:S(2)}) copy-start(f32[1,2,96]{2,1,0:T(2,128)} %b_out_ref.1) | copy-start | bytes 2308
  64.6 6.6 %copy-start.8 = (bf16[768,1024]{1,0:T(8,128)(2,1)S(1)}, bf16[768,1024]{1,0:T(8,128)(2,1)}, u32[]{:S(2)}) copy-start(bf16[768,1024]{1,0:T(8,128)(2,1)} %constant.13.clone.spread_ref) | copy-start | bytes 4718596
  64.6 46.1 %all-to-all-start = ((f32[32,6,32,128]{3,2,1,0:T(8,128)}), f32[32,6,32,128]{3,2,1,0:T(8,128)}, u32[]{:S(2)}, u32[]{:S(2)}) async-start(f32[32,6,32,128]{3,2,1,0:T(8,128)} %get-tuple-element.21), calls=%async_computation | async-start | bytes 6291456 | tf_op jit(solution)/shard_map/all_to_all | solution.py:624
  94.9 1.6 copy-start.2
  96.6 1.4 copy-start.14
  97.9 1.3 copy-start.16
  99.2 1.3 copy-start.18
  100.5 1.4 copy-start.20
  101.9 1.3 copy-start.22
  110.8 48.0 %all-to-all-start.2 = ((f32[32,6,32,128]{3,2,1,0:T(8,128)}), f32[32,6,32,128]{3,2,1,0:T(8,128)}, u32[]{:S(2)}, u32[]{:S(2)}) async-start(f32[32,6,32,128]{3,2,1,0:T(8,128)} %copy-done.2), calls=%async_computation.2 | async-start | bytes 6291456 | tf_op jit(solution)/shard_map/all_to_all | solution.py:624
  120.9 10.6 %copy-start.12 = (bf16[2,2,256,256]{3,2,1,0:T(8,128)(2,1)S(1)}, bf16[2,2,256,256]{3,2,1,0:T(8,128)(2,1)}, u32[]{:S(2)}) copy-start(bf16[2,2,256,256]{3,2,1,0:T(8,128)(2,1)} %constant.12.clone.tab_ref) | copy-start | bytes 1572868
  120.9 10.6 %copy-start.15 = (bf16[4096,256]{1,0:T(8,128)(2,1)S(1)}, bf16[4096,256]{1,0:T(8,128)(2,1)}, u32[]{:S(2)}) copy-start(bf16[4096,256]{1,0:T(8,128)(2,1)} %copy-done.14) | copy-start | bytes 6291460
  120.9 10.6 %copy-start.17 = (bf16[4096,256]{1,0:T(8,128)(2,1)S(1)}, bf16[4096,256]{1,0:T(8,128)(2,1)}, u32[]{:S(2)}) copy-start(bf16[4096,256]{1,0:T(8,128)(2,1)} %copy-done.16) | copy-start | bytes 6291460
  120.9 10.6 %copy-start.19 = (bf16[4096,256]{1,0:T(8,128)(2,1)S(1)}, bf16[4096,256]{1,0:T(8,128)(2,1)}, u32[]{:S(2)}) copy-start(bf16[4096,256]{1,0:T(8,128)(2,1)} %copy-done.18) | copy-start | bytes 6291460
  120.9 10.6 %copy-start.21 = (bf16[4096,256]{1,0:T(8,128)(2,1)S(1)}, bf16[4096,256]{1,0:T(8,128)(2,1)}, u32[]{:S(2)}) copy-start(bf16[4096,256]{1,0:T(8,128)(2,1)} %copy-done.20) | copy-start | bytes 6291460
  121.0 10.6 %copy-start.23 = (bf16[4096,256]{1,0:T(8,128)(2,1)S(1)}, bf16[4096,256]{1,0:T(8,128)(2,1)}, u32[]{:S(2)}) copy-start(bf16[4096,256]{1,0:T(8,128)(2,1)} %copy-done.22) | copy-start | bytes 6291460
  129.3 2.0 copy-start.13
  149.0 1.7 copy-start.1
  150.7 58.3 %copy-start.3 = (bf16[96,8,1024]{2,1,0:T(8,128)(2,1)S(1)}, bf16[96,8,1024]{2,1,0:T(8,128)(2,1)}, u32[]{:S(2)}) copy-start(bf16[96,8,1024]{2,1,0:T(8,128)(2,1)} %cot_ref.1) | copy-start | bytes 4718596
  158.8 50.3 %copy-start.9 = (bf16[2,512,512]{2,1,0:T(8,128)(2,1)S(1)}, bf16[2,512,512]{2,1,0:T(8,128)(2,1)}, u32[]{:S(2)}) copy-start(bf16[2,512,512]{2,1,0:T(8,128)(2,1)} %constant.11.clone.tab_ref) | copy-start | bytes 3145732
  211.7 10.1 %collective-permute-start.5 = (f32[2,8,1024]{2,1,0:T(8,128)S(1)}, f32[2,8,1024]{2,1,0:T(8,128)S(1)}, u32[]{:S(2)}, u32[]{:S(2)}) collective-permute-start(f32[2,8,1024]{2,1,0:T(8,128)S(1)} %get-tuple-element.36.back_hbm.one_ref), channel_id=1, source_target_pairs={{0,3},{1,2},{2,1},{3,0},{4,7},{5,6},{6,5},{7,4},{8,11},{9,10},{10,... | collective-permute-start | bytes 196616 | tf_op jit(solution)/shard_map/ppermute | solution.py:629
  217.2 4.6 %collective-permute-start.4 = (f32[2,8,1024]{2,1,0:T(8,128)S(1)}, f32[2,8,1024]{2,1,0:T(8,128)S(1)}, u32[]{:S(2)}, u32[]{:S(2)}) collective-permute-start(f32[2,8,1024]{2,1,0:T(8,128)S(1)} %get-tuple-element.36.back_hbm.one_ref), channel_id=1, source_target_pairs={{0,2},{1,3},{2,0},{3,1},{4,6},{5,7},{6,4},{7,5},{8,10},{9,11},{10,... | collective-permute-start | bytes 196616 | tf_op jit(solution)/shard_map/ppermute | solution.py:629
  217.7 4.1 %collective-permute-start.3 = (f32[2,8,1024]{2,1,0:T(8,128)S(1)}, f32[2,8,1024]{2,1,0:T(8,128)S(1)}, u32[]{:S(2)}, u32[]{:S(2)}) collective-permute-start(f32[2,8,1024]{2,1,0:T(8,128)S(1)} %get-tuple-element.36.back_hbm.one_ref), channel_id=1, source_target_pairs={{0,1},{1,0},{2,3},{3,2},{4,5},{5,4},{6,7},{7,6},{8,9},{9,8},{10,11... | collective-permute-start | bytes 196616 | tf_op jit(solution)/shard_map/ppermute | solution.py:629
  (2 other events, 2.1 us)

commit v7 on v6

--- a/solution.py
+++ b/solution.py
@@ -133,12 +133,14 @@
     out_hbm, mark_ref,
     x_ref, tab_ref, wire_ref, in_sems, out_sems,
 ):
-    copies = bring(
-        [(x_hbm, x_ref)] + [(tab_hbm.at[p], tab_ref.at[p]) for p in range(2)], in_sems
-    )
+    pairs = [(x_hbm, x_ref)] + [(tab_hbm.at[p], tab_ref.at[p]) for p in range(2)]
+    copies = [pltpu.make_async_copy(src, dst, in_sems.at[i]) for i, (src, dst) in enumerate(pairs)]
+    copies[0].start()
+    copies[1].start()
     mark_ref[...] = jnp.zeros((8, 128), f32)
     out_copies = []
     copies[0].wait()
+    copies[2].start()
     for parity in range(2):
         copies[1 + parity].wait()
         value = dot(tab_ref[parity], x_ref[...].reshape(LANES, LON), NT)

time: 224 us -> 224 us (level)
  no operation moved by 1% of the time
where the time goes in v7:
time: 224 us; the launch traced here: 223 us
  blocking collectives  97.1 us (43%)
  Pallas kernels  68.2 us (30%)
  starting transfers between devices  26.4 us (12%)
  waiting for transfers between devices  15.6 us (7%)
  local copies, waits for them, and re-layouts  14.9 us (7%)
    all_to_all x2, blocking collectives, exchange(): return lax.all_to_all(value, 'lat', split_axis=0, concat_axis=0, tiled=True)  97.1 us
    pallas_call x1, Pallas kernels, field_modes(): pl.pallas_call(field_modes_kernel, name='field_modes', grid=(STEPS,), in_...  22.6 us
    pallas_call x1, Pallas kernels, pull_modes(): pl.pallas_call(pull_modes_kernel, name='pull_modes', grid=(STEPS,), in_sp...  17.4 us
    all_to_all x2, starting transfers between devices, exchange(): return lax.all_to_all(value, 'lat', split_axis=0, concat_axis=0, tiled=True)  15.7 us
    all_to_all x2, waiting for transfers between devices, exchange(): return lax.all_to_all(value, 'lat', split_axis=0, concat_axis=0, tiled=True)  15.6 us
    unnamed x52, local copies, waits for them, and re-layouts  14.1 us
    ppermute x6, starting transfers between devices, group_terms(): lax.ppermute(value, 'grp', [(j, j ^ step) for j in range(4)])  10.7 us
    pallas_call x1, Pallas kernels, grad_modes(): pl.pallas_call(grad_modes_kernel, name='grad_modes', grid=(STEPS,), in_sp...  8.3 us
  transfers between devices with their start and end apart: 8, of which 2 were waited for; matrix products, arithmetic and copies ran while one was open for 0% of the time, Pallas kernels for 26%

profile of v7, /device:TPU:1, one launch (start us, length us, event | category | flops | bytes accessed | tf_op | source)
XLA Modules:
  0.0 223.3 jit_solution(11080017269058720763)
XLA Ops:
  0.6 1.5 token_sums.1.sums_ref.one_ref
  2.2 4.2 %collective-permute-start.2 = (f32[2,8,1024]{2,1,0:T(8,128)S(1)}, f32[2,8,1024]{2,1,0:T(8,128)S(1)}, u32[]{:S(2)}, u32[]{:S(2)}) collective-permute-start(f32[2,8,1024]{2,1,0:T(8,128)S(1)} %token_sums.1.sums_ref.one_ref), channel_id=1, source_target_pairs={{0,3},{1,2},{2,1},{3,0},{4,7},{5,6},{6,5},{7,4},{8,11},{9,10},{10,... | collective-permute-start | bytes 196616 | tf_op jit(solution)/shard_map/ppermute | solution.py:631
  6.4 0.1 collective-permute-start.1
  6.5 0.3 collective-permute-start
  6.9 5.4 %lon_grad.1 = (f32[32,6,32,128]{3,2,1,0:T(8,128)}, f32[8,128]{1,0:T(8,128)S(1)}) custom-call(bf16[96,8,1024]{2,1,0:T(8,128)(2,1)} %cot_ref.1, bf16[2,512,1024]{2,1,0:T(8,128)(2,1)} %constant.14.clone.tab_hbm, f32[2,8,1024]{2,1,0:T(8,128)S(1)} %token_sums.1.sums_ref.one_ref), custom_call_target="tpu_custom_call" | custom-call | flops 4831838208 | bytes 7340032 | tf_op jit(solution)/shard_map/lon_grad/pallas_call | solution.py:219
  12.6 0.1 broadcast_in_dim.27.shift_ref
  12.9 4.9 %lon_field.1 = (f32[32,6,32,128]{3,2,1,0:T(8,128)S(1)}, f32[2,8,1024]{2,1,0:T(8,128)S(1)}) custom-call(bf16[96,8,1024]{2,1,0:T(8,128)(2,1)S(1)} %copy-done, bf16[2,2,512,512]{3,2,1,0:T(8,128)(2,1)} %constant.10.clone.tab_hbm, f32[6,1,128]{2,1,0:T(1,128)S(1)} %broadcast_in_dim.26.gain_ref, f32[6,1,128]{2,1,0:T(1,128)S(1)} %broadcast_in_dim.27.shift_ref, ...), custom_call_target="tpu_custom_call" | custom-call | flops 4831838208 | bytes 7340032 | tf_op jit(solution)/shard_map/lon_field/pallas_call | solution.py:241
  17.8 46.8 %all_to_all.20.block_ref = f32[32,6,32,128]{3,2,1,0:T(8,128)} all-to-all(f32[32,6,32,128]{3,2,1,0:T(8,128)S(1)} %get-tuple-element.23), channel_id=1, replica_groups=mesh['lat'=32,'grp'=4] {'lat'}, dimensions={0} | all-to-all | bytes 6291456 | tf_op jit(solution)/shard_map/all_to_all | solution.py:626
  64.6 6.5 %all-to-all-start = ((f32[32,6,32,128]{3,2,1,0:T(8,128)}), f32[32,6,32,128]{3,2,1,0:T(8,128)}, u32[]{:S(2)}, u32[]{:S(2)}) async-start(f32[32,6,32,128]{3,2,1,0:T(8,128)} %get-tuple-element.21), calls=%async_computation | async-start | bytes 6291456 | tf_op jit(solution)/shard_map/all_to_all | solution.py:626
  71.3 1.0 copy-done.10
  72.3 22.6 %field_modes.1 = (f32[32,6,32,128]{3,2,1,0:T(8,128)S(1)}, bf16[4096,256]{1,0:T(8,128)(2,1)S(1)}, bf16[4096,256]{1,0:T(8,128)(2,1)S(1)}, bf16[4096,256]{1,0:T(8,1...) custom-call(f32[32,6,32,128]{3,2,1,0:T(8,128)} %all_to_all.20.block_ref, ...), custom_call_target="tpu_custom_call" | custom-call | flops 25769803776 | bytes 14680064 | tf_op jit(solution)/shard_map/field_modes/pallas_call | solution.py:453
  94.9 1.6 copy-done.2
  96.6 1.4 copy-done.14
  97.9 1.3 copy-done.16
  99.2 1.3 copy-done.18
  100.5 1.4 copy-done.20
  101.9 1.3 copy-done.22
  103.2 7.5 %all-to-all-done.block_ref = f32[32,6,32,128]{3,2,1,0:T(8,128)} async-done(((f32[32,6,32,128]{3,2,1,0:T(8,128)}), f32[32,6,32,128]{3,2,1,0:T(8,128)}, u32[]{:S(2)}, u32[]{:S(2)}) %all-to-all-start) | async-done | bytes 3145760 | tf_op jit(solution)/shard_map/all_to_all | solution.py:626
  110.8 9.1 %all-to-all-start.2 = ((f32[32,6,32,128]{3,2,1,0:T(8,128)}), f32[32,6,32,128]{3,2,1,0:T(8,128)}, u32[]{:S(2)}, u32[]{:S(2)}) async-start(f32[32,6,32,128]{3,2,1,0:T(8,128)} %copy-done.2), calls=%async_computation.2 | async-start | bytes 6291456 | tf_op jit(solution)/shard_map/all_to_all | solution.py:626
  119.9 1.0 copy-done.11
  121.0 8.3 %grad_modes.1.grad_ref = f32[4096,256]{1,0:T(8,128)S(1)} custom-call(f32[32,6,32,128]{3,2,1,0:T(8,128)} %all-to-all-done.block_ref, bf16[2,2,256,256]{3,2,1,0:T(8,128)(2,1)S(1)} %copy-done.11, bf16[768,1024]{1,0:T(8,128)(2,1)S(1)} %copy-done.8), custom_call_target="tpu_custom_call" | custom-call | flops 12884901888 | bytes 8388608 | tf_op jit(solution)/shard_map/grad_modes/pallas_call | solution.py:437
  129.3 2.0 copy-done.13
  131.3 0.3 broadcast_in_dim.25.cubes_hbm.cubes_ref
  131.6 17.4 %pull_modes.1 = f32[32,208,128]{2,1,0:T(8,128)S(1)} custom-call(f32[4096,256]{1,0:T(8,128)} %copy-done.13, bf16[4096,256]{1,0:T(8,128)(2,1)S(1)} %copy-done.15, bf16[4096,256]{1,0:T(8,128)(2,1)S(1)} %copy-done.17, bf16[4096,256]{1,0:T(8,128)(2,1)S(1)} %copy-done.19, bf16[4096,256]{1,0:T(8,128)(2,1)S(1)} %copy-done.21, bf16[4096,256]{1,0:T(8,128)(2,1)S(1)} %copy-done.23, ...), custom_call_target="tpu_custom_call" | custom-call | flops 17179869184 | bytes 14680064 | tf_op jit(solution)/shard_map/pull_modes/pallas_call | solution.py:475
  149.0 1.7 copy-done.1
  150.7 8.0 %all-to-all-done.2.block_hbm = f32[32,6,32,128]{3,2,1,0:T(8,128)} async-done(((f32[32,6,32,128]{3,2,1,0:T(8,128)}), f32[32,6,32,128]{3,2,1,0:T(8,128)}, u32[]{:S(2)}, u32[]{:S(2)}) %all-to-all-start.2) | async-done | bytes 3145760 | tf_op jit(solution)/shard_map/all_to_all | solution.py:626
  158.8 50.3 %all_to_all.21.block_ref = f32[32,208,128]{2,1,0:T(8,128)S(1)} all-to-all(f32[32,208,128]{2,1,0:T(8,128)} %copy-done.1), channel_id=1, replica_groups=mesh['lat'=32,'grp'=4] {'lat'}, dimensions={0} | all-to-all | bytes 6815744 | tf_op jit(solution)/shard_map/all_to_all | solution.py:626
  209.1 2.6 %pulled.1 = (f32[96,8,1024]{2,1,0:T(8,128)S(1)}, f32[2,8,1024]{2,1,0:T(8,128)S(1)}, f32[1,1152]{1,0:T(1,128)}) custom-call(f32[32,208,128]{2,1,0:T(8,128)S(1)} %all_to_all.21.block_ref, bf16[2,512,512]{2,1,0:T(8,128)(2,1)S(1)} %copy-done.9, bf16[96,8,1024]{2,1,0:T(8,128)(2,1)S(1)} %copy-done, bf16[96,8,1024]{2,1,0:T(8,128)(2,1)S(1)} %copy-done.3, ...), custom_call_target="tpu_custom_call" | custom-call | flops 3221225472 | bytes 10485760 | tf_op jit(solution)/shard_map/pulled/pallas_call | solution.py:662
  211.7 5.5 %collective-permute-start.5 = (f32[2,8,1024]{2,1,0:T(8,128)S(1)}, f32[2,8,1024]{2,1,0:T(8,128)S(1)}, u32[]{:S(2)}, u32[]{:S(2)}) collective-permute-start(f32[2,8,1024]{2,1,0:T(8,128)S(1)} %get-tuple-element.36.back_hbm.one_ref), channel_id=1, source_target_pairs={{0,3},{1,2},{2,1},{3,0},{4,7},{5,6},{6,5},{7,4},{8,11},{9,10},{10,... | collective-permute-start | bytes 196616 | tf_op jit(solution)/shard_map/ppermute | solution.py:631
  217.2 0.5 collective-permute-start.4
  217.7 4.1 %mixed.1 = bf16[96,8,1024]{2,1,0:T(8,128)(2,1)} custom-call(f32[32,6,32,128]{3,2,1,0:T(8,128)} %all-to-all-done.2.block_hbm, bf16[2,512,512]{2,1,0:T(8,128)(2,1)S(1)} %copy-done.9, bf16[96,8,1024]{2,1,0:T(8,128)(2,1)S(1)} %copy-done, f32[2,8,1024]{2,1,0:T(8,128)S(1)} %get-tuple-element.34.stat_ref, ...), custom_call_target="tpu_custom_call" | custom-call | flops 3221225472 | bytes 10485760 | tf_op jit(solution)/shard_map/mixed/pallas_call | solution.py:675
  221.9 1.3 finish.1
  (55 shorter events, 0.5 us)
Async XLA Ops:
  2.1 10.2 %copy-start.24 = (f32[96]{0:T(128)S(1)}, f32[96]{0:T(128)}, u32[]{:S(2)}) copy-start(f32[96]{0:T(128)} %param.15) | copy-start | bytes 1156
  2.2 10.3 %copy-start.25 = (f32[96]{0:T(128)S(1)}, f32[96]{0:T(128)}, u32[]{:S(2)}) copy-start(f32[96]{0:T(128)} %param.16) | copy-start | bytes 1156
  2.2 10.7 %copy-start = (bf16[96,8,1024]{2,1,0:T(8,128)(2,1)S(1)}, bf16[96,8,1024]{2,1,0:T(8,128)(2,1)}, u32[]{:S(2)}) copy-start(bf16[96,8,1024]{2,1,0:T(8,128)(2,1)} %tok_ref.5) | copy-start | bytes 4718596
  2.2 10.7 %collective-permute-start.2 = (f32[2,8,1024]{2,1,0:T(8,128)S(1)}, f32[2,8,1024]{2,1,0:T(8,128)S(1)}, u32[]{:S(2)}, u32[]{:S(2)}) collective-permute-start(f32[2,8,1024]{2,1,0:T(8,128)S(1)} %token_sums.1.sums_ref.one_ref), channel_id=1, source_target_pairs={{0,3},{1,2},{2,1},{3,0},{4,7},{5,6},{6,5},{7,4},{8,11},{9,10},{10,... | collective-permute-start | bytes 196616 | tf_op jit(solution)/shard_map/ppermute | solution.py:631
  6.4 6.5 %collective-permute-start.1 = (f32[2,8,1024]{2,1,0:T(8,128)S(1)}, f32[2,8,1024]{2,1,0:T(8,128)S(1)}, u32[]{:S(2)}, u32[]{:S(2)}) collective-permute-start(f32[2,8,1024]{2,1,0:T(8,128)S(1)} %token_sums.1.sums_ref.one_ref), channel_id=1, source_target_pairs={{0,2},{1,3},{2,0},{3,1},{4,6},{5,7},{6,4},{7,5},{8,10},{9,11},{10,... | collective-permute-start | bytes 196616 | tf_op jit(solution)/shard_map/ppermute | solution.py:631
  6.5 6.3 %collective-permute-start = (f32[2,8,1024]{2,1,0:T(8,128)S(1)}, f32[2,8,1024]{2,1,0:T(8,128)S(1)}, u32[]{:S(2)}, u32[]{:S(2)}) collective-permute-start(f32[2,8,1024]{2,1,0:T(8,128)S(1)} %token_sums.1.sums_ref.one_ref), channel_id=1, source_target_pairs={{0,1},{1,0},{2,3},{3,2},{4,5},{5,4},{6,7},{7,6},{8,9},{9,8},{10,11... | collective-permute-start | bytes 196616 | tf_op jit(solution)/shard_map/ppermute | solution.py:631
  64.6 6.6 %copy-start.4 = (f32[1,2,96,96]{3,2,1,0:T(8,128)S(1)}, f32[1,2,96,96]{3,2,1,0:T(8,128)}, u32[]{:S(2)}) copy-start(f32[1,2,96,96]{3,2,1,0:T(8,128)} %w_in_ref.3) | copy-start | bytes 221188
  64.6 6.6 %copy-start.5 = (f32[1,2,96,96]{3,2,1,0:T(8,128)S(1)}, f32[1,2,96,96]{3,2,1,0:T(8,128)}, u32[]{:S(2)}) copy-start(f32[1,2,96,96]{3,2,1,0:T(8,128)} %w_out_ref.3) | copy-start | bytes 221188
  64.6 6.6 %copy-start.6 = (f32[1,2,96]{2,1,0:T(2,128)S(1)}, f32[1,2,96]{2,1,0:T(2,128)}, u32[]{:S(2)}) copy-start(f32[1,2,96]{2,1,0:T(2,128)} %b_in_ref.1) | copy-start | bytes 2308
  64.6 6.6 %copy-start.7 = (f32[1,2,96]{2,1,0:T(2,128)S(1)}, f32[1,2,96]{2,1,0:T(2,128)}, u32[]{:S(2)}) copy-start(f32[1,2,96]{2,1,0:T(2,128)} %b_out_ref.1) | copy-start | bytes 2308
  64.6 6.6 %copy-start.8 = (bf16[768,1024]{1,0:T(8,128)(2,1)S(1)}, bf16[768,1024]{1,0:T(8,128)(2,1)}, u32[]{:S(2)}) copy-start(bf16[768,1024]{1,0:T(8,128)(2,1)} %constant.13.clone.spread_ref) | copy-start | bytes 4718596
  64.6 46.1 %all-to-all-start = ((f32[32,6,32,128]{3,2,1,0:T(8,128)}), f32[32,6,32,128]{3,2,1,0:T(8,128)}, u32[]{:S(2)}, u32[]{:S(2)}) async-start(f32[32,6,32,128]{3,2,1,0:T(8,128)} %get-tuple-element.21), calls=%async_computation | async-start | bytes 6291456 | tf_op jit(solution)/shard_map/all_to_all | solution.py:626
  94.9 1.6 copy-start.2
  96.6 1.4 copy-start.14
  97.9 1.3 copy-start.16
  99.2 1.3 copy-start.18
  100.5 1.4 copy-start.20
  101.9 1.3 copy-start.22
  110.8 48.0 %all-to-all-start.2 = ((f32[32,6,32,128]{3,2,1,0:T(8,128)}), f32[32,6,32,128]{3,2,1,0:T(8,128)}, u32[]{:S(2)}, u32[]{:S(2)}) async-start(f32[32,6,32,128]{3,2,1,0:T(8,128)} %copy-done.2), calls=%async_computation.2 | async-start | bytes 6291456 | tf_op jit(solution)/shard_map/all_to_all | solution.py:626
  120.9 10.6 %copy-start.12 = (bf16[2,2,256,256]{3,2,1,0:T(8,128)(2,1)S(1)}, bf16[2,2,256,256]{3,2,1,0:T(8,128)(2,1)}, u32[]{:S(2)}) copy-start(bf16[2,2,256,256]{3,2,1,0:T(8,128)(2,1)} %constant.12.clone.tab_ref) | copy-start | bytes 1572868
  120.9 10.6 %copy-start.15 = (bf16[4096,256]{1,0:T(8,128)(2,1)S(1)}, bf16[4096,256]{1,0:T(8,128)(2,1)}, u32[]{:S(2)}) copy-start(bf16[4096,256]{1,0:T(8,128)(2,1)} %copy-done.14) | copy-start | bytes 6291460
  120.9 10.6 %copy-start.17 = (bf16[4096,256]{1,0:T(8,128)(2,1)S(1)}, bf16[4096,256]{1,0:T(8,128)(2,1)}, u32[]{:S(2)}) copy-start(bf16[4096,256]{1,0:T(8,128)(2,1)} %copy-done.16) | copy-start | bytes 6291460
  120.9 10.6 %copy-start.19 = (bf16[4096,256]{1,0:T(8,128)(2,1)S(1)}, bf16[4096,256]{1,0:T(8,128)(2,1)}, u32[]{:S(2)}) copy-start(bf16[4096,256]{1,0:T(8,128)(2,1)} %copy-done.18) | copy-start | bytes 6291460
  120.9 10.6 %copy-start.21 = (bf16[4096,256]{1,0:T(8,128)(2,1)S(1)}, bf16[4096,256]{1,0:T(8,128)(2,1)}, u32[]{:S(2)}) copy-start(bf16[4096,256]{1,0:T(8,128)(2,1)} %copy-done.20) | copy-start | bytes 6291460
  121.0 10.6 %copy-start.23 = (bf16[4096,256]{1,0:T(8,128)(2,1)S(1)}, bf16[4096,256]{1,0:T(8,128)(2,1)}, u32[]{:S(2)}) copy-start(bf16[4096,256]{1,0:T(8,128)(2,1)} %copy-done.22) | copy-start | bytes 6291460
  129.3 2.0 copy-start.13
  149.0 1.7 copy-start.1
  150.7 58.3 %copy-start.3 = (bf16[96,8,1024]{2,1,0:T(8,128)(2,1)S(1)}, bf16[96,8,1024]{2,1,0:T(8,128)(2,1)}, u32[]{:S(2)}) copy-start(bf16[96,8,1024]{2,1,0:T(8,128)(2,1)} %cot_ref.1) | copy-start | bytes 4718596
  158.8 50.3 %copy-start.9 = (bf16[2,512,512]{2,1,0:T(8,128)(2,1)S(1)}, bf16[2,512,512]{2,1,0:T(8,128)(2,1)}, u32[]{:S(2)}) copy-start(bf16[2,512,512]{2,1,0:T(8,128)(2,1)} %constant.11.clone.tab_ref) | copy-start | bytes 3145732
  211.7 10.1 %collective-permute-start.5 = (f32[2,8,1024]{2,1,0:T(8,128)S(1)}, f32[2,8,1024]{2,1,0:T(8,128)S(1)}, u32[]{:S(2)}, u32[]{:S(2)}) collective-permute-start(f32[2,8,1024]{2,1,0:T(8,128)S(1)} %get-tuple-element.36.back_hbm.one_ref), channel_id=1, source_target_pairs={{0,3},{1,2},{2,1},{3,0},{4,7},{5,6},{6,5},{7,4},{8,11},{9,10},{10,... | collective-permute-start | bytes 196616 | tf_op jit(solution)/shard_map/ppermute | solution.py:631
  217.2 4.6 %collective-permute-start.4 = (f32[2,8,1024]{2,1,0:T(8,128)S(1)}, f32[2,8,1024]{2,1,0:T(8,128)S(1)}, u32[]{:S(2)}, u32[]{:S(2)}) collective-permute-start(f32[2,8,1024]{2,1,0:T(8,128)S(1)} %get-tuple-element.36.back_hbm.one_ref), channel_id=1, source_target_pairs={{0,2},{1,3},{2,0},{3,1},{4,6},{5,7},{6,4},{7,5},{8,10},{9,11},{10,... | collective-permute-start | bytes 196616 | tf_op jit(solution)/shard_map/ppermute | solution.py:631
  217.7 4.1 %collective-permute-start.3 = (f32[2,8,1024]{2,1,0:T(8,128)S(1)}, f32[2,8,1024]{2,1,0:T(8,128)S(1)}, u32[]{:S(2)}, u32[]{:S(2)}) collective-permute-start(f32[2,8,1024]{2,1,0:T(8,128)S(1)} %get-tuple-element.36.back_hbm.one_ref), channel_id=1, source_target_pairs={{0,1},{1,0},{2,3},{3,2},{4,5},{5,4},{6,7},{7,6},{8,9},{9,8},{10,11... | collective-permute-start | bytes 196616 | tf_op jit(solution)/shard_map/ppermute | solution.py:631
  (2 other events, 2.1 us)
